TPU v7x, 32 devices: a whole 2x2x4 slice. The times are simulated.
32 devices in a mesh: groups: 2 (over y), loop: 4 (over z), narrow: 2 (over x), sub: 2 (over core).
Axes of the slice: x: 2, y: 2, z: 4, core: 2. Of those that a mesh axis runs over, the one named last changes fastest.
Arguments:
- block_input_rows: bfloat16 [1024, 3072], P(('groups', 'loop'), ('narrow', 'sub')), parts along dimension 0, may hold values from -240 to 240
- frozen_up_weight: bfloat16 [3072, 12288], P(('narrow', 'sub'), 'loop'), may hold values from -0.109375 to 0.109375
- frozen_down_weight: bfloat16 [12288, 3072], P('loop', ('narrow', 'sub')), may hold values from -0.0546875 to 0.0546875
- down_first_factor: bfloat16 [12288, 64], replicated, may hold values from -0.0546875 to 0.0546875
- down_second_factor: bfloat16 [64, 3072], replicated, may hold values from -0.75 to 0.75
- modulation: float32 [8, 3, 3072], P(None, None, ('narrow', 'sub')), may hold values from -4 to 4
- timestep_index: int32 [2], P('groups'), parts along dimension 0, may hold values from 0 to 7
- cotangent: bfloat16 [1024, 3072], P(('groups', 'loop'), ('narrow', 'sub')), parts along dimension 0, may hold values from -0.25 to 0.25
Outputs:
- block_update: bfloat16 [1024, 3072], P(('groups', 'loop'), ('narrow', 'sub')), parts along dimension 0
- down_first_gradient: float32 [24576, 64], P(('groups', 'loop')), parts along dimension 0
- down_second_gradient: float32 [128, 3072], P('groups', ('narrow', 'sub')), parts along dimension 0
There are 2 independent parts, one for each index of `groups`. A program takes and returns all parts, laid end to end along the dimension named above; an argument that names none is the same for every part. Nothing has to cross between parts.
All inputs are finite; a program needn't handle non-finite values.
Results may differ from a plain program's by a relative error of at most 0.02.
Values may be sent and summed in bfloat16 or wider, within the bound.
No kernel may reach another device: no remote copies, remote signals or barrier semaphores. Data moves between devices by JAX's collectives and lax.ppermute only.
A program may use at most 64 MiB of HBM per device.

v0:
```python
import jax
import jax.numpy as jnp
from jax import lax
from jax.sharding import PartitionSpec as P

MODEL_WIDTH = 3072


adapter_scale = 0.5
norm_eps = 1e-06
gelu_coef = 0.7978845608028654


def gelu_value(pre_value):
    inner_arg = gelu_coef * (pre_value + 0.044715 * pre_value * pre_value * pre_value)
    return 0.5 * pre_value * (1.0 + jnp.tanh(inner_arg))


def inner_row_values(left_mat, right_mat):
    return lax.dot_general(
        left_mat, right_mat, (((0,), (0,)), ((), ())), preferred_element_type=jnp.float32
    )


def inner_row_values_exact(left_mat, right_mat):
    return lax.dot_general(
        left_mat,
        right_mat,
        (((0,), (0,)), ((), ())),
        preferred_element_type=jnp.float32,
        precision=lax.Precision.HIGHEST,
    )


def times_transposed(left_mat, right_mat):
    return lax.dot_general(
        left_mat, right_mat, (((1,), (1,)), ((), ())), preferred_element_type=jnp.float32
    )


def row_modulation(first_row, row_span, total_rows, timestep_index, modulation):
    sample_total = timestep_index.shape[0]
    step_total = modulation.shape[0]
    row_ids = first_row + lax.iota(jnp.int32, row_span)
    sample_of = row_ids // (total_rows // sample_total)
    sample_pick = (sample_of[:, None] == lax.iota(jnp.int32, sample_total)[None, :]).astype(
        jnp.int32
    )
    step_of = jnp.sum(sample_pick * timestep_index[None, :], axis=1)
    onehot = (step_of[:, None] == lax.iota(jnp.int32, step_total)[None, :]).astype(jnp.float32)
    table_flat = modulation.reshape(step_total, -1)
    picked = jnp.dot(onehot, table_flat, precision=lax.Precision.HIGHEST).reshape(row_span, 3, -1)
    return (picked[:, 0], picked[:, 1], picked[:, 2])


def normalize(feat_rows, row_sums, mod_shift, mod_scale):
    row_mean = row_sums[0] / MODEL_WIDTH
    row_msq = row_sums[1] / MODEL_WIDTH
    inv_std = lax.rsqrt(row_msq - row_mean * row_mean + norm_eps)
    return (
        (feat_rows - row_mean[:, None]) * inv_std[:, None] * (1.0 + mod_scale) + mod_shift
    ).astype(jnp.bfloat16)


def per_device(
    block_input_rows,
    frozen_up_weight,
    frozen_down_weight,
    down_first_factor,
    down_second_factor,
    modulation,
    timestep_index,
    cotangent,
):
    loop_size = lax.axis_size("loop")
    loop_position = lax.axis_index("loop")
    wide_position = lax.axis_index(("narrow", "sub"))
    row_count, feature_count = block_input_rows.shape
    total_rows = row_count * loop_size
    hidden_unit_count = frozen_up_weight.shape[1]
    local_down_first_factor = lax.dynamic_slice_in_dim(
        down_first_factor, loop_position * hidden_unit_count, hidden_unit_count, 0
    )
    local_down_second_factor = lax.dynamic_slice_in_dim(
        down_second_factor, wide_position * feature_count, feature_count, 1
    )
    input_f = block_input_rows.astype(jnp.float32)
    row_sums = lax.psum(
        (jnp.sum(input_f, axis=1), jnp.sum(input_f * input_f, axis=1)), ("narrow", "sub")
    )
    mod_shift, mod_scale, mod_gate = row_modulation(
        loop_position * row_count, row_count, total_rows, timestep_index, modulation
    )
    normed_local = normalize(input_f, row_sums, mod_shift, mod_scale)
    normed = lax.all_gather(normed_local, "loop", axis=0, tiled=True)
    up_part = jnp.dot(normed, frozen_up_weight, preferred_element_type=jnp.float32)
    pre_act = lax.psum(up_part.astype(jnp.bfloat16), ("narrow", "sub")).astype(jnp.float32)
    activated_units = gelu_value(pre_act).astype(jnp.bfloat16)
    frozen_down_output = lax.psum_scatter(
        jnp.dot(activated_units, frozen_down_weight, preferred_element_type=jnp.float32).astype(
            jnp.bfloat16
        ),
        "loop",
        scatter_dimension=0,
        tiled=True,
    ).astype(jnp.float32)
    low_part = jnp.dot(activated_units, local_down_first_factor, preferred_element_type=jnp.float32)
    lowrank_down_output = lax.psum_scatter(
        low_part.astype(jnp.bfloat16), "loop", scatter_dimension=0, tiled=True
    ).astype(jnp.float32)
    branch_output = frozen_down_output + adapter_scale * jnp.dot(
        lowrank_down_output,
        local_down_second_factor.astype(jnp.float32),
        precision=lax.Precision.HIGHEST,
    )
    block_update = (mod_gate * branch_output).astype(jnp.bfloat16)
    backward_local_rows = (mod_gate * cotangent.astype(jnp.float32)).astype(jnp.bfloat16)
    low_back_part = times_transposed(backward_local_rows, local_down_second_factor)
    low_back_sum = lax.psum(low_back_part.astype(jnp.bfloat16), ("narrow", "sub"))
    lowrank_backward_total = lax.all_gather(low_back_sum, "loop", axis=0, tiled=True)
    down_first_gradient = adapter_scale * inner_row_values(activated_units, lowrank_backward_total)
    down_second_contribution = adapter_scale * inner_row_values_exact(
        lowrank_down_output, backward_local_rows.astype(jnp.float32)
    )
    down_second_gradient = lax.psum(down_second_contribution.astype(jnp.bfloat16), "loop").astype(
        jnp.float32
    )
    return (block_update, down_first_gradient, down_second_gradient)


def solution(mesh):
    in_specs = (
        P(("groups", "loop"), ("narrow", "sub")),
        P(("narrow", "sub"), "loop"),
        P("loop", ("narrow", "sub")),
        P(),
        P(),
        P(None, None, ("narrow", "sub")),
        P("groups"),
        P(("groups", "loop"), ("narrow", "sub")),
    )
    out_specs = (
        P(("groups", "loop"), ("narrow", "sub")),
        P(("groups", "loop"), None),
        P("groups", ("narrow", "sub")),
    )
    return jax.shard_map(
        per_device, mesh=mesh, in_specs=in_specs, out_specs=out_specs, check_vma=False
    )
```

profile of v0, /device:TPU:0, one launch (start us, length us, event | category | flops | bytes accessed | tf_op | source)
XLA Modules:
  0.0 206.9 jit_solution(11648606771733166252)
XLA Ops:
  7.2 0.0 copy-start
  7.2 0.0 all-reduce.4.cloned.1.call-start
  7.2 1.2 convert_reduce_fusion
  9.0 8.3 %all-reduce = (f32[128]{0:T(128)S(1)}, f32[128]{0:T(128)S(1)}) all-reduce(f32[128]{0:T(128)S(1)} %get-tuple-element.4, f32[128]{0:T(128)S(1)} %get-tuple-element.3), channel_id=1, replica_groups=mesh['groups'=2,'loop'=4,'narrow'=2,'sub'=2] {'narrow','sub'}, use_global_device_ids=true, to_apply=%region_3.0 | all-reduce | flops 256 | bytes 2048 | tf_op jit(solution)/shard_map/psum | solution.py:88
  17.4 1.6 fusion.18
  19.0 1.1 fusion.12
  20.1 19.6 %all_gather.6 = bf16[512,768]{1,0:T(8,128)(2,1)S(1)} all-gather(bf16[128,768]{1,0:T(8,128)(2,1)S(1)} %fusion.12), channel_id=1, replica_groups=mesh['groups'=2,'loop'=4,'narrow'=2,'sub'=2] {'loop'}, dimensions={0}, use_global_device_ids=true | all-gather | bytes 983040 | tf_op jit(solution)/shard_map/all_gather | solution.py:95
  39.7 6.3 %convolution_convert_fusion = bf16[512,3072]{1,0:T(8,128)(2,1)} fusion(bf16[512,768]{1,0:T(8,128)(2,1)S(1)} %all_gather.6, bf16[768,3072]{1,0:T(8,128)(2,1)} %param.9), kind=kOutput, calls=%fused_computation.10 | convolution fusion | flops 2417491968 | bytes 8650752 | tf_op jit(solution)/shard_map/dot_general | solution.py:96
  46.0 0.0 all-reduce.4.cloned.1.call-update
  46.1 0.0 reduce-scatter.7.cloned.1.call-start
  46.1 0.0 copy-start.1
  46.1 67.2 %all-reduce.4.cloned.1.call-done = bf16[512,3072]{1,0:T(8,128)(2,1)} async-done(((bf16[512,3072]{1,0:T(8,128)(2,1)}), bf16[512,3072]{1,0:T(8,128)(2,1)}) %all-reduce.4.cloned.1.call-update) | async-done | bytes 3145744 | tf_op jit(solution)/shard_map/psum | solution.py:97
  113.4 0.0 copy-done
  113.4 4.2 %convolution_convert_fusion.2 = bf16[512,64]{0,1:T(8,128)(2,1)S(1)} fusion(bf16[12288,64]{0,1:T(8,128)(2,1)S(1)} %copy-done, s32[]{:T(128)S(6)} %select_n.17, bf16[512,3072]{1,0:T(8,128)(2,1)} %all-reduce.4.cloned.1.call-done), kind=kOutput, calls=%fused_computation.19 | convolution fusion | flops 217088000 | bytes 3604484 | tf_op jit(solution)/shard_map/dot_general | solution.py:107
  117.6 0.8 copy.11
  118.4 0.0 reduce-scatter.7.cloned.1.call-update
  118.4 0.0 all-reduce.6.cloned.1.call-start
  118.4 19.4 %reduce-scatter.7.cloned.1.call-done = bf16[128,64]{1,0:T(8,128)(2,1)} async-done(((bf16[512,64]{1,0:T(8,128)(2,1)}), bf16[128,64]{1,0:T(8,128)(2,1)}) %reduce-scatter.7.cloned.1.call-update) | async-done | bytes 16400
  137.8 0.0 copy-done.1
  137.8 1.6 fusion.8
  139.4 0.0 all-reduce.6.cloned.1.call-update
  139.5 0.0 copy-start.3
  139.5 0.0 reduce-scatter.5.cloned.1.call-start
  139.5 8.1 %convolution_convert_fusion.1 = bf16[512,768]{1,0:T(8,128)(2,1)} fusion(bf16[3072,768]{1,0:T(8,128)(2,1)} %param.10, bf16[512,3072]{1,0:T(8,128)(2,1)} %all-reduce.4.cloned.1.call-done), kind=kOutput, calls=%fused_computation.12 | convolution fusion | flops 2432040960 | bytes 8650752 | tf_op jit(solution)/shard_map/dot_general | solution.py:100
  147.7 0.0 reduce-scatter.5.cloned.1.call-update
  147.7 0.2 convolution_convert_fusion.3
  147.9 10.7 %psum.38 = bf16[128,64]{1,0:T(8,128)(2,1)S(1)} all-reduce(bf16[128,64]{1,0:T(8,128)(2,1)S(1)} %convolution_convert_fusion.3), channel_id=1, replica_groups=mesh['groups'=2,'loop'=4,'narrow'=2,'sub'=2] {'narrow','sub'}, use_global_device_ids=true, to_apply=%region_7.8 | all-reduce | flops 8192 | bytes 32768 | tf_op jit(solution)/shard_map/psum | solution.py:119
  158.6 13.5 %all_gather.7 = bf16[512,64]{1,0:T(8,128)(2,1)S(1)} all-gather(bf16[128,64]{1,0:T(8,128)(2,1)S(1)} %psum.38), channel_id=1, replica_groups=mesh['groups'=2,'loop'=4,'narrow'=2,'sub'=2] {'loop'}, dimensions={0}, use_global_device_ids=true | all-gather | bytes 81920 | tf_op jit(solution)/shard_map/all_gather | solution.py:120
  172.1 5.2 %convolution_multiply_fusion = f32[3072,64]{0,1:T(8,128)} fusion(bf16[512,64]{1,0:T(8,128)(2,1)S(1)} %all_gather.7, bf16[512,3072]{1,0:T(8,128)(2,1)} %all-reduce.4.cloned.1.call-done), kind=kOutput, calls=%fused_computation.11 | convolution fusion | flops 217251840 | bytes 3997696 | tf_op jit(solution)/shard_map/dot_general | solution.py:20
  177.3 1.6 convert_element_type.60
  178.9 19.6 %reduce-scatter.5.cloned.1.call-done = bf16[128,768]{1,0:T(8,128)(2,1)} async-done(((bf16[512,768]{1,0:T(8,128)(2,1)}), bf16[128,768]{1,0:T(8,128)(2,1)}) %reduce-scatter.5.cloned.1.call-update) | async-done | bytes 196624 | tf_op jit(solution)/shard_map/reduce_scatter | solution.py:99
  198.6 1.8 fusion.7
  (6 shorter events, 0.0 us)
Async XLA Ops:
  7.2 106.2 %copy-start = (bf16[12288,64]{0,1:T(8,128)(2,1)S(1)}, bf16[12288,64]{0,1:T(8,128)(2,1)}, u32[]{:S(2)}) copy-start(bf16[12288,64]{0,1:T(8,128)(2,1)} %param.11) | copy-start | bytes 4718596
  7.2 106.2 %all-reduce.4.cloned.1.call-start = ((), (), s32[]{:S(2)}) async-start(), calls=%async_computation.2 | async-start | bytes 6291456 | tf_op jit(solution)/shard_map/psum | solution.py:97
  46.1 91.8 %reduce-scatter.7.cloned.1.call-start = ((), (), s32[]{:S(2)}) async-start(), calls=%async_computation.5 | async-start | bytes 163840
  46.1 91.7 %copy-start.1 = (bf16[128,768]{1,0:T(8,128)(2,1)S(1)}, bf16[128,768]{1,0:T(8,128)(2,1)}, u32[]{:S(2)}) copy-start(bf16[128,768]{1,0:T(8,128)(2,1)} %param.15) | copy-start | bytes 589828
  118.4 58.9 %all-reduce.6.cloned.1.call-start = ((), (), s32[]{:S(2)}) async-start(), calls=%async_computation.4 | async-start | bytes 196608 | tf_op jit(solution)/shard_map/psum | solution.py:125
  139.5 8.2 %copy-start.3 = (bf16[64,3072]{1,0:T(8,128)(2,1)S(1)}, bf16[64,3072]{1,0:T(8,128)(2,1)}, u32[]{:S(2)}) copy-start(bf16[64,3072]{1,0:T(8,128)(2,1)} %param.12) | copy-start | bytes 1179652
  139.5 59.1 %reduce-scatter.5.cloned.1.call-start = ((), (), s32[]{:S(2)}) async-start(), calls=%async_computation.3 | async-start | bytes 983040 | tf_op jit(solution)/shard_map/reduce_scatter | solution.py:99
  172.1 26.4 %copy-start.2 = (bf16[128,64]{1,0:T(8,128)(2,1)S(1)}, bf16[128,64]{1,0:T(8,128)(2,1)}, u32[]{:S(2)}) copy-start(bf16[128,64]{1,0:T(8,128)(2,1)} %reduce-scatter.7.cloned.1.call-done) | copy-start | bytes 49156
Sparse Core Ops, SparseCore 0:
  46.2 67.1 all-reduce.3
  118.5 19.2 reduce-scatter.6
  140.8 32.3 all-reduce.5
  175.4 23.1 reduce-scatter.4
where the time goes:
time: 207 us
  waiting for transfers between devices  106 us (51%)
  blocking collectives  52.2 us (25%)
  matrix products  29 us (14%)
  between operations  14.5 us (7%)
  other arithmetic  3.9 us (2%)
    psum x1, waiting for transfers between devices, per_device(): lax.psum(up_part.astype(jnp.bfloat16), ('narrow', 'sub'))  67.2 us
    reduce_scatter x1, waiting for transfers between devices, per_device(): lax.psum_scatter(jnp.dot(activated_units, frozen_down_weight, preferred_e...  19.6 us
    all_gather x1, blocking collectives, per_device(): normed = lax.all_gather(normed_local, 'loop', axis=0, tiled=True)  19.6 us
    unnamed x5, waiting for transfers between devices  19.5 us
    all_gather x1, blocking collectives, per_device(): lax.all_gather(low_back_sum, 'loop', axis=0, tiled=True)  13.5 us
    psum x1, blocking collectives, per_device(): lax.psum(low_back_part.astype(jnp.bfloat16), ('narrow', 'sub'))  10.7 us
    psum x1, blocking collectives, per_device(): lax.psum((jnp.sum(input_f, axis=1), jnp.sum(input_f * input_f, axis=1)),...  8.34 us
    dot_general x1, matrix products, per_device(): jnp.dot(activated_units, frozen_down_weight, preferred_element_type=jnp.f...  8.12 us
  transfers between devices with their start and end apart: 4, of which 3 were waited for; matrix products, arithmetic and copies ran while one was open for 7% of the time, Pallas kernels for 0%

commit v1 on v0

v1 whole, which is shorter than its diff:
```python
import jax
import jax.numpy as jnp
from jax import lax
from jax.sharding import PartitionSpec as P

adapter_scale = 0.5
norm_eps = 1e-06
gelu_coef = 0.7978845608028654
f32 = jnp.float32
bf16 = jnp.bfloat16


def gelu_value(pre_value):
    inner_arg = gelu_coef * (pre_value + 0.044715 * pre_value * pre_value * pre_value)
    return 0.5 * pre_value * (1.0 + jnp.tanh(inner_arg))


def dot(left, right):
    return jnp.dot(left, right, preferred_element_type=f32)


def swap(value, axis, distance):
    size = lax.axis_size(axis)
    return lax.ppermute(value, axis, [(i, i ^ distance) for i in range(size)])


def shift(value, axis, distance):
    size = lax.axis_size(axis)
    return lax.ppermute(value, axis, [(i, (i + distance) % size) for i in range(size)])


def sum_over(value, axis, kind):
    distance = 1
    while distance < lax.axis_size(axis):
        value = value.astype(kind)
        value = value.astype(f32) + swap(value, axis, distance).astype(f32)
        distance *= 2
    return value


def per_device(
    block_input_rows,
    frozen_up_weight,
    frozen_down_weight,
    down_first_factor,
    down_second_factor,
    modulation,
    timestep_index,
    cotangent,
):
    loop_size = lax.axis_size("loop")
    loop_position = lax.axis_index("loop")
    wide_position = lax.axis_index(("narrow", "sub"))
    sub_position = lax.axis_index("sub")
    wide_size = lax.axis_size("narrow") * lax.axis_size("sub")
    rows, features = block_input_rows.shape
    model_width = features * wide_size
    hidden = frozen_up_weight.shape[1]
    half = hidden // 2
    rank = down_first_factor.shape[1]
    first_factor = lax.dynamic_slice_in_dim(down_first_factor, loop_position * hidden, hidden, 0)
    second_factor = lax.dynamic_slice_in_dim(
        down_second_factor, wide_position * features, features, 1
    )
    step = lax.dynamic_index_in_dim(modulation, timestep_index[0], 0, keepdims=False)
    mod_shift, mod_scale, mod_gate = step[0:1], step[1:2], step[2:3]

    input_f = block_input_rows.astype(f32)
    back_rows = (mod_gate * cotangent.astype(f32)).astype(bf16)
    low_back_part = lax.dot_general(
        back_rows, second_factor, (((1,), (1,)), ((), ())), preferred_element_type=f32
    )
    packed = jnp.concatenate(
        [
            low_back_part,
            jnp.sum(input_f, axis=1, keepdims=True),
            jnp.sum(input_f * input_f, axis=1, keepdims=True),
        ],
        axis=1,
    )
    packed = sum_over(sum_over(packed, "sub", f32), "narrow", f32)
    row_mean = packed[:, rank : rank + 1] / model_width
    row_msq = packed[:, rank + 1 : rank + 2] / model_width
    low_back = packed[:, :rank].astype(bf16)
    inv_std = lax.rsqrt(row_msq - row_mean * row_mean + norm_eps)
    normed = ((input_f - row_mean) * inv_std * (1.0 + mod_scale) + mod_shift).astype(bf16)

    travelling = jnp.concatenate([normed, low_back], axis=1)
    first_gradient = None
    down_sum = None
    own_down = None
    for block in range(loop_size):
        block_normed = travelling[:, :features]
        block_low_back = travelling[:, features:]
        if block < loop_size - 1:
            travelling = shift(travelling, "loop", -1)
        up_part = dot(block_normed, frozen_up_weight).astype(bf16)
        kept = lax.dynamic_slice_in_dim(up_part, sub_position * half, half, 1)
        sent = lax.dynamic_slice_in_dim(up_part, (1 - sub_position) * half, half, 1)
        chip_sum = (kept.astype(f32) + swap(sent, "sub", 1).astype(f32)).astype(bf16)
        pre_act = sum_over(chip_sum, "narrow", bf16)
        own_half = gelu_value(pre_act).astype(bf16)
        other_half = swap(own_half, "sub", 1)
        activated = jnp.where(
            sub_position == 0,
            jnp.concatenate([own_half, other_half], axis=1),
            jnp.concatenate([other_half, own_half], axis=1),
        )
        low_part = dot(activated, first_factor)
        down_part = dot(activated, frozen_down_weight)
        joined = jnp.concatenate([down_part, low_part], axis=1)
        gradient_part = lax.dot_general(
            block_low_back, activated, (((0,), (0,)), ((), ())), preferred_element_type=f32
        )
        first_gradient = gradient_part if block == 0 else first_gradient + gradient_part
        if block == 0:
            own_down = joined.astype(bf16)
        else:
            if block > 1:
                joined = joined + down_sum.astype(f32)
            down_sum = shift(joined.astype(bf16), "loop", -1)
    total = own_down.astype(f32) + down_sum.astype(f32)
    base_down, low_down = total[:, :features], total[:, features:]
    branch = base_down + adapter_scale * jnp.dot(
        low_down, second_factor.astype(f32), precision=lax.Precision.HIGHEST
    )
    block_update = (mod_gate * branch).astype(bf16)
    contribution = adapter_scale * lax.dot_general(
        low_down,
        back_rows.astype(f32),
        (((0,), (0,)), ((), ())),
        preferred_element_type=f32,
        precision=lax.Precision.HIGHEST,
    )
    second_gradient = contribution.astype(bf16)
    if loop_size == 4:
        first, second, third = [shift(second_gradient, "loop", k).astype(f32) for k in (1, 2, 3)]
        second_gradient = (second_gradient.astype(f32) + second) + (first + third)
    else:
        second_gradient = lax.psum(second_gradient, "loop").astype(f32)
    return (block_update, adapter_scale * first_gradient.T, second_gradient)


def solution(mesh):
    in_specs = (
        P(("groups", "loop"), ("narrow", "sub")),
        P(("narrow", "sub"), "loop"),
        P("loop", ("narrow", "sub")),
        P(),
        P(),
        P(None, None, ("narrow", "sub")),
        P("groups"),
        P(("groups", "loop"), ("narrow", "sub")),
    )
    out_specs = (
        P(("groups", "loop"), ("narrow", "sub")),
        P(("groups", "loop"), None),
        P("groups", ("narrow", "sub")),
    )
    return jax.shard_map(
        per_device, mesh=mesh, in_specs=in_specs, out_specs=out_specs, check_vma=False
    )
```

time: 207 us -> 104 us (0.50)
  waiting for transfers between devices: 106 us -> 26.8 us
  blocking collectives: 52.2 us -> 0 us
  starting transfers between devices: 0.16 us -> 34.9 us
  between operations: 14.5 us -> 1.78 us
  other arithmetic: 3.9 us -> 7.78 us
    psum x2 -> x0, waiting for transfers between devices: 67.2 us -> none  [the longest x1 67.2 us: per_device(): lax.psum(up_part.astype(jnp.bfloat16), ('narrow', 'sub'))]
    ppermute x0 -> x23, starting transfers between devices: none -> 34.9 us  [the longest x9 24 us: shift(): lax.ppermute(value, axis, [(i, (i + distance) % size) for i in range(size)])]
    all_gather x2 -> x0, blocking collectives: 33.2 us -> none  [the longest x1 19.6 us: per_device(): normed = lax.all_gather(normed_local, 'loop', axis=0, tiled=True)]
    ppermute x0 -> x23, waiting for transfers between devices: none -> 26.8 us  [the longest x9 20.3 us: shift(): lax.ppermute(value, axis, [(i, (i + distance) % size) for i in range(size)])]
    reduce_scatter x1 -> x0, waiting for transfers between devices: 19.6 us -> none  [per_device(): lax.psum_scatter(jnp.dot(activated_units, frozen_down_weight, preferred_e...]
    unnamed x5 -> x0, waiting for transfers between devices: 19.5 us -> none
    psum x2 -> x0, blocking collectives: 19 us -> none  [the longest x1 10.7 us: per_device(): lax.psum(low_back_part.astype(jnp.bfloat16), ('narrow', 'sub'))]
    convert_element_type x2 -> x11, other arithmetic: 2.71 us -> 4.92 us  [the longest x4 3.31 us: per_device(): own_half = gelu_value(pre_act).astype(bf16)]
  transfers between devices with their start and end apart: 4 -> 23, of which waited for: 3 -> 11; matrix products, arithmetic and copies ran while one was open for 7% -> 32% of each run, Pallas kernels for 0% -> 0%
where the time goes in v1:
time: 104 us
  starting transfers between devices  34.9 us (34%)
  matrix products  29.9 us (29%)
  waiting for transfers between devices  26.8 us (26%)
  other arithmetic  7.78 us (7%)
  local copies, waits for them, and re-layouts  2.5 us (2%)
  between operations  1.78 us (2%)
    ppermute x9, starting transfers between devices, shift(): lax.ppermute(value, axis, [(i, (i + distance) % size) for i in range(size)])  24 us
    dot_general x12, matrix products, dot(): return jnp.dot(left, right, preferred_element_type=f32)  21.2 us
    ppermute x9, waiting for transfers between devices, shift(): lax.ppermute(value, axis, [(i, (i + distance) % size) for i in range(size)])  20.3 us
    ppermute x14, starting transfers between devices, swap(): return lax.ppermute(value, axis, [(i, i ^ distance) for i in range(size)])  10.9 us
    ppermute x14, waiting for transfers between devices, swap(): return lax.ppermute(value, axis, [(i, i ^ distance) for i in range(size)])  6.52 us
    dot_general x4, matrix products, per_device(): lax.dot_general(block_low_back, activated, (((0,), (0,)), ((), ())), pref...  5.32 us
    convert_element_type x4, other arithmetic, per_device(): own_half = gelu_value(pre_act).astype(bf16)  3.31 us
  transfers between devices with their start and end apart: 23, of which 11 were waited for; matrix products, arithmetic and copies ran while one was open for 32% of the time, Pallas kernels for 0%

profile of v1, /device:TPU:0, one launch (start us, length us, event | category | flops | bytes accessed | tf_op | source)
XLA Modules:
  0.0 103.6 jit_solution(18296290855059136674)
XLA Ops:
  5.9 2.9 %collective-permute-start.1 = (f32[128,66]{0,1:T(8,128)S(1)}, f32[128,66]{0,1:T(8,128)S(1)}, u32[]{:S(2)}, u32[]{:S(2)}) collective-permute-start(f32[128,66]{0,1:T(8,128)S(1)} %fusion.61), channel_id=1, source_target_pairs={{0,2},{2,0},{1,3},{3,1},{4,6},{6,4},{5,7},{7,5},{8,10},{10,8},{9,1... | collective-permute-start | bytes 101384 | tf_op jit(solution)/shard_map/ppermute | solution.py:24
  8.8 1.9 %collective-permute-done.1 = f32[128,66]{0,1:T(8,128)S(1)} collective-permute-done((f32[128,66]{0,1:T(8,128)S(1)}, f32[128,66]{0,1:T(8,128)S(1)}, u32[]{:S(2)}, u32[]{:S(2)}) %collective-permute-start.1) | collective-permute-done | bytes 33824 | tf_op jit(solution)/shard_map/ppermute | solution.py:24
  12.7 4.2 %collective-permute-start.5 = (bf16[128,832]{1,0:T(8,128)(2,1)S(1)}, bf16[128,832]{1,0:T(8,128)(2,1)S(1)}, u32[]{:S(2)}, u32[]{:S(2)}) collective-permute-start(bf16[128,832]{1,0:T(8,128)(2,1)S(1)} %pad_maximum_fusion), channel_id=1, source_target_pairs={{0,12},{4,0},{8,4},{12,8},{1,13},{5,1},{9,5},{13,9},{2,14},{6,2},{... | collective-permute-start | bytes 638984 | tf_op jit(solution)/shard_map/ppermute | solution.py:29
  16.8 3.3 %convolution_convert_fusion.3 = bf16[128,3072]{1,0:T(8,128)(2,1)S(1)} fusion(bf16[128,768]{1,0:T(8,128)(2,1)S(1)} %fusion.28, bf16[768,3072]{1,0:T(8,128)(2,1)} %param.9), kind=kOutput, calls=%fused_computation.3 | convolution fusion | flops 604372992 | bytes 5701632 | tf_op jit(solution)/shard_map/dot_general | solution.py:19
  21.8 4.3 %collective-permute-start.6 = (bf16[128,832]{1,0:T(8,128)(2,1)S(1)}, bf16[128,832]{1,0:T(8,128)(2,1)S(1)}, u32[]{:S(2)}, u32[]{:S(2)}) collective-permute-start(bf16[128,832]{1,0:T(8,128)(2,1)S(1)} %collective-permute-done.5), channel_id=1, source_target_pairs={{0,12},{4,0},{8,4},{12,8},{1,13},{5,1},{9,5},{13,9},{2,14},{6,2},{... | collective-permute-start | bytes 638984 | tf_op jit(solution)/shard_map/ppermute | solution.py:29
  26.2 1.6 %collective-permute-start.3 = (bf16[128,1536]{1,0:T(8,128)(2,1)S(1)}, bf16[128,1536]{1,0:T(8,128)(2,1)S(1)}, u32[]{:S(2)}, u32[]{:S(2)}) collective-permute-start(bf16[128,1536]{1,0:T(8,128)(2,1)S(1)} %add_convert_fusion.3), channel_id=1, source_target_pairs={{0,2},{2,0},{1,3},{3,1},{4,6},{6,4},{5,7},{7,5},{8,10},{10,8},{9,1... | collective-permute-start | bytes 1179656 | tf_op jit(solution)/shard_map/ppermute | solution.py:24
  27.8 3.8 %collective-permute-done.6 = bf16[128,832]{1,0:T(8,128)(2,1)S(1)} collective-permute-done((bf16[128,832]{1,0:T(8,128)(2,1)S(1)}, bf16[128,832]{1,0:T(8,128)(2,1)S(1)}, u32[]{:S(2)}, u32[]{:S(2)}) %collective-permute-start.6) | collective-permute-done | bytes 213024 | tf_op jit(solution)/shard_map/ppermute | solution.py:29
  32.5 4.3 %collective-permute-start.7 = (bf16[128,832]{1,0:T(8,128)(2,1)S(1)}, bf16[128,832]{1,0:T(8,128)(2,1)S(1)}, u32[]{:S(2)}, u32[]{:S(2)}) collective-permute-start(bf16[128,832]{1,0:T(8,128)(2,1)S(1)} %collective-permute-done.6), channel_id=1, source_target_pairs={{0,12},{4,0},{8,4},{12,8},{1,13},{5,1},{9,5},{13,9},{2,14},{6,2},{... | collective-permute-start | bytes 638984 | tf_op jit(solution)/shard_map/ppermute | solution.py:29
  37.0 1.6 %collective-permute-start.15 = (bf16[128,1536]{1,0:T(8,128)(2,1)S(1)}, bf16[128,1536]{1,0:T(8,128)(2,1)S(1)}, u32[]{:S(2)}, u32[]{:S(2)}) collective-permute-start(bf16[128,1536]{1,0:T(8,128)(2,1)S(1)} %add_convert_fusion), channel_id=1, source_target_pairs={{0,2},{2,0},{1,3},{3,1},{4,6},{6,4},{5,7},{7,5},{8,10},{10,8},{9,1... | collective-permute-start | bytes 1179656 | tf_op jit(solution)/shard_map/ppermute | solution.py:24
  38.5 3.8 %collective-permute-done.7 = bf16[128,832]{1,0:T(8,128)(2,1)S(1)} collective-permute-done((bf16[128,832]{1,0:T(8,128)(2,1)S(1)}, bf16[128,832]{1,0:T(8,128)(2,1)S(1)}, u32[]{:S(2)}, u32[]{:S(2)}) %collective-permute-start.7) | collective-permute-done | bytes 213024 | tf_op jit(solution)/shard_map/ppermute | solution.py:29
  44.2 1.6 %collective-permute-start.12 = (bf16[128,1536]{1,0:T(8,128)(2,1)S(1)}, bf16[128,1536]{1,0:T(8,128)(2,1)}, u32[]{:S(2)}, u32[]{:S(2)}) collective-permute-start(bf16[128,1536]{1,0:T(8,128)(2,1)S(1)} %add_convert_fusion.1), channel_id=1, source_target_pairs={{0,2},{2,0},{1,3},{3,1},{4,6},{6,4},{5,7},{7,5},{8,10},{10,8},{9,1... | collective-permute-start | bytes 1179656 | tf_op jit(solution)/shard_map/ppermute | solution.py:24
  45.8 3.2 %collective-permute-done.15 = bf16[128,1536]{1,0:T(8,128)(2,1)S(1)} collective-permute-done((bf16[128,1536]{1,0:T(8,128)(2,1)S(1)}, bf16[128,1536]{1,0:T(8,128)(2,1)S(1)}, u32[]{:S(2)}, u32[]{:S(2)}) %collective-permute-start.15) | collective-permute-done | bytes 393248 | tf_op jit(solution)/shard_map/ppermute | solution.py:24
  49.5 1.6 %collective-permute-start.9 = (bf16[128,1536]{1,0:T(8,128)(2,1)S(1)}, bf16[128,1536]{1,0:T(8,128)(2,1)}, u32[]{:S(2)}, u32[]{:S(2)}) collective-permute-start(bf16[128,1536]{1,0:T(8,128)(2,1)S(1)} %add_convert_fusion.2), channel_id=1, source_target_pairs={{0,2},{2,0},{1,3},{3,1},{4,6},{6,4},{5,7},{7,5},{8,10},{10,8},{9,1... | collective-permute-start | bytes 1179656 | tf_op jit(solution)/shard_map/ppermute | solution.py:24
  52.9 4.1 %convolution_convert_fusion.5 = bf16[128,768]{1,0:T(8,128)(2,1)} fusion(bf16[3072,768]{1,0:T(8,128)(2,1)} %param.10, bf16[128,1536]{1,0:T(8,128)(2,1)} %copy-done.10, bf16[128,1536]{1,0:T(8,128)(2,1)S(1)} %fusion.6, pred[]{:T(512)S(6)} %eq.2), kind=kOutput, calls=%fused_computation.14 | convolution fusion | flops 607617024 | bytes 5701633 | tf_op jit(solution)/shard_map/dot_general | solution.py:19
  57.5 1.3 %fusion.16 = bf16[128,1536]{1,0:T(8,128)(2,1)S(1)} fusion(bf16[128,1536]{1,0:T(8,128)(2,1)} %collective-permute-done.12, bf16[128,1536]{1,0:T(8,128)(2,1)S(1)} %add_convert_fusion.1), kind=kLoop, calls=%fused_computation.33 | loop fusion | flops 2359296 | bytes 1179648 | tf_op jit(solution)/shard_map/convert_element_type | solution.py:102
  58.9 1.5 %convolution_convert_fusion.6 = bf16[128,64]{0,1:T(8,128)(2,1)S(1)} fusion(bf16[12288,64]{0,1:T(8,128)(2,1)S(1)} %copy-done, s32[]{:T(128)S(6)} %select_n.48, bf16[128,1536]{1,0:T(8,128)(2,1)} %collective-permute-done.16, bf16[128,1536]{1,0:T(8,128)(2,1)S(1)} %fusion.21, pred[]{:T(512)S(6)} %eq.2), kind=kOutput, calls=%fused_computation.17 | convolution fusion | flops 53878784 | bytes 1196037 | tf_op jit(solution)/shard_map/dot_general | solution.py:19
  60.6 3.4 %convolution_convert_fusion.4 = bf16[128,768]{1,0:T(8,128)(2,1)S(1)} fusion(bf16[3072,768]{1,0:T(8,128)(2,1)} %param.10, bf16[128,1536]{1,0:T(8,128)(2,1)} %collective-permute-done.16, bf16[128,1536]{1,0:T(8,128)(2,1)S(1)} %fusion.21, pred[]{:T(512)S(6)} %eq.2), kind=kOutput, calls=%fused_computation.13 | convolution fusion | flops 607617024 | bytes 5701633 | tf_op jit(solution)/shard_map/dot_general | solution.py:19
  64.1 3.2 %collective-permute-start.17 = (bf16[128,832]{1,0:T(8,128)(2,1)S(1)}, bf16[128,832]{1,0:T(8,128)(2,1)S(1)}, u32[]{:S(2)}, u32[]{:S(2)}) collective-permute-start(bf16[128,832]{1,0:T(8,128)(2,1)S(1)} %pad_maximum_fusion.1), channel_id=1, source_target_pairs={{0,12},{4,0},{8,4},{12,8},{1,13},{5,1},{9,5},{13,9},{2,14},{6,2},{... | collective-permute-start | bytes 638984 | tf_op jit(solution)/shard_map/ppermute | solution.py:29
  67.3 1.5 %fusion.47 = f32[3072,64]{0,1:T(8,128)S(1)} fusion(bf16[128,832]{1,0:T(8,128)(2,1)} %copy-done.6, bf16[128,1536]{1,0:T(8,128)(2,1)} %collective-permute-done.16, bf16[128,1536]{1,0:T(8,128)(2,1)S(1)} %fusion.21, pred[]{:T(512)S(6)} %eq.2), kind=kOutput, calls=%fused_computation.84 | convolution fusion | flops 53870592 | bytes 1605633 | tf_op jit(solution)/shard_map/dot_general | solution.py:112
  69.2 1.3 %fusion.11 = bf16[128,1536]{1,0:T(8,128)(2,1)S(1)} fusion(bf16[128,1536]{1,0:T(8,128)(2,1)} %collective-permute-done.9, bf16[128,1536]{1,0:T(8,128)(2,1)S(1)} %add_convert_fusion.2), kind=kLoop, calls=%fused_computation.28 | loop fusion | flops 2359296 | bytes 1179648 | tf_op jit(solution)/shard_map/convert_element_type | solution.py:102
  70.8 3.5 %fusion.62 = f32[128,768]{1,0:T(8,128)S(1)} fusion(bf16[3072,768]{1,0:T(8,128)(2,1)} %param.10, bf16[128,1536]{1,0:T(8,128)(2,1)} %collective-permute-done.13, bf16[128,1536]{1,0:T(8,128)(2,1)S(1)} %fusion.16, pred[]{:T(512)S(6)} %eq.2), kind=kOutput, calls=%fused_computation.110 | convolution fusion | flops 607518720 | bytes 5898241 | tf_op jit(solution)/shard_map/dot_general | solution.py:19
  74.3 1.6 %fusion.32 = f32[128,64]{1,0:T(8,128)S(1)} fusion(bf16[12288,64]{0,1:T(8,128)(2,1)S(1)} %copy-done, s32[]{:T(128)S(6)} %select_n.48, bf16[128,1536]{1,0:T(8,128)(2,1)} %collective-permute-done.13, bf16[128,1536]{1,0:T(8,128)(2,1)S(1)} %fusion.16, pred[]{:T(512)S(6)} %eq.2), kind=kOutput, calls=%fused_computation.65 | convolution fusion | flops 53870592 | bytes 1212421 | tf_op jit(solution)/shard_map/dot_general | solution.py:19
  75.9 1.4 %collective-permute-start.18 = (bf16[128,832]{1,0:T(8,128)(2,1)S(1)}, bf16[128,832]{1,0:T(8,128)(2,1)S(1)}, u32[]{:S(2)}, u32[]{:S(2)}) collective-permute-start(bf16[128,832]{1,0:T(8,128)(2,1)S(1)} %fusion.23), channel_id=1, source_target_pairs={{0,12},{4,0},{8,4},{12,8},{1,13},{5,1},{9,5},{13,9},{2,14},{6,2},{... | collective-permute-start | bytes 638984 | tf_op jit(solution)/shard_map/ppermute | solution.py:29
  77.3 1.5 %convolution_add_fusion.2 = f32[3072,64]{0,1:T(8,128)S(1)} fusion(f32[3072,64]{0,1:T(8,128)S(1)} %convolution_add_fusion, bf16[128,832]{1,0:T(8,128)(2,1)} %copy-done.4, bf16[128,1536]{1,0:T(8,128)(2,1)} %collective-permute-done.13, bf16[128,1536]{1,0:T(8,128)(2,1)S(1)} %fusion.16, pred[]{:T(512)S(6)} %eq.2), kind=kOutput, calls=%fused_computation.6 | convolution fusion | flops 54067200 | bytes 2392065 | tf_op jit(solution)/shard_map/dot_general | solution.py:112
  80.0 4.0 %collective-permute-done.18 = bf16[128,832]{1,0:T(8,128)(2,1)S(1)} collective-permute-done((bf16[128,832]{1,0:T(8,128)(2,1)S(1)}, bf16[128,832]{1,0:T(8,128)(2,1)S(1)}, u32[]{:S(2)}, u32[]{:S(2)}) %collective-permute-start.18) | collective-permute-done | bytes 213024 | tf_op jit(solution)/shard_map/ppermute | solution.py:29
  84.1 2.4 %collective-permute-start.19 = (bf16[128,832]{1,0:T(8,128)(2,1)S(1)}, bf16[128,832]{1,0:T(8,128)(2,1)S(1)}, u32[]{:S(2)}, u32[]{:S(2)}) collective-permute-start(bf16[128,832]{1,0:T(8,128)(2,1)S(1)} %fusion.22), channel_id=1, source_target_pairs={{0,12},{4,0},{8,4},{12,8},{1,13},{5,1},{9,5},{13,9},{2,14},{6,2},{... | collective-permute-start | bytes 638984 | tf_op jit(solution)/shard_map/ppermute | solution.py:29
  86.5 2.0 %fusion = f32[3072,64]{0,1:T(8,128)} fusion(f32[3072,64]{0,1:T(8,128)S(1)} %convolution_add_fusion.2, bf16[128,832]{1,0:T(8,128)(2,1)} %copy-done.5, bf16[128,1536]{1,0:T(8,128)(2,1)S(1)} %collective-permute-done.10, bf16[128,1536]{1,0:T(8,128)(2,1)S(1)} %fusion.11, pred[]{:T(512)S(6)} %eq.2), kind=kOutput, calls=%fused_computation.7 | convolution fusion | flops 54263808 | bytes 2392065 | tf_op jit(solution)/shard_map/dot_general | solution.py:112
  88.5 2.7 %collective-permute-done.19 = bf16[128,832]{1,0:T(8,128)(2,1)S(1)} collective-permute-done((bf16[128,832]{1,0:T(8,128)(2,1)S(1)}, bf16[128,832]{1,0:T(8,128)(2,1)S(1)}, u32[]{:S(2)}, u32[]{:S(2)}) %collective-permute-start.19) | collective-permute-done | bytes 213024 | tf_op jit(solution)/shard_map/ppermute | solution.py:29
  91.5 3.5 %collective-permute-start.22 = (bf16[64,768]{1,0:T(8,128)(2,1)S(1)}, bf16[64,768]{1,0:T(8,128)(2,1)S(1)}, u32[]{:S(2)}, u32[]{:S(2)}) collective-permute-start(bf16[64,768]{1,0:T(8,128)(2,1)S(1)} %fusion.1), channel_id=1, source_target_pairs={{0,12},{4,0},{8,4},{12,8},{1,13},{5,1},{9,5},{13,9},{2,14},{6,2},{... | collective-permute-start | bytes 294920 | tf_op jit(solution)/shard_map/ppermute | solution.py:29
  95.6 1.9 %fusion.30 = bf16[128,768]{1,0:T(8,128)(2,1)} fusion(f32[128,832]{1,0:T(8,128)S(1)} %convert_add_fusion, f32[768]{0:T(1024)S(1)} %get-tuple-element.6, bf16[64,3072]{1,0:T(8,128)(2,1)} %param.12, s32[]{:T(128)S(6)} %select_n.44), kind=kOutput, calls=%fused_computation.62 | convolution fusion | flops 75890688 | bytes 723972 | tf_op jit(solution)/shard_map/dot_general | solution.py:124
  97.5 4.0 %collective-permute-done.21 = bf16[64,768]{1,0:T(8,128)(2,1)S(1)} collective-permute-done((bf16[64,768]{1,0:T(8,128)(2,1)S(1)}, bf16[64,768]{1,0:T(8,128)(2,1)S(1)}, u32[]{:S(2)}, u32[]{:S(2)}) %collective-permute-start.21) | collective-permute-done | bytes 98336 | tf_op jit(solution)/shard_map/ppermute | solution.py:29
  101.5 1.3 %collective-permute-done.20 = bf16[64,768]{1,0:T(8,128)(2,1)S(1)} collective-permute-done((bf16[64,768]{1,0:T(8,128)(2,1)S(1)}, bf16[64,768]{1,0:T(8,128)(2,1)S(1)}, u32[]{:S(2)}, u32[]{:S(2)}) %collective-permute-start.20) | collective-permute-done | bytes 98336 | tf_op jit(solution)/shard_map/ppermute | solution.py:29
  (91 shorter events, 17.8 us)
Async XLA Ops:
  0.6 51.2 %copy-start = (bf16[12288,64]{0,1:T(8,128)(2,1)S(1)}, bf16[12288,64]{0,1:T(8,128)(2,1)}, u32[]{:S(2)}) copy-start(bf16[12288,64]{0,1:T(8,128)(2,1)} %param.11) | copy-start | bytes 4718596
  4.5 1.4 %collective-permute-start = (f32[128,66]{0,1:T(8,128)S(1)}, f32[128,66]{0,1:T(8,128)S(1)}, u32[]{:S(2)}, u32[]{:S(2)}) collective-permute-start(f32[128,66]{0,1:T(8,128)S(1)} %pad_maximum_fusion.2), channel_id=1, source_target_pairs={{0,1},{1,0},{2,3},{3,2},{4,5},{5,4},{6,7},{7,6},{8,9},{9,8},{10,11... | collective-permute-start | bytes 101384 | tf_op jit(solution)/shard_map/ppermute | solution.py:24
  5.9 4.8 %collective-permute-start.1 = (f32[128,66]{0,1:T(8,128)S(1)}, f32[128,66]{0,1:T(8,128)S(1)}, u32[]{:S(2)}, u32[]{:S(2)}) collective-permute-start(f32[128,66]{0,1:T(8,128)S(1)} %fusion.61), channel_id=1, source_target_pairs={{0,2},{2,0},{1,3},{3,1},{4,6},{6,4},{5,7},{7,5},{8,10},{10,8},{9,1... | collective-permute-start | bytes 101384 | tf_op jit(solution)/shard_map/ppermute | solution.py:24
  12.7 8.2 %collective-permute-start.5 = (bf16[128,832]{1,0:T(8,128)(2,1)S(1)}, bf16[128,832]{1,0:T(8,128)(2,1)S(1)}, u32[]{:S(2)}, u32[]{:S(2)}) collective-permute-start(bf16[128,832]{1,0:T(8,128)(2,1)S(1)} %pad_maximum_fusion), channel_id=1, source_target_pairs={{0,12},{4,0},{8,4},{12,8},{1,13},{5,1},{9,5},{13,9},{2,14},{6,2},{... | collective-permute-start | bytes 638984 | tf_op jit(solution)/shard_map/ppermute | solution.py:29
  16.8 4.0 %copy-start.1 = (bf16[768,3072]{1,0:T(8,128)(2,1)S(1)}, bf16[768,3072]{1,0:T(8,128)(2,1)}, u32[]{:S(2)}) copy-start(bf16[768,3072]{1,0:T(8,128)(2,1)} %param.9) | copy-start | bytes 14155780
  20.2 6.0 %collective-permute-start.2 = (bf16[128,1536]{1,0:T(8,128)(2,1)S(1)}, bf16[128,1536]{1,0:T(8,128)(2,1)S(1)}, u32[]{:S(2)}, u32[]{:S(2)}) collective-permute-start(bf16[128,1536]{1,0:T(8,128)(2,1)S(1)} %constant_dynamic-slice_fusion.5), channel_id=1, source_target_pairs={{0,1},{1,0},{2,3},{3,2},{4,5},{5,4},{6,7},{7,6},{8,9},{9,8},{10,11... | collective-permute-start | bytes 1179656 | tf_op jit(solution)/shard_map/ppermute | solution.py:24
  21.7 15.1 %collective-permute-start.14 = (bf16[128,1536]{1,0:T(8,128)(2,1)S(1)}, bf16[128,1536]{1,0:T(8,128)(2,1)S(1)}, u32[]{:S(2)}, u32[]{:S(2)}) collective-permute-start(bf16[128,1536]{1,0:T(8,128)(2,1)S(1)} %constant_dynamic-slice_fusion.2), channel_id=1, source_target_pairs={{0,1},{1,0},{2,3},{3,2},{4,5},{5,4},{6,7},{7,6},{8,9},{9,8},{10,11... | collective-permute-start | bytes 1179656 | tf_op jit(solution)/shard_map/ppermute | solution.py:24
  21.8 9.8 %collective-permute-start.6 = (bf16[128,832]{1,0:T(8,128)(2,1)S(1)}, bf16[128,832]{1,0:T(8,128)(2,1)S(1)}, u32[]{:S(2)}, u32[]{:S(2)}) collective-permute-start(bf16[128,832]{1,0:T(8,128)(2,1)S(1)} %collective-permute-done.5), channel_id=1, source_target_pairs={{0,12},{4,0},{8,4},{12,8},{1,13},{5,1},{9,5},{13,9},{2,14},{6,2},{... | collective-permute-start | bytes 638984 | tf_op jit(solution)/shard_map/ppermute | solution.py:29
  26.2 17.0 %collective-permute-start.3 = (bf16[128,1536]{1,0:T(8,128)(2,1)S(1)}, bf16[128,1536]{1,0:T(8,128)(2,1)S(1)}, u32[]{:S(2)}, u32[]{:S(2)}) collective-permute-start(bf16[128,1536]{1,0:T(8,128)(2,1)S(1)} %add_convert_fusion.3), channel_id=1, source_target_pairs={{0,2},{2,0},{1,3},{3,1},{4,6},{6,4},{5,7},{7,5},{8,10},{10,8},{9,1... | collective-permute-start | bytes 1179656 | tf_op jit(solution)/shard_map/ppermute | solution.py:24
  32.4 11.7 %collective-permute-start.11 = (bf16[128,1536]{1,0:T(8,128)(2,1)S(1)}, bf16[128,1536]{1,0:T(8,128)(2,1)S(1)}, u32[]{:S(2)}, u32[]{:S(2)}) collective-permute-start(bf16[128,1536]{1,0:T(8,128)(2,1)S(1)} %constant_dynamic-slice_fusion.3), channel_id=1, source_target_pairs={{0,1},{1,0},{2,3},{3,2},{4,5},{5,4},{6,7},{7,6},{8,9},{9,8},{10,11... | collective-permute-start | bytes 1179656 | tf_op jit(solution)/shard_map/ppermute | solution.py:24
  32.5 9.8 %collective-permute-start.7 = (bf16[128,832]{1,0:T(8,128)(2,1)S(1)}, bf16[128,832]{1,0:T(8,128)(2,1)S(1)}, u32[]{:S(2)}, u32[]{:S(2)}) collective-permute-start(bf16[128,832]{1,0:T(8,128)(2,1)S(1)} %collective-permute-done.6), channel_id=1, source_target_pairs={{0,12},{4,0},{8,4},{12,8},{1,13},{5,1},{9,5},{13,9},{2,14},{6,2},{... | collective-permute-start | bytes 638984 | tf_op jit(solution)/shard_map/ppermute | solution.py:29
  37.0 12.0 %collective-permute-start.15 = (bf16[128,1536]{1,0:T(8,128)(2,1)S(1)}, bf16[128,1536]{1,0:T(8,128)(2,1)S(1)}, u32[]{:S(2)}, u32[]{:S(2)}) collective-permute-start(bf16[128,1536]{1,0:T(8,128)(2,1)S(1)} %add_convert_fusion), channel_id=1, source_target_pairs={{0,2},{2,0},{1,3},{3,1},{4,6},{6,4},{5,7},{7,5},{8,10},{10,8},{9,1... | collective-permute-start | bytes 1179656 | tf_op jit(solution)/shard_map/ppermute | solution.py:24
  43.2 6.2 %collective-permute-start.8 = (bf16[128,1536]{1,0:T(8,128)(2,1)S(1)}, bf16[128,1536]{1,0:T(8,128)(2,1)S(1)}, u32[]{:S(2)}, u32[]{:S(2)}) collective-permute-start(bf16[128,1536]{1,0:T(8,128)(2,1)S(1)} %constant_dynamic-slice_fusion.4), channel_id=1, source_target_pairs={{0,1},{1,0},{2,3},{3,2},{4,5},{5,4},{6,7},{7,6},{8,9},{9,8},{10,11... | collective-permute-start | bytes 1179656 | tf_op jit(solution)/shard_map/ppermute | solution.py:24
  43.6 7.5 %collective-permute-start.4 = (bf16[128,1536]{1,0:T(8,128)(2,1)S(1)}, bf16[128,1536]{1,0:T(8,128)(2,1)S(1)}, u32[]{:S(2)}, u32[]{:S(2)}) collective-permute-start(bf16[128,1536]{1,0:T(8,128)(2,1)S(1)} %fusion.6), channel_id=1, source_target_pairs={{0,1},{1,0},{2,3},{3,2},{4,5},{5,4},{6,7},{7,6},{8,9},{9,8},{10,11... | collective-permute-start | bytes 1179656 | tf_op jit(solution)/shard_map/ppermute | solution.py:24
  44.2 13.3 %collective-permute-start.12 = (bf16[128,1536]{1,0:T(8,128)(2,1)S(1)}, bf16[128,1536]{1,0:T(8,128)(2,1)}, u32[]{:S(2)}, u32[]{:S(2)}) collective-permute-start(bf16[128,1536]{1,0:T(8,128)(2,1)S(1)} %add_convert_fusion.1), channel_id=1, source_target_pairs={{0,2},{2,0},{1,3},{3,1},{4,6},{6,4},{5,7},{7,5},{8,10},{10,8},{9,1... | collective-permute-start | bytes 1179656 | tf_op jit(solution)/shard_map/ppermute | solution.py:24
  49.3 9.6 %collective-permute-start.16 = (bf16[128,1536]{1,0:T(8,128)(2,1)S(1)}, bf16[128,1536]{1,0:T(8,128)(2,1)}, u32[]{:S(2)}, u32[]{:S(2)}) collective-permute-start(bf16[128,1536]{1,0:T(8,128)(2,1)S(1)} %fusion.21), channel_id=1, source_target_pairs={{0,1},{1,0},{2,3},{3,2},{4,5},{5,4},{6,7},{7,6},{8,9},{9,8},{10,11... | collective-permute-start | bytes 1179656 | tf_op jit(solution)/shard_map/ppermute | solution.py:24
  49.5 19.6 %collective-permute-start.9 = (bf16[128,1536]{1,0:T(8,128)(2,1)S(1)}, bf16[128,1536]{1,0:T(8,128)(2,1)}, u32[]{:S(2)}, u32[]{:S(2)}) collective-permute-start(bf16[128,1536]{1,0:T(8,128)(2,1)S(1)} %add_convert_fusion.2), channel_id=1, source_target_pairs={{0,2},{2,0},{1,3},{3,1},{4,6},{6,4},{5,7},{7,5},{8,10},{10,8},{9,1... | collective-permute-start | bytes 1179656 | tf_op jit(solution)/shard_map/ppermute | solution.py:24
  58.9 11.9 %collective-permute-start.13 = (bf16[128,1536]{1,0:T(8,128)(2,1)S(1)}, bf16[128,1536]{1,0:T(8,128)(2,1)}, u32[]{:S(2)}, u32[]{:S(2)}) collective-permute-start(bf16[128,1536]{1,0:T(8,128)(2,1)S(1)} %fusion.16), channel_id=1, source_target_pairs={{0,1},{1,0},{2,3},{3,2},{4,5},{5,4},{6,7},{7,6},{8,9},{9,8},{10,11... | collective-permute-start | bytes 1179656 | tf_op jit(solution)/shard_map/ppermute | solution.py:24
  64.0 4.7 %copy-start.9 = (f32[128,66]{0,1:T(8,128)S(1)}, f32[128,66]{0,1:T(8,128)}, u32[]{:S(2)}) copy-start(f32[128,66]{0,1:T(8,128)} %copy-done.8) | copy-start | bytes 101380
  64.0 4.7 %copy-start.11 = (bf16[128,1536]{1,0:T(8,128)(2,1)S(1)}, bf16[128,1536]{1,0:T(8,128)(2,1)}, u32[]{:S(2)}) copy-start(bf16[128,1536]{1,0:T(8,128)(2,1)} %copy-done.10) | copy-start | bytes 1179652
  64.1 11.8 %collective-permute-start.17 = (bf16[128,832]{1,0:T(8,128)(2,1)S(1)}, bf16[128,832]{1,0:T(8,128)(2,1)S(1)}, u32[]{:S(2)}, u32[]{:S(2)}) collective-permute-start(bf16[128,832]{1,0:T(8,128)(2,1)S(1)} %pad_maximum_fusion.1), channel_id=1, source_target_pairs={{0,12},{4,0},{8,4},{12,8},{1,13},{5,1},{9,5},{13,9},{2,14},{6,2},{... | collective-permute-start | bytes 638984 | tf_op jit(solution)/shard_map/ppermute | solution.py:29
  70.5 8.3 %collective-permute-start.10 = (bf16[128,1536]{1,0:T(8,128)(2,1)S(1)}, bf16[128,1536]{1,0:T(8,128)(2,1)S(1)}, u32[]{:S(2)}, u32[]{:S(2)}) collective-permute-start(bf16[128,1536]{1,0:T(8,128)(2,1)S(1)} %fusion.11), channel_id=1, source_target_pairs={{0,1},{1,0},{2,3},{3,2},{4,5},{5,4},{6,7},{7,6},{8,9},{9,8},{10,11... | collective-permute-start | bytes 1179656 | tf_op jit(solution)/shard_map/ppermute | solution.py:24
  70.8 8.1 %slice-start = ((s8[4718592]{0:T(1024)(128)(4,1)}), s8[4194304]{0:T(1024)(128)(4,1)S(1)}, s32[]{:S(2)}) async-start(s8[4718592]{0:T(1024)(128)(4,1)} %bitcast.23), calls=%async_computation | async-start | bytes 8388608
  74.3 4.5 %slice-start.1 = ((s8[4718592]{0:T(1024)(128)(4,1)}), s8[524288]{0:T(1024)(128)(4,1)S(1)}, s32[]{:S(2)}) async-start(s8[4718592]{0:T(1024)(128)(4,1)} %bitcast.23), calls=%async_computation.1 | async-start | bytes 1048576
  75.9 8.0 %collective-permute-start.18 = (bf16[128,832]{1,0:T(8,128)(2,1)S(1)}, bf16[128,832]{1,0:T(8,128)(2,1)S(1)}, u32[]{:S(2)}, u32[]{:S(2)}) collective-permute-start(bf16[128,832]{1,0:T(8,128)(2,1)S(1)} %fusion.23), channel_id=1, source_target_pairs={{0,12},{4,0},{8,4},{12,8},{1,13},{5,1},{9,5},{13,9},{2,14},{6,2},{... | collective-permute-start | bytes 638984 | tf_op jit(solution)/shard_map/ppermute | solution.py:29
  84.0 7.1 %copy-start.3 = (bf16[128,768]{1,0:T(8,128)(2,1)S(1)}, bf16[128,768]{1,0:T(8,128)(2,1)}, u32[]{:S(2)}) copy-start(bf16[128,768]{1,0:T(8,128)(2,1)} %convolution_convert_fusion.5) | copy-start | bytes 589828
  84.1 7.1 %copy-start.7 = (bf16[128,64]{1,0:T(8,128)(2,1)S(1)}, bf16[128,64]{1,0:T(8,128)(2,1)}, u32[]{:S(2)}) copy-start(bf16[128,64]{1,0:T(8,128)(2,1)} %copy.16) | copy-start | bytes 49156
  84.1 7.1 %copy-start.2 = (bf16[128,768]{1,0:T(8,128)(2,1)S(1)}, bf16[128,768]{1,0:T(8,128)(2,1)}, u32[]{:S(2)}) copy-start(bf16[128,768]{1,0:T(8,128)(2,1)} %param.15) | copy-start | bytes 589828
  84.1 7.1 %collective-permute-start.19 = (bf16[128,832]{1,0:T(8,128)(2,1)S(1)}, bf16[128,832]{1,0:T(8,128)(2,1)S(1)}, u32[]{:S(2)}, u32[]{:S(2)}) collective-permute-start(bf16[128,832]{1,0:T(8,128)(2,1)S(1)} %fusion.22), channel_id=1, source_target_pairs={{0,12},{4,0},{8,4},{12,8},{1,13},{5,1},{9,5},{13,9},{2,14},{6,2},{... | collective-permute-start | bytes 638984 | tf_op jit(solution)/shard_map/ppermute | solution.py:29
  91.5 6.0 %collective-permute-start.22 = (bf16[64,768]{1,0:T(8,128)(2,1)S(1)}, bf16[64,768]{1,0:T(8,128)(2,1)S(1)}, u32[]{:S(2)}, u32[]{:S(2)}) collective-permute-start(bf16[64,768]{1,0:T(8,128)(2,1)S(1)} %fusion.1), channel_id=1, source_target_pairs={{0,12},{4,0},{8,4},{12,8},{1,13},{5,1},{9,5},{13,9},{2,14},{6,2},{... | collective-permute-start | bytes 294920 | tf_op jit(solution)/shard_map/ppermute | solution.py:29
  95.0 6.5 %collective-permute-start.21 = (bf16[64,768]{1,0:T(8,128)(2,1)S(1)}, bf16[64,768]{1,0:T(8,128)(2,1)S(1)}, u32[]{:S(2)}, u32[]{:S(2)}) collective-permute-start(bf16[64,768]{1,0:T(8,128)(2,1)S(1)} %fusion.1), channel_id=1, source_target_pairs={{0,4},{4,8},{8,12},{12,0},{1,5},{5,9},{9,13},{13,1},{2,6},{6,10},{... | collective-permute-start | bytes 294920 | tf_op jit(solution)/shard_map/ppermute | solution.py:29
  95.0 7.9 %collective-permute-start.20 = (bf16[64,768]{1,0:T(8,128)(2,1)S(1)}, bf16[64,768]{1,0:T(8,128)(2,1)S(1)}, u32[]{:S(2)}, u32[]{:S(2)}) collective-permute-start(bf16[64,768]{1,0:T(8,128)(2,1)S(1)} %fusion.1), channel_id=1, source_target_pairs={{0,8},{4,12},{8,0},{12,4},{1,9},{5,13},{9,1},{13,5},{2,10},{6,14},... | collective-permute-start | bytes 294920 | tf_op jit(solution)/shard_map/ppermute | solution.py:29
  (5 other events, 4.0 us)

commit v2 on v1

v2 whole, which is shorter than its diff:
```python
import functools

import jax
import jax.numpy as jnp
from jax import lax
from jax.experimental import pallas as pl
from jax.experimental.pallas import tpu as pltpu
from jax.sharding import PartitionSpec as P

adapter_scale = 0.5
norm_eps = 1e-06
gelu_coef = 0.7978845608028654
f32 = jnp.float32
bf16 = jnp.bfloat16
LANES = 128


def gelu_value(pre_value):
    inner_arg = gelu_coef * (pre_value + 0.044715 * pre_value * pre_value * pre_value)
    return 0.5 * pre_value * (1.0 + jnp.tanh(inner_arg))


def dot(left, right):
    return jnp.dot(left, right, preferred_element_type=f32)


def dot_transposed(left, right):
    return lax.dot_general(left, right, (((1,), (1,)), ((), ())), preferred_element_type=f32)


def dot_rows(left, right):
    return lax.dot_general(left, right, (((0,), (0,)), ((), ())), preferred_element_type=f32)


def split_dot(product, left, right):
    high = left.astype(bf16)
    low = (left - high.astype(f32)).astype(bf16)
    return product(high, right) + product(low, right)


def swap(value, axis, distance):
    size = lax.axis_size(axis)
    return lax.ppermute(value, axis, [(i, i ^ distance) for i in range(size)])


def shift(value, axis, distance):
    size = lax.axis_size(axis)
    return lax.ppermute(value, axis, [(i, (i + distance) % size) for i in range(size)])


def exchange(value, axis, kind):
    distance, size = 1, lax.axis_size(axis)
    while True:
        other = swap(value, axis, distance)
        distance *= 2
        if distance >= size:
            return value, other
        value = (value.astype(f32) + other.astype(f32)).astype(kind)


def call(body, outs, arrays, after=(), scratch=(), remote=(), scalars=(), grant=24 * 2**20):
    vmem = pl.BlockSpec(memory_space=pltpu.VMEM)
    specs = [pl.BlockSpec(memory_space=pltpu.SMEM)] * len(scalars)
    specs += [pl.BlockSpec(memory_space=pltpu.HBM)] * len(remote) + [vmem] * len(arrays)
    count = len(specs)
    specs += [pl.BlockSpec(memory_space=pl.ANY)] * len(after)
    total = len(specs)

    def kernel(*refs):
        body(*refs[:count], *refs[total:])

    return pl.pallas_call(
        kernel,
        out_shape=[jax.ShapeDtypeStruct(shape, kind) for shape, kind in outs],
        in_specs=specs,
        out_specs=[vmem] * len(outs),
        scratch_shapes=list(scratch),
        compiler_params=pltpu.CompilerParams(vmem_limit_bytes=grant),
        cost_estimate=pl.CostEstimate(flops=1024, bytes_accessed=1024, transcendentals=0),
        name=body.__name__,
    )(*scalars, *remote, *arrays, *after)


def cut(width):
    return width // 2 // LANES * LANES


def columns(width, step=512):
    return [slice(at, min(at + step, width)) for at in range(0, width, step)]


def rows_at(place, count):
    return pl.ds(pl.multiple_of(place * count, count), count)


def own_core():
    return lax.axis_index("sub")


def row_sums(step, x_hbm, cot_hbm, mod_hbm, second_hbm, packed, x, back, mod, factor, cot, table, sems):
    rows, features = x.shape
    rank = factor.shape[0]
    block = lax.axis_index("narrow") * lax.axis_size("sub") + lax.axis_index("sub")
    at = pl.ds(pl.multiple_of(block * features, LANES), features)
    copies = [
        pltpu.make_async_copy(mod_hbm, table, sems.at[0]),
        pltpu.make_async_copy(cot_hbm, cot, sems.at[1]),
        pltpu.make_async_copy(second_hbm.at[:, at], factor, sems.at[2]),
        pltpu.make_async_copy(x_hbm, x, sems.at[3]),
    ]
    for copy in copies:
        copy.start()
    copies[0].wait()
    for kind in range(3):
        mod[kind : kind + 1, :] = table[kind, pl.ds(step[0], 1), :]
    for copy in copies[1:]:
        copy.wait()
    back_rows = (mod[2:3, :] * cot[...].astype(f32)).astype(bf16)
    back[...] = back_rows
    padded = jnp.concatenate([factor[...], jnp.zeros((LANES - rank, features), bf16)], axis=0)
    low = dot_transposed(back_rows, padded)
    values = x[...].astype(f32)
    total = jnp.sum(values, axis=1, keepdims=True)
    squares = jnp.sum(values * values, axis=1, keepdims=True)
    lane = lax.broadcasted_iota(jnp.int32, (rows, LANES), 1)
    packed[...] = jnp.where(lane == rank, total, jnp.where(lane == rank + 1, squares, low))


def load_weight(weight_hbm, weight, sem):
    copy = pltpu.make_async_copy(weight_hbm, weight, sem)
    copy.start()
    copy.wait()


def add_packed(left, right, out):
    out[...] = left[...] + right[...]


def store_product(at, product, count, kept, left, right):
    kept[:, at] = product[:count]
    if at.start < left.shape[1]:
        left[:, at] = product[count:]
    else:
        right[:, slice(at.start - left.shape[1], at.stop - left.shape[1])] = product[count:]


def up_columns(width):
    middle = cut(width)
    return columns(middle) + [slice(at.start + middle, at.stop + middle) for at in columns(width - middle)]


def up_rows(normed, weight, kept, left, right):
    middle = normed.shape[0] // 2
    features = weight.shape[0]
    own = own_core()
    rows = jnp.concatenate(
        [normed[rows_at(own, middle), :features], normed[rows_at(1 - own, middle), :features]],
        axis=0,
    )
    for at in up_columns(weight.shape[1]):
        store_product(at, dot(rows, weight[:, at]).astype(bf16), middle, kept, left, right)


def normalize_up(model_width, rank, x, mine, other, mod, weight, travelling, kept, left, right):
    features = x.shape[1]
    packed = mine[...] + other[...]
    row_mean = packed[:, rank : rank + 1] / model_width
    row_msq = packed[:, rank + 1 : rank + 2] / model_width
    inv_std = lax.rsqrt(row_msq - row_mean * row_mean + norm_eps)
    travelling[:, :features] = (
        (x[...].astype(f32) - row_mean) * inv_std * (1.0 + mod[1:2, :]) + mod[0:1, :]
    ).astype(bf16)
    travelling[:, features:] = packed.astype(bf16)
    quarter = x.shape[0] // 4
    own = own_core()
    rows = jnp.concatenate(
        [
            travelling[rows_at(own, quarter), :features],
            travelling[rows_at(2 + own, quarter), :features],
            travelling[rows_at(1 - own, quarter), :features],
            travelling[rows_at(3 - own, quarter), :features],
        ],
        axis=0,
    )
    for at in up_columns(weight.shape[1]):
        product = dot(rows, weight[:, at]).astype(bf16)
        store_product(at, product, 2 * quarter, kept, left, right)


def sum_rows(kept, left, right, rows, out):
    middle = left.shape[1]
    out[:, :middle] = (kept[rows, :middle].astype(f32) + left[rows, :].astype(f32)).astype(bf16)
    out[:, middle:] = (kept[rows, middle:].astype(f32) + right[rows, :].astype(f32)).astype(bf16)


def add_own(kept, left, right, travelling, first, last, passed):
    middle = first.shape[0]
    sum_rows(kept, left, right, slice(0, middle), first)
    sum_rows(kept, left, right, slice(middle, 2 * middle), last)
    passed[...] = travelling[...]


def add_cores(kept, left, right, out):
    sum_rows(kept, left, right, slice(0, out.shape[0]), out)


def add_cores_pass(kept, left, right, last, out, passed):
    sum_rows(kept, left, right, slice(0, out.shape[0]), out)
    passed[...] = last[...]


def gelu_rows(mine, other, left, right):
    width = left.shape[1]
    for out, base in ((left, 0), (right, width)):
        for at in columns(out.shape[1]):
            source = slice(at.start + base, at.stop + base)
            pre_act = mine[:, source].astype(f32) + other[:, source].astype(f32)
            out[:, at] = gelu_value(pre_act).astype(bf16)


def two_halves(own, other):
    return [jnp.concatenate([a[...], b[...]], axis=0) for a, b in zip(own, other)]


def low_product(activated, first):
    left, right = activated
    hidden = left.shape[1] + right.shape[1]
    base = lax.axis_index("loop") * hidden
    factor_left = first[:, pl.ds(pl.multiple_of(base, LANES), left.shape[1])]
    factor_right = first[:, pl.ds(pl.multiple_of(base + left.shape[1], LANES), right.shape[1])]
    return dot_transposed(left, factor_left) + dot_transposed(right, factor_right)


def down_product(activated, weight, at):
    left, right = activated
    middle = left.shape[1]
    return dot(left, weight[:middle, at]) + dot(right, weight[middle:, at])


def store_rows(out, at, value):
    middle = value.shape[0] // 2
    own = own_core()
    out[rows_at(own, middle), at] = value[:middle].astype(out.dtype)
    out[rows_at(1 - own, middle), at] = value[middle:].astype(out.dtype)


def down_rows(left, right, other_left, other_right, weight, first, out):
    activated = two_halves((left, right), (other_left, other_right))
    features = weight.shape[1]
    low = low_product(activated, first)
    low = jnp.concatenate([low, jnp.zeros((low.shape[0], LANES - low.shape[1]), f32)], axis=1)
    store_rows(out, slice(features, features + LANES), low)
    for at in columns(features, 256):
        store_rows(out, at, down_product(activated, weight, at))


def down_rows_add(left, right, other_left, other_right, weight, first, received, out, total):
    down_rows(left, right, other_left, other_right, weight, first, total)
    out[...] = (total[...] + received[...].astype(f32)).astype(bf16)


def down_own(left, right, other_left, other_right, weight, first, out):
    middle = out.shape[0] // 2
    down_rows(left, right, other_left, other_right, weight, first, out.at[:middle])
    out[middle:] = jnp.zeros((middle, out.shape[1]), f32)


def down_own_add(left, right, other_left, other_right, weight, first, received, out):
    down_own(left, right, other_left, other_right, weight, first, out)
    out[...] += received[...].astype(f32)


def first_gradient_part(*refs):
    blocks, out = refs[:-1], refs[-1]
    own = own_core()
    rank = out.shape[0]
    features = blocks[4].shape[1] - LANES
    middle = blocks[0].shape[1]
    factors = []
    for at in range(0, len(blocks), 5):
        count = blocks[at].shape[0]
        travelling = blocks[at + 4]
        factors += [travelling[rows_at(own, count), features:], travelling[rows_at(1 - own, count), features:]]
    factors = jnp.concatenate(factors, axis=0)
    for half, base in ((0, 0), (1, middle)):
        for at in columns(blocks[half].shape[1]):
            right = []
            for place in range(0, len(blocks), 5):
                right += [blocks[place + half][:, at], blocks[place + 2 + half][:, at]]
            product = dot_rows(factors, jnp.concatenate(right, axis=0))
            out[:, slice(at.start + base, at.stop + base)] = product[:rank]


def first_gradient_end(left, right, other_left, other_right, travelling, part, out):
    own = own_core()
    rank = out.shape[0]
    count = left.shape[0]
    features = travelling.shape[1] - LANES
    factors = jnp.concatenate(
        [travelling[rows_at(2 + own, count), features:], travelling[rows_at(3 - own, count), features:]],
        axis=0,
    )
    base = 0
    for mine, other in ((left, other_left), (right, other_right)):
        for at in columns(mine.shape[1]):
            product = dot_rows(factors, jnp.concatenate([mine[:, at], other[:, at]], axis=0))
            to = slice(at.start + base, at.stop + base)
            out[:, to] = adapter_scale * (part[:, to] + product[:rank])
        base += mine.shape[1]


def second_gradient_part(
    left, right, other_left, other_right, first, own_down, received, back, out, low_total, low
):
    activated = two_halves((left, right), (other_left, other_right))
    rank = first.shape[0]
    features = back.shape[1]
    store_rows(low, slice(0, rank), low_product(activated, first))
    sums = received[:, features : features + rank].astype(f32) + own_down[:, features : features + rank]
    middle = low.shape[0]
    sums = jnp.concatenate([sums[:middle], sums[middle:] + low[...]], axis=0)
    low_total[...] = sums
    out[...] = (adapter_scale * split_dot(dot_rows, sums, back[...])).astype(bf16)


def update_rows(
    left, right, other_left, other_right, weight, own_down, received, low_total, factor, mod, out, total
):
    activated = two_halves((left, right), (other_left, other_right))
    features = weight.shape[1]
    for at in columns(features, 256):
        store_rows(total, at, down_product(activated, weight, at))
    gate = mod[2:3, :]
    low = adapter_scale * split_dot(dot, low_total[...], factor[...])
    base = received[:, :features].astype(f32) + own_down[:, :features] + low
    middle = total.shape[0]
    out[:middle] = (gate * base[:middle]).astype(bf16)
    out[middle:] = (gate * (base[middle:] + total[...])).astype(bf16)


def add_four(own, one, two, three, out):
    out[...] = (own[...].astype(f32) + two[...].astype(f32)) + (
        one[...].astype(f32) + three[...].astype(f32)
    )


def per_device(
    block_input_rows,
    frozen_up_weight,
    frozen_down_weight,
    down_first_factor,
    down_second_factor,
    modulation,
    timestep_index,
    cotangent,
):
    loop_size = lax.axis_size("loop")
    wide_size = lax.axis_size("narrow") * lax.axis_size("sub")
    rows, features = block_input_rows.shape
    hidden = frozen_up_weight.shape[1]
    rank = down_first_factor.shape[1]
    middle, quarter = rows // 2, rows // 4
    wide = features + LANES
    first = down_first_factor.T
    part = cut(hidden)
    dma = pltpu.SemaphoreType.DMA

    def swap_halves(left, right):
        return [swap(left, "sub", 1), swap(right, "sub", 1)]

    packed, x, back, mod, second = call(
        row_sums,
        [
            ((rows, LANES), f32),
            ((rows, features), bf16),
            ((rows, features), bf16),
            ((8, features), f32),
            ((rank, features), bf16),
        ],
        [],
        scratch=[
            pltpu.VMEM((rows, features), bf16),
            pltpu.VMEM((3, modulation.shape[0], features), f32),
            dma((4,)),
        ],
        scalars=[timestep_index],
        remote=[block_input_rows, cotangent, jnp.transpose(modulation, (1, 0, 2)), down_second_factor],
    )
    (packed,) = call(
        add_packed, [((rows, LANES), f32)], [packed, swap(packed, "sub", 1)], [back]
    )
    (up_weight,) = call(
        load_weight,
        [((features, hidden), bf16)],
        [],
        [packed],
        scratch=[dma],
        remote=[frozen_up_weight],
    )
    mine, other = exchange(packed, "narrow", f32)
    body = functools.partial(normalize_up, wide_size * features, rank)
    body.__name__ = "normalize_up"

    def halves(count):
        return [((count, part), bf16), ((count, hidden - part), bf16)]

    travelling, kept, left, right = call(
        body,
        [((rows, wide), bf16), ((middle, hidden), bf16), *halves(middle)],
        [x, mine, other, mod, up_weight],
    )
    first_sum, last_sum, travelling = call(
        add_own,
        [((quarter, hidden), bf16), ((quarter, hidden), bf16), ((rows, wide), bf16)],
        [kept, *swap_halves(left, right), travelling],
    )
    first_pair = exchange(first_sum, "narrow", bf16)
    if loop_size == 4:
        near, far = swap(travelling, "loop", 1), swap(travelling, "loop", 2)
        blocks = [near, swap(far, "loop", 1), far]
    else:
        blocks = [travelling]
        for _ in range(loop_size - 1):
            blocks.append(shift(blocks[-1], "loop", -1))
        blocks = blocks[1:]
    pairs = []
    activated = []

    def activate(pair, after):
        left, right = call(gelu_rows, halves(pair[0].shape[0]), list(pair), after)
        activated.append([left, right, *swap_halves(left, right)])
        return activated[-1]

    after = [first_sum]
    for place, block in enumerate(blocks):
        if place == 2:
            after = activate(pairs[0], after)[:1]
        kept, left, right = call(
            up_rows,
            [((middle, hidden), bf16), *halves(middle)],
            [block, up_weight],
            after,
        )
        after = [kept]
        if place == 0:
            after = activate(first_pair, after)
        operands = [kept, *swap_halves(left, right)]
        if place < loop_size - 2:
            (value,) = call(add_cores, [((middle, hidden), bf16)], operands, after)
        else:
            value, last_sum = call(
                add_cores_pass,
                [((middle, hidden), bf16), ((quarter, hidden), bf16)],
                [*operands, last_sum],
                after,
            )
        after = [value]
        pairs.append(exchange(value, "narrow", bf16))
    last_pair = exchange(last_sum, "narrow", bf16)

    down_sum = None
    own_down = None
    for place in range(loop_size - 1):
        if len(activated) < place + 2:
            after = activate(pairs[place], after)[:1]
        operands = [*activated[place + 1], frozen_down_weight, first]
        if down_sum is None:
            (joined,) = call(down_rows, [((rows, wide), bf16)], operands, after)
        else:
            (joined,) = call(
                down_rows_add,
                [((rows, wide), bf16)],
                [*operands, down_sum],
                after,
                scratch=[pltpu.VMEM((rows, wide), f32)],
            )
        after = [joined]
        operands = [*activated[0], frozen_down_weight, first]
        if loop_size != 4:
            down_sum = shift(joined, "loop", -1)
            if place == 0:
                (own_down,) = call(down_own, [((rows, wide), f32)], operands, after)
                after = [own_down]
        elif place == 0:
            own_part = swap(joined, "loop", 1)
        elif place == 1:
            down_sum = swap(joined, "loop", 1)
            (own_down,) = call(down_own_add, [((rows, wide), f32)], [*operands, own_part], after)
            after = [own_down]
        else:
            down_sum = swap(joined, "loop", 2)
    gathered = []
    for parts, block in zip(activated, [travelling] + blocks):
        gathered += [*parts, block]
    (gradient,) = call(first_gradient_part, [((rank, hidden), f32)], gathered, after)
    last = activate(last_pair, [gradient])
    contribution, low_total = call(
        second_gradient_part,
        [((rank, features), bf16), ((rows, rank), f32)],
        [*last, first, own_down, down_sum, back],
        scratch=[pltpu.VMEM((middle, rank), f32)],
    )
    (block_update,) = call(
        update_rows,
        [((rows, features), bf16)],
        [*last, frozen_down_weight, own_down, down_sum, low_total, second, mod],
        scratch=[pltpu.VMEM((middle, features), f32)],
    )
    (first_gradient,) = call(
        first_gradient_end,
        [((rank, hidden), f32)],
        [*last, travelling, gradient],
        [low_total],
    )
    if loop_size == 4:
        others = [shift(contribution, "loop", k) for k in (1, 2, 3)]
        (second_gradient,) = call(
            add_four, [((rank, features), f32)], [contribution, *others], [block_update]
        )
    else:
        second_gradient = lax.psum(contribution, "loop").astype(f32)
    return (block_update, first_gradient.T, second_gradient)


def solution(mesh):
    in_specs = (
        P(("groups", "loop"), ("narrow", "sub")),
        P(("narrow", "sub"), "loop"),
        P("loop", ("narrow", "sub")),
        P(),
        P(),
        P(None, None, ("narrow", "sub")),
        P("groups"),
        P(("groups", "loop"), ("narrow", "sub")),
    )
    out_specs = (
        P(("groups", "loop"), ("narrow", "sub")),
        P(("groups", "loop"), None),
        P("groups", ("narrow", "sub")),
    )
    return jax.shard_map(
        per_device, mesh=mesh, in_specs=in_specs, out_specs=out_specs, check_vma=False
    )
```

time: 104 us -> 91.2 us (0.88)
  matrix products: 29.9 us -> 0 us
  Pallas kernels: 0 us -> 15.1 us
  waiting for transfers between devices: 26.8 us -> 41.9 us
  starting transfers between devices: 34.9 us -> 25.3 us
  other arithmetic: 7.78 us -> 0.01 us
  local copies, waits for them, and re-layouts: 2.5 us -> 7.01 us
    ppermute x14 -> x31, waiting for transfers between devices: 6.52 us -> 37.9 us  [swap(): return lax.ppermute(value, axis, [(i, i ^ distance) for i in range(size)])]
    dot_general x19 -> x0, matrix products: 29.9 us -> none  [the longest x12 21.2 us: dot(): return jnp.dot(left, right, preferred_element_type=f32)]
    ppermute x9 -> x3, starting transfers between devices: 24 us -> 3.87 us  [shift(): lax.ppermute(value, axis, [(i, (i + distance) % size) for i in range(size)])]
    ppermute x9 -> x3, waiting for transfers between devices: 20.3 us -> 3.99 us  [shift(): lax.ppermute(value, axis, [(i, (i + distance) % size) for i in range(size)])]
    pallas_call x0 -> x25, Pallas kernels: none -> 15.1 us  [call(): pl.pallas_call(kernel, out_shape=[jax.ShapeDtypeStruct(shape, kind) for s...]
    ppermute x14 -> x31, starting transfers between devices: 10.9 us -> 21.4 us  [swap(): return lax.ppermute(value, axis, [(i, i ^ distance) for i in range(size)])]
    unnamed x28 -> x18, local copies, waits for them, and re-layouts: 1.41 us -> 7.01 us
    convert_element_type x11 -> x0, other arithmetic: 4.92 us -> none  [the longest x4 3.31 us: per_device(): own_half = gelu_value(pre_act).astype(bf16)]
  transfers between devices with their start and end apart: 23 -> 34, of which waited for: 11 -> 22; matrix products, arithmetic and copies ran while one was open for 32% -> 0% of each run, Pallas kernels for 0% -> 13%
where the time goes in v2:
time: 91.2 us; the launch traced here: 90.8 us
  waiting for transfers between devices  41.9 us (46%)
  starting transfers between devices  25.3 us (28%)
  Pallas kernels  15.1 us (17%)
  local copies, waits for them, and re-layouts  7.01 us (8%)
  between operations  1.58 us (2%)
    ppermute x31, waiting for transfers between devices, swap(): return lax.ppermute(value, axis, [(i, i ^ distance) for i in range(size)])  37.9 us
    ppermute x31, starting transfers between devices, swap(): return lax.ppermute(value, axis, [(i, i ^ distance) for i in range(size)])  21.4 us
    pallas_call x25, Pallas kernels, call(): pl.pallas_call(kernel, out_shape=[jax.ShapeDtypeStruct(shape, kind) for s...  15.1 us
    unnamed x18, local copies, waits for them, and re-layouts  7.01 us
    ppermute x3, waiting for transfers between devices, shift(): lax.ppermute(value, axis, [(i, (i + distance) % size) for i in range(size)])  3.99 us
    ppermute x3, starting transfers between devices, shift(): lax.ppermute(value, axis, [(i, (i + distance) % size) for i in range(size)])  3.87 us
  transfers between devices with their start and end apart: 34, of which 22 were waited for; matrix products, arithmetic and copies ran while one was open for 0% of the time, Pallas kernels for 13%

profile of v2, /device:TPU:0, one launch (start us, length us, event | category | flops | bytes accessed | tf_op | source)
XLA Modules:
  0.0 90.8 jit_solution(17225252072919366661)
XLA Ops:
  1.3 1.0 %copy-done.3 = bf16[64,3072]{1,0:T(8,128)(2,1)S(1)} copy-done((bf16[64,3072]{1,0:T(8,128)(2,1)S(1)}, bf16[64,3072]{1,0:T(8,128)(2,1)}, u32[]{:S(2)}) %copy-start.3) | copy-done | bytes 393240
  2.3 0.9 %copy-done.4 = bf16[128,768]{1,0:T(8,128)(2,1)S(1)} copy-done((bf16[128,768]{1,0:T(8,128)(2,1)S(1)}, bf16[128,768]{1,0:T(8,128)(2,1)}, u32[]{:S(2)}) %copy-start.4) | copy-done | bytes 196632
  7.3 2.9 %collective-permute-start.1 = (f32[128,128]{1,0:T(8,128)S(1)}, f32[128,128]{1,0:T(8,128)S(1)}, u32[]{:S(2)}, u32[]{:S(2)}) collective-permute-start(f32[128,128]{1,0:T(8,128)S(1)} %add_packed.1.refs_1_), channel_id=1, source_target_pairs={{0,2},{2,0},{1,3},{3,1},{4,6},{6,4},{5,7},{7,5},{8,10},{10,8},{9,1... | collective-permute-start | bytes 196616 | tf_op jit(solution)/shard_map/ppermute | solution.py:43
  10.2 2.3 %copy-done.1 = bf16[768,3072]{1,0:T(8,128)(2,1)S(1)} copy-done((bf16[768,3072]{1,0:T(8,128)(2,1)S(1)}, bf16[768,3072]{1,0:T(8,128)(2,1)}, u32[]{:S(2)}) %copy-start.1) | copy-done | bytes 4718616
  12.9 1.0 %normalize_up.1 = (bf16[128,896]{1,0:T(8,128)(2,1)S(1)}, bf16[64,3072]{1,0:T(8,128)(2,1)S(1)}, bf16[64,1536]{1,0:T(8,128)(2,1)S(1)}, bf16[64,1536]{1,0:T(8,128)(2,1)S(1)}) custom-call(bf16[128,768]{1,0:T(8,128)(2,1)S(1)} %get-tuple-element.38.refs_0_, f32[128,128]{1,0:T(8,128)S(1)} %add_packed.1.refs_1_, f32[128,128]{1,0:T(8,128)S(1)} %collective-permute-done.1.refs_2_, ...), custom_call_target="tpu_custom_call" | custom-call | flops 1024 | bytes 1024 | tf_op jit(solution)/shard_map/normalize_up/pallas_call | solution.py:72
  14.4 0.9 %collective-permute-done.2.refs_1_ = bf16[64,1536]{1,0:T(8,128)(2,1)S(1)} collective-permute-done((bf16[64,1536]{1,0:T(8,128)(2,1)S(1)}, bf16[64,1536]{1,0:T(8,128)(2,1)S(1)}, u32[]{:S(2)}, u32[]{:S(2)}) %collective-permute-start.2) | collective-permute-done | bytes 196640 | tf_op jit(solution)/shard_map/ppermute | solution.py:43
  15.7 1.7 %collective-permute-start.5 = (bf16[128,896]{1,0:T(8,128)(2,1)S(1)}, bf16[128,896]{1,0:T(8,128)(2,1)S(1)}, u32[]{:S(2)}, u32[]{:S(2)}) collective-permute-start(bf16[128,896]{1,0:T(8,128)(2,1)S(1)} %get-tuple-element.46.refs_4_), channel_id=1, source_target_pairs={{0,4},{4,0},{8,12},{12,8},{1,5},{5,1},{9,13},{13,9},{2,6},{6,2},{1... | collective-permute-start | bytes 688136 | tf_op jit(solution)/shard_map/ppermute | solution.py:43
  17.5 1.5 %collective-permute-start.8 = (bf16[32,3072]{1,0:T(8,128)(2,1)S(1)}, bf16[32,3072]{1,0:T(8,128)(2,1)S(1)}, u32[]{:S(2)}, u32[]{:S(2)}) collective-permute-start(bf16[32,3072]{1,0:T(8,128)(2,1)S(1)} %get-tuple-element.47.refs_2_.refs_0_), channel_id=1, source_target_pairs={{0,2},{2,0},{1,3},{3,1},{4,6},{6,4},{5,7},{7,5},{8,10},{10,8},{9,1... | collective-permute-start | bytes 589832 | tf_op jit(solution)/shard_map/ppermute | solution.py:43
  19.0 2.6 %collective-permute-start.4 = (bf16[128,896]{1,0:T(8,128)(2,1)S(1)}, bf16[128,896]{1,0:T(8,128)(2,1)S(1)}, u32[]{:S(2)}, u32[]{:S(2)}) collective-permute-start(bf16[128,896]{1,0:T(8,128)(2,1)S(1)} %get-tuple-element.46.refs_4_), channel_id=1, source_target_pairs={{0,8},{4,12},{8,0},{12,4},{1,9},{5,13},{9,1},{13,5},{2,10},{6,14},... | collective-permute-start | bytes 688136 | tf_op jit(solution)/shard_map/ppermute | solution.py:43
  21.6 5.6 %collective-permute-done.5.refs_0_.refs_9_ = bf16[128,896]{1,0:T(8,128)(2,1)S(1)} collective-permute-done((bf16[128,896]{1,0:T(8,128)(2,1)S(1)}, bf16[128,896]{1,0:T(8,128)(2,1)S(1)}, u32[]{:S(2)}, u32[]{:S(2)}) %collective-permute-start.5) | collective-permute-done | bytes 229408 | tf_op jit(solution)/shard_map/ppermute | solution.py:43
  29.3 2.7 %collective-permute-done.4.refs_0_.refs_19_ = bf16[128,896]{1,0:T(8,128)(2,1)S(1)} collective-permute-done((bf16[128,896]{1,0:T(8,128)(2,1)S(1)}, bf16[128,896]{1,0:T(8,128)(2,1)S(1)}, u32[]{:S(2)}, u32[]{:S(2)}) %collective-permute-start.4) | collective-permute-done | bytes 229408 | tf_op jit(solution)/shard_map/ppermute | solution.py:43
  32.9 5.4 %collective-permute-done.12.refs_0_.refs_14_ = bf16[128,896]{1,0:T(8,128)(2,1)S(1)} collective-permute-done((bf16[128,896]{1,0:T(8,128)(2,1)S(1)}, bf16[128,896]{1,0:T(8,128)(2,1)S(1)}, u32[]{:S(2)}, u32[]{:S(2)}) %collective-permute-start.12) | collective-permute-done | bytes 229408 | tf_op jit(solution)/shard_map/ppermute | solution.py:43
  39.7 0.9 %collective-permute-done.13.refs_1_ = bf16[64,1536]{1,0:T(8,128)(2,1)S(1)} collective-permute-done((bf16[64,1536]{1,0:T(8,128)(2,1)S(1)}, bf16[64,1536]{1,0:T(8,128)(2,1)S(1)}, u32[]{:S(2)}, u32[]{:S(2)}) %collective-permute-start.13) | collective-permute-done | bytes 196640 | tf_op jit(solution)/shard_map/ppermute | solution.py:43
  41.0 1.1 %collective-permute-start.20 = (bf16[64,3072]{1,0:T(8,128)(2,1)S(1)}, bf16[64,3072]{1,0:T(8,128)(2,1)S(1)}, u32[]{:S(2)}, u32[]{:S(2)}) collective-permute-start(bf16[64,3072]{1,0:T(8,128)(2,1)S(1)} %add_cores.3.refs_2_.refs_0_), channel_id=1, source_target_pairs={{0,2},{2,0},{1,3},{3,1},{4,6},{6,4},{5,7},{7,5},{8,10},{10,8},{9,1... | collective-permute-start | bytes 1179656 | tf_op jit(solution)/shard_map/ppermute | solution.py:43
  45.6 1.8 %collective-permute-start.23 = (bf16[64,3072]{1,0:T(8,128)(2,1)S(1)}, bf16[64,3072]{1,0:T(8,128)(2,1)S(1)}, u32[]{:S(2)}, u32[]{:S(2)}) collective-permute-start(bf16[64,3072]{1,0:T(8,128)(2,1)S(1)} %get-tuple-element.63.refs_6_.refs_0_), channel_id=1, source_target_pairs={{0,2},{2,0},{1,3},{3,1},{4,6},{6,4},{5,7},{7,5},{8,10},{10,8},{9,1... | collective-permute-start | bytes 1179656 | tf_op jit(solution)/shard_map/ppermute | solution.py:43
  47.4 1.0 %down_rows.2.refs_2_ = bf16[128,896]{1,0:T(8,128)(2,1)S(1)} custom-call(bf16[64,1536]{1,0:T(8,128)(2,1)S(1)} %get-tuple-element.56.refs_2_.refs_0_.refs_5_, bf16[64,1536]{1,0:T(8,128)(2,1)S(1)} %get-tuple-element.62.refs_1_.refs_6_, bf16[64,1536]{1,0:T(8,128)(2,1)S(1)} %collective-permute-done.18.refs_2_.refs_7_, ...), custom_call_target="tpu_custom_call" | custom-call | flops 1024 | bytes 1024 | tf_op jit(solution)/shard_map/down_rows/pallas_call | solution.py:72
  49.0 4.0 %collective-permute-done.20.refs_1_ = bf16[64,3072]{1,0:T(8,128)(2,1)S(1)} collective-permute-done((bf16[64,3072]{1,0:T(8,128)(2,1)S(1)}, bf16[64,3072]{1,0:T(8,128)(2,1)S(1)}, u32[]{:S(2)}, u32[]{:S(2)}) %collective-permute-start.20) | collective-permute-done | bytes 393248 | tf_op jit(solution)/shard_map/ppermute | solution.py:43
  54.0 0.9 %collective-permute-done.21.refs_2_.refs_12_ = bf16[64,1536]{1,0:T(8,128)(2,1)S(1)} collective-permute-done((bf16[64,1536]{1,0:T(8,128)(2,1)S(1)}, bf16[64,1536]{1,0:T(8,128)(2,1)S(1)}, u32[]{:S(2)}, u32[]{:S(2)}) %collective-permute-start.21) | collective-permute-done | bytes 196640 | tf_op jit(solution)/shard_map/ppermute | solution.py:43
  55.2 1.0 %down_rows.3.refs_7_ = bf16[128,896]{1,0:T(8,128)(2,1)S(1)} custom-call(bf16[64,1536]{1,0:T(8,128)(2,1)S(1)} %get-tuple-element.64.refs_0_.refs_6_.refs_10_, bf16[64,1536]{1,0:T(8,128)(2,1)S(1)} %get-tuple-element.65.refs_1_.refs_11_, bf16[64,1536]{1,0:T(8,128)(2,1)S(1)} %collective-permute-done.21.refs_2_.refs_12_, ...), custom_call_target="tpu_custom_call" | custom-call | flops 1024 | bytes 1024 | tf_op jit(solution)/shard_map/down_rows/pallas_call | solution.py:72
  56.5 0.9 %down_own_add.1.refs_2_.refs_5_ = f32[128,896]{1,0:T(8,128)S(1)} custom-call(bf16[32,1536]{1,0:T(8,128)(2,1)S(1)} %get-tuple-element.51.refs_3_.refs_0_, bf16[32,1536]{1,0:T(8,128)(2,1)S(1)} %get-tuple-element.52.refs_4_.refs_1_, bf16[32,1536]{1,0:T(8,128)(2,1)S(1)} %collective-permute-done.9.refs_5_.refs_2_, ...), custom_call_target="tpu_custom_call" | custom-call | flops 1024 | bytes 1024 | tf_op jit(solution)/shard_map/down_own_add/pallas_call | solution.py:72
  57.4 3.3 %collective-permute-done.23.refs_1_ = bf16[64,3072]{1,0:T(8,128)(2,1)S(1)} collective-permute-done((bf16[64,3072]{1,0:T(8,128)(2,1)S(1)}, bf16[64,3072]{1,0:T(8,128)(2,1)S(1)}, u32[]{:S(2)}, u32[]{:S(2)}) %collective-permute-start.23) | collective-permute-done | bytes 393248 | tf_op jit(solution)/shard_map/ppermute | solution.py:43
  61.7 1.1 %collective-permute-start.17 = (bf16[32,3072]{1,0:T(8,128)(2,1)S(1)}, bf16[32,3072]{1,0:T(8,128)(2,1)S(1)}, u32[]{:S(2)}, u32[]{:S(2)}) collective-permute-start(bf16[32,3072]{1,0:T(8,128)(2,1)S(1)} %get-tuple-element.61.refs_0_), channel_id=1, source_target_pairs={{0,2},{2,0},{1,3},{3,1},{4,6},{6,4},{5,7},{7,5},{8,10},{10,8},{9,1... | collective-permute-start | bytes 589832 | tf_op jit(solution)/shard_map/ppermute | solution.py:43
  62.7 1.2 %collective-permute-done.27.refs_6_ = bf16[128,896]{1,0:T(8,128)(2,1)S(1)} collective-permute-done((bf16[128,896]{1,0:T(8,128)(2,1)S(1)}, bf16[128,896]{1,0:T(8,128)(2,1)S(1)}, u32[]{:S(2)}, u32[]{:S(2)}) %collective-permute-start.27) | collective-permute-done | bytes 229408 | tf_op jit(solution)/shard_map/ppermute | solution.py:43
  64.0 1.1 %down_rows_add.1.refs_20_ = bf16[128,896]{1,0:T(8,128)(2,1)S(1)} custom-call(bf16[64,1536]{1,0:T(8,128)(2,1)S(1)} %get-tuple-element.66.refs_0_.refs_7_.refs_15_, bf16[64,1536]{1,0:T(8,128)(2,1)S(1)} %get-tuple-element.67.refs_1_.refs_16_, bf16[64,1536]{1,0:T(8,128)(2,1)S(1)} %collective-permute-done.25.refs_2_.refs_17_, ...), custom_call_target="tpu_custom_call" | custom-call | flops 1024 | bytes 1024 | tf_op jit(solution)/shard_map/down_rows_add/pallas_call | solution.py:72
  65.1 1.4 %collective-permute-start.30 = (bf16[128,896]{1,0:T(8,128)(2,1)S(1)}, bf16[128,896]{1,0:T(8,128)(2,1)S(1)}, u32[]{:S(2)}, u32[]{:S(2)}) collective-permute-start(bf16[128,896]{1,0:T(8,128)(2,1)S(1)} %down_rows_add.1.refs_20_), channel_id=1, source_target_pairs={{0,8},{4,12},{8,0},{12,4},{1,9},{5,13},{9,1},{13,5},{2,10},{6,14},... | collective-permute-start | bytes 688136 | tf_op jit(solution)/shard_map/ppermute | solution.py:43
  67.1 1.5 %collective-permute-done.17.refs_1_ = bf16[32,3072]{1,0:T(8,128)(2,1)S(1)} collective-permute-done((bf16[32,3072]{1,0:T(8,128)(2,1)S(1)}, bf16[32,3072]{1,0:T(8,128)(2,1)S(1)}, u32[]{:S(2)}, u32[]{:S(2)}) %collective-permute-start.17) | collective-permute-done | bytes 196640 | tf_op jit(solution)/shard_map/ppermute | solution.py:43
  70.3 7.5 %collective-permute-done.30.refs_6_ = bf16[128,896]{1,0:T(8,128)(2,1)S(1)} collective-permute-done((bf16[128,896]{1,0:T(8,128)(2,1)S(1)}, bf16[128,896]{1,0:T(8,128)(2,1)S(1)}, u32[]{:S(2)}, u32[]{:S(2)}) %collective-permute-start.30) | collective-permute-done | bytes 229408 | tf_op jit(solution)/shard_map/ppermute | solution.py:43
  78.4 2.9 %collective-permute-start.32 = (bf16[64,768]{1,0:T(8,128)(2,1)S(1)}, bf16[64,768]{1,0:T(8,128)(2,1)S(1)}, u32[]{:S(2)}, u32[]{:S(2)}) collective-permute-start(bf16[64,768]{1,0:T(8,128)(2,1)S(1)} %get-tuple-element.72.refs_0_), channel_id=1, source_target_pairs={{0,8},{4,12},{8,0},{12,4},{1,9},{5,13},{9,1},{13,5},{2,10},{6,14},... | collective-permute-start | bytes 294920 | tf_op jit(solution)/shard_map/ppermute | solution.py:48
  82.2 1.3 %first_gradient_end.1 = f32[64,3072]{1,0:T(8,128)} custom-call(bf16[32,1536]{1,0:T(8,128)(2,1)S(1)} %get-tuple-element.68.refs_0_, bf16[32,1536]{1,0:T(8,128)(2,1)S(1)} %get-tuple-element.69.refs_1_, bf16[32,1536]{1,0:T(8,128)(2,1)S(1)} %collective-permute-done.28.refs_2_, bf16[32,1536]{1,0:T(8,128)(2,1)S(1)} %collective-permute-done.29.refs_3_, ...), custom_call_target="tpu_custom_call" | custom-call | flops 1024 | bytes 1024 | tf_op jit(solution)/shard_map/first_gradient_end/pallas_call | solution.py:72
  83.5 1.7 %update_rows.1.refs_4_ = bf16[128,768]{1,0:T(8,128)(2,1)} custom-call(bf16[32,1536]{1,0:T(8,128)(2,1)S(1)} %get-tuple-element.68.refs_0_, bf16[32,1536]{1,0:T(8,128)(2,1)S(1)} %get-tuple-element.69.refs_1_, bf16[32,1536]{1,0:T(8,128)(2,1)S(1)} %collective-permute-done.28.refs_2_, bf16[32,1536]{1,0:T(8,128)(2,1)S(1)} %collective-permute-done.29.refs_3_, ...), custom_call_target="tpu_custom_call" | custom-call | flops 1024 | bytes 1024 | tf_op jit(solution)/shard_map/update_rows/pallas_call | solution.py:72
  85.9 3.3 %collective-permute-done.32.refs_2_ = bf16[64,768]{1,0:T(8,128)(2,1)S(1)} collective-permute-done((bf16[64,768]{1,0:T(8,128)(2,1)S(1)}, bf16[64,768]{1,0:T(8,128)(2,1)S(1)}, u32[]{:S(2)}, u32[]{:S(2)}) %collective-permute-start.32) | collective-permute-done | bytes 98336 | tf_op jit(solution)/shard_map/ppermute | solution.py:48
  89.2 0.9 %copy-done.2 = bf16[128,768]{1,0:T(8,128)(2,1)S(1)} copy-done((bf16[128,768]{1,0:T(8,128)(2,1)S(1)}, bf16[128,768]{1,0:T(8,128)(2,1)}, u32[]{:S(2)}) %copy-start.2) | copy-done | bytes 196632
  (80 shorter events, 21.8 us)
Async XLA Ops:
  7.3 5.6 %collective-permute-start.1 = (f32[128,128]{1,0:T(8,128)S(1)}, f32[128,128]{1,0:T(8,128)S(1)}, u32[]{:S(2)}, u32[]{:S(2)}) collective-permute-start(f32[128,128]{1,0:T(8,128)S(1)} %add_packed.1.refs_1_), channel_id=1, source_target_pairs={{0,2},{2,0},{1,3},{3,1},{4,6},{6,4},{5,7},{7,5},{8,10},{10,8},{9,1... | collective-permute-start | bytes 196616 | tf_op jit(solution)/shard_map/ppermute | solution.py:43
  13.8 1.5 %collective-permute-start.2 = (bf16[64,1536]{1,0:T(8,128)(2,1)S(1)}, bf16[64,1536]{1,0:T(8,128)(2,1)S(1)}, u32[]{:S(2)}, u32[]{:S(2)}) collective-permute-start(bf16[64,1536]{1,0:T(8,128)(2,1)S(1)} %get-tuple-element.43), channel_id=1, source_target_pairs={{0,1},{1,0},{2,3},{3,2},{4,5},{5,4},{6,7},{7,6},{8,9},{9,8},{10,11... | collective-permute-start | bytes 589832 | tf_op jit(solution)/shard_map/ppermute | solution.py:43
  13.9 1.7 %collective-permute-start.3 = (bf16[64,1536]{1,0:T(8,128)(2,1)S(1)}, bf16[64,1536]{1,0:T(8,128)(2,1)S(1)}, u32[]{:S(2)}, u32[]{:S(2)}) collective-permute-start(bf16[64,1536]{1,0:T(8,128)(2,1)S(1)} %get-tuple-element.44), channel_id=1, source_target_pairs={{0,1},{1,0},{2,3},{3,2},{4,5},{5,4},{6,7},{7,6},{8,9},{9,8},{10,11... | collective-permute-start | bytes 589832 | tf_op jit(solution)/shard_map/ppermute | solution.py:43
  15.7 11.4 %collective-permute-start.5 = (bf16[128,896]{1,0:T(8,128)(2,1)S(1)}, bf16[128,896]{1,0:T(8,128)(2,1)S(1)}, u32[]{:S(2)}, u32[]{:S(2)}) collective-permute-start(bf16[128,896]{1,0:T(8,128)(2,1)S(1)} %get-tuple-element.46.refs_4_), channel_id=1, source_target_pairs={{0,4},{4,0},{8,12},{12,8},{1,5},{5,1},{9,13},{13,9},{2,6},{6,2},{1... | collective-permute-start | bytes 688136 | tf_op jit(solution)/shard_map/ppermute | solution.py:43
  17.5 11.0 %collective-permute-start.8 = (bf16[32,3072]{1,0:T(8,128)(2,1)S(1)}, bf16[32,3072]{1,0:T(8,128)(2,1)S(1)}, u32[]{:S(2)}, u32[]{:S(2)}) collective-permute-start(bf16[32,3072]{1,0:T(8,128)(2,1)S(1)} %get-tuple-element.47.refs_2_.refs_0_), channel_id=1, source_target_pairs={{0,2},{2,0},{1,3},{3,1},{4,6},{6,4},{5,7},{7,5},{8,10},{10,8},{9,1... | collective-permute-start | bytes 589832 | tf_op jit(solution)/shard_map/ppermute | solution.py:43
  19.0 13.0 %collective-permute-start.4 = (bf16[128,896]{1,0:T(8,128)(2,1)S(1)}, bf16[128,896]{1,0:T(8,128)(2,1)S(1)}, u32[]{:S(2)}, u32[]{:S(2)}) collective-permute-start(bf16[128,896]{1,0:T(8,128)(2,1)S(1)} %get-tuple-element.46.refs_4_), channel_id=1, source_target_pairs={{0,8},{4,12},{8,0},{12,4},{1,9},{5,13},{9,1},{13,5},{2,10},{6,14},... | collective-permute-start | bytes 688136 | tf_op jit(solution)/shard_map/ppermute | solution.py:43
  27.9 4.1 %collective-permute-start.6 = (bf16[64,1536]{1,0:T(8,128)(2,1)S(1)}, bf16[64,1536]{1,0:T(8,128)(2,1)S(1)}, u32[]{:S(2)}, u32[]{:S(2)}) collective-permute-start(bf16[64,1536]{1,0:T(8,128)(2,1)S(1)} %get-tuple-element.49), channel_id=1, source_target_pairs={{0,1},{1,0},{2,3},{3,2},{4,5},{5,4},{6,7},{7,6},{8,9},{9,8},{10,11... | collective-permute-start | bytes 589832 | tf_op jit(solution)/shard_map/ppermute | solution.py:43
  28.0 4.0 %collective-permute-start.7 = (bf16[64,1536]{1,0:T(8,128)(2,1)S(1)}, bf16[64,1536]{1,0:T(8,128)(2,1)S(1)}, u32[]{:S(2)}, u32[]{:S(2)}) collective-permute-start(bf16[64,1536]{1,0:T(8,128)(2,1)S(1)} %get-tuple-element.50), channel_id=1, source_target_pairs={{0,1},{1,0},{2,3},{3,2},{4,5},{5,4},{6,7},{7,6},{8,9},{9,8},{10,11... | collective-permute-start | bytes 589832 | tf_op jit(solution)/shard_map/ppermute | solution.py:43
  28.7 3.3 %collective-permute-start.10 = (bf16[32,1536]{1,0:T(8,128)(2,1)S(1)}, bf16[32,1536]{1,0:T(8,128)(2,1)S(1)}, u32[]{:S(2)}, u32[]{:S(2)}) collective-permute-start(bf16[32,1536]{1,0:T(8,128)(2,1)S(1)} %get-tuple-element.52.refs_4_.refs_1_), channel_id=1, source_target_pairs={{0,1},{1,0},{2,3},{3,2},{4,5},{5,4},{6,7},{7,6},{8,9},{9,8},{10,11... | collective-permute-start | bytes 294920 | tf_op jit(solution)/shard_map/ppermute | solution.py:43
  28.8 3.2 %collective-permute-start.9 = (bf16[32,1536]{1,0:T(8,128)(2,1)S(1)}, bf16[32,1536]{1,0:T(8,128)(2,1)S(1)}, u32[]{:S(2)}, u32[]{:S(2)}) collective-permute-start(bf16[32,1536]{1,0:T(8,128)(2,1)S(1)} %get-tuple-element.51.refs_3_.refs_0_), channel_id=1, source_target_pairs={{0,1},{1,0},{2,3},{3,2},{4,5},{5,4},{6,7},{7,6},{8,9},{9,8},{10,11... | collective-permute-start | bytes 294920 | tf_op jit(solution)/shard_map/ppermute | solution.py:43
  32.0 6.3 %collective-permute-start.12 = (bf16[128,896]{1,0:T(8,128)(2,1)S(1)}, bf16[128,896]{1,0:T(8,128)(2,1)S(1)}, u32[]{:S(2)}, u32[]{:S(2)}) collective-permute-start(bf16[128,896]{1,0:T(8,128)(2,1)S(1)} %collective-permute-done.4.refs_0_.refs_19_), channel_id=1, source_target_pairs={{0,4},{4,0},{8,12},{12,8},{1,5},{5,1},{9,13},{13,9},{2,6},{6,2},{1... | collective-permute-start | bytes 688136 | tf_op jit(solution)/shard_map/ppermute | solution.py:43
  32.1 10.4 %collective-permute-start.11 = (bf16[64,3072]{1,0:T(8,128)(2,1)S(1)}, bf16[64,3072]{1,0:T(8,128)(2,1)S(1)}, u32[]{:S(2)}, u32[]{:S(2)}) collective-permute-start(bf16[64,3072]{1,0:T(8,128)(2,1)S(1)} %add_cores.2.refs_2_.refs_0_), channel_id=1, source_target_pairs={{0,2},{2,0},{1,3},{3,1},{4,6},{6,4},{5,7},{7,5},{8,10},{10,8},{9,1... | collective-permute-start | bytes 1179656 | tf_op jit(solution)/shard_map/ppermute | solution.py:43
  39.1 1.5 %collective-permute-start.13 = (bf16[64,1536]{1,0:T(8,128)(2,1)S(1)}, bf16[64,1536]{1,0:T(8,128)(2,1)S(1)}, u32[]{:S(2)}, u32[]{:S(2)}) collective-permute-start(bf16[64,1536]{1,0:T(8,128)(2,1)S(1)} %get-tuple-element.54), channel_id=1, source_target_pairs={{0,1},{1,0},{2,3},{3,2},{4,5},{5,4},{6,7},{7,6},{8,9},{9,8},{10,11... | collective-permute-start | bytes 589832 | tf_op jit(solution)/shard_map/ppermute | solution.py:43
  39.2 1.7 %collective-permute-start.14 = (bf16[64,1536]{1,0:T(8,128)(2,1)S(1)}, bf16[64,1536]{1,0:T(8,128)(2,1)S(1)}, u32[]{:S(2)}, u32[]{:S(2)}) collective-permute-start(bf16[64,1536]{1,0:T(8,128)(2,1)S(1)} %get-tuple-element.55), channel_id=1, source_target_pairs={{0,1},{1,0},{2,3},{3,2},{4,5},{5,4},{6,7},{7,6},{8,9},{9,8},{10,11... | collective-permute-start | bytes 589832 | tf_op jit(solution)/shard_map/ppermute | solution.py:43
  41.0 12.0 %collective-permute-start.20 = (bf16[64,3072]{1,0:T(8,128)(2,1)S(1)}, bf16[64,3072]{1,0:T(8,128)(2,1)S(1)}, u32[]{:S(2)}, u32[]{:S(2)}) collective-permute-start(bf16[64,3072]{1,0:T(8,128)(2,1)S(1)} %add_cores.3.refs_2_.refs_0_), channel_id=1, source_target_pairs={{0,2},{2,0},{1,3},{3,1},{4,6},{6,4},{5,7},{7,5},{8,10},{10,8},{9,1... | collective-permute-start | bytes 1179656 | tf_op jit(solution)/shard_map/ppermute | solution.py:43
  43.7 1.5 %collective-permute-start.15 = (bf16[64,1536]{1,0:T(8,128)(2,1)S(1)}, bf16[64,1536]{1,0:T(8,128)(2,1)S(1)}, u32[]{:S(2)}, u32[]{:S(2)}) collective-permute-start(bf16[64,1536]{1,0:T(8,128)(2,1)S(1)} %get-tuple-element.58), channel_id=1, source_target_pairs={{0,1},{1,0},{2,3},{3,2},{4,5},{5,4},{6,7},{7,6},{8,9},{9,8},{10,11... | collective-permute-start | bytes 589832 | tf_op jit(solution)/shard_map/ppermute | solution.py:43
  43.7 1.7 %collective-permute-start.16 = (bf16[64,1536]{1,0:T(8,128)(2,1)S(1)}, bf16[64,1536]{1,0:T(8,128)(2,1)S(1)}, u32[]{:S(2)}, u32[]{:S(2)}) collective-permute-start(bf16[64,1536]{1,0:T(8,128)(2,1)S(1)} %get-tuple-element.59), channel_id=1, source_target_pairs={{0,1},{1,0},{2,3},{3,2},{4,5},{5,4},{6,7},{7,6},{8,9},{9,8},{10,11... | collective-permute-start | bytes 589832 | tf_op jit(solution)/shard_map/ppermute | solution.py:43
  44.2 3.1 %collective-permute-start.18 = (bf16[64,1536]{1,0:T(8,128)(2,1)S(1)}, bf16[64,1536]{1,0:T(8,128)(2,1)S(1)}, u32[]{:S(2)}, u32[]{:S(2)}) collective-permute-start(bf16[64,1536]{1,0:T(8,128)(2,1)S(1)} %get-tuple-element.56.refs_2_.refs_0_.refs_5_), channel_id=1, source_target_pairs={{0,1},{1,0},{2,3},{3,2},{4,5},{5,4},{6,7},{7,6},{8,9},{9,8},{10,11... | collective-permute-start | bytes 589832 | tf_op jit(solution)/shard_map/ppermute | solution.py:43
  44.3 3.0 %collective-permute-start.19 = (bf16[64,1536]{1,0:T(8,128)(2,1)S(1)}, bf16[64,1536]{1,0:T(8,128)(2,1)S(1)}, u32[]{:S(2)}, u32[]{:S(2)}) collective-permute-start(bf16[64,1536]{1,0:T(8,128)(2,1)S(1)} %get-tuple-element.62.refs_1_.refs_6_), channel_id=1, source_target_pairs={{0,1},{1,0},{2,3},{3,2},{4,5},{5,4},{6,7},{7,6},{8,9},{9,8},{10,11... | collective-permute-start | bytes 589832 | tf_op jit(solution)/shard_map/ppermute | solution.py:43
  45.6 15.2 %collective-permute-start.23 = (bf16[64,3072]{1,0:T(8,128)(2,1)S(1)}, bf16[64,3072]{1,0:T(8,128)(2,1)S(1)}, u32[]{:S(2)}, u32[]{:S(2)}) collective-permute-start(bf16[64,3072]{1,0:T(8,128)(2,1)S(1)} %get-tuple-element.63.refs_6_.refs_0_), channel_id=1, source_target_pairs={{0,2},{2,0},{1,3},{3,1},{4,6},{6,4},{5,7},{7,5},{8,10},{10,8},{9,1... | collective-permute-start | bytes 1179656 | tf_op jit(solution)/shard_map/ppermute | solution.py:43
  48.4 8.1 %collective-permute-start.24 = (bf16[128,896]{1,0:T(8,128)(2,1)S(1)}, bf16[128,896]{1,0:T(8,128)(2,1)S(1)}, u32[]{:S(2)}, u32[]{:S(2)}) collective-permute-start(bf16[128,896]{1,0:T(8,128)(2,1)S(1)} %down_rows.2.refs_2_), channel_id=1, source_target_pairs={{0,4},{4,0},{8,12},{12,8},{1,5},{5,1},{9,13},{13,9},{2,6},{6,2},{1... | collective-permute-start | bytes 688136 | tf_op jit(solution)/shard_map/ppermute | solution.py:43
  53.4 1.5 %collective-permute-start.21 = (bf16[64,1536]{1,0:T(8,128)(2,1)S(1)}, bf16[64,1536]{1,0:T(8,128)(2,1)S(1)}, u32[]{:S(2)}, u32[]{:S(2)}) collective-permute-start(bf16[64,1536]{1,0:T(8,128)(2,1)S(1)} %get-tuple-element.64.refs_0_.refs_6_.refs_10_), channel_id=1, source_target_pairs={{0,1},{1,0},{2,3},{3,2},{4,5},{5,4},{6,7},{7,6},{8,9},{9,8},{10,11... | collective-permute-start | bytes 589832 | tf_op jit(solution)/shard_map/ppermute | solution.py:43
  53.5 1.7 %collective-permute-start.22 = (bf16[64,1536]{1,0:T(8,128)(2,1)S(1)}, bf16[64,1536]{1,0:T(8,128)(2,1)S(1)}, u32[]{:S(2)}, u32[]{:S(2)}) collective-permute-start(bf16[64,1536]{1,0:T(8,128)(2,1)S(1)} %get-tuple-element.65.refs_1_.refs_11_), channel_id=1, source_target_pairs={{0,1},{1,0},{2,3},{3,2},{4,5},{5,4},{6,7},{7,6},{8,9},{9,8},{10,11... | collective-permute-start | bytes 589832 | tf_op jit(solution)/shard_map/ppermute | solution.py:43
  56.2 7.8 %collective-permute-start.27 = (bf16[128,896]{1,0:T(8,128)(2,1)S(1)}, bf16[128,896]{1,0:T(8,128)(2,1)S(1)}, u32[]{:S(2)}, u32[]{:S(2)}) collective-permute-start(bf16[128,896]{1,0:T(8,128)(2,1)S(1)} %down_rows.3.refs_7_), channel_id=1, source_target_pairs={{0,4},{4,0},{8,12},{12,8},{1,5},{5,1},{9,13},{13,9},{2,6},{6,2},{1... | collective-permute-start | bytes 688136 | tf_op jit(solution)/shard_map/ppermute | solution.py:43
  61.1 2.9 %collective-permute-start.25 = (bf16[64,1536]{1,0:T(8,128)(2,1)S(1)}, bf16[64,1536]{1,0:T(8,128)(2,1)S(1)}, u32[]{:S(2)}, u32[]{:S(2)}) collective-permute-start(bf16[64,1536]{1,0:T(8,128)(2,1)S(1)} %get-tuple-element.66.refs_0_.refs_7_.refs_15_), channel_id=1, source_target_pairs={{0,1},{1,0},{2,3},{3,2},{4,5},{5,4},{6,7},{7,6},{8,9},{9,8},{10,11... | collective-permute-start | bytes 589832 | tf_op jit(solution)/shard_map/ppermute | solution.py:43
  61.2 2.8 %collective-permute-start.26 = (bf16[64,1536]{1,0:T(8,128)(2,1)S(1)}, bf16[64,1536]{1,0:T(8,128)(2,1)S(1)}, u32[]{:S(2)}, u32[]{:S(2)}) collective-permute-start(bf16[64,1536]{1,0:T(8,128)(2,1)S(1)} %get-tuple-element.67.refs_1_.refs_16_), channel_id=1, source_target_pairs={{0,1},{1,0},{2,3},{3,2},{4,5},{5,4},{6,7},{7,6},{8,9},{9,8},{10,11... | collective-permute-start | bytes 589832 | tf_op jit(solution)/shard_map/ppermute | solution.py:43
  61.7 6.9 %collective-permute-start.17 = (bf16[32,3072]{1,0:T(8,128)(2,1)S(1)}, bf16[32,3072]{1,0:T(8,128)(2,1)S(1)}, u32[]{:S(2)}, u32[]{:S(2)}) collective-permute-start(bf16[32,3072]{1,0:T(8,128)(2,1)S(1)} %get-tuple-element.61.refs_0_), channel_id=1, source_target_pairs={{0,2},{2,0},{1,3},{3,1},{4,6},{6,4},{5,7},{7,5},{8,10},{10,8},{9,1... | collective-permute-start | bytes 589832 | tf_op jit(solution)/shard_map/ppermute | solution.py:43
  65.1 12.6 %collective-permute-start.30 = (bf16[128,896]{1,0:T(8,128)(2,1)S(1)}, bf16[128,896]{1,0:T(8,128)(2,1)S(1)}, u32[]{:S(2)}, u32[]{:S(2)}) collective-permute-start(bf16[128,896]{1,0:T(8,128)(2,1)S(1)} %down_rows_add.1.refs_20_), channel_id=1, source_target_pairs={{0,8},{4,12},{8,0},{12,4},{1,9},{5,13},{9,1},{13,5},{2,10},{6,14},... | collective-permute-start | bytes 688136 | tf_op jit(solution)/shard_map/ppermute | solution.py:43
  68.8 1.4 %collective-permute-start.29 = (bf16[32,1536]{1,0:T(8,128)(2,1)S(1)}, bf16[32,1536]{1,0:T(8,128)(2,1)S(1)}, u32[]{:S(2)}, u32[]{:S(2)}) collective-permute-start(bf16[32,1536]{1,0:T(8,128)(2,1)S(1)} %get-tuple-element.69.refs_1_), channel_id=1, source_target_pairs={{0,1},{1,0},{2,3},{3,2},{4,5},{5,4},{6,7},{7,6},{8,9},{9,8},{10,11... | collective-permute-start | bytes 294920 | tf_op jit(solution)/shard_map/ppermute | solution.py:43
  78.3 7.6 %collective-permute-start.31 = (bf16[64,768]{1,0:T(8,128)(2,1)S(1)}, bf16[64,768]{1,0:T(8,128)(2,1)S(1)}, u32[]{:S(2)}, u32[]{:S(2)}) collective-permute-start(bf16[64,768]{1,0:T(8,128)(2,1)S(1)} %get-tuple-element.72.refs_0_), channel_id=1, source_target_pairs={{0,4},{4,8},{8,12},{12,0},{1,5},{5,9},{9,13},{13,1},{2,6},{6,10},{... | collective-permute-start | bytes 294920 | tf_op jit(solution)/shard_map/ppermute | solution.py:48
  78.4 10.8 %collective-permute-start.32 = (bf16[64,768]{1,0:T(8,128)(2,1)S(1)}, bf16[64,768]{1,0:T(8,128)(2,1)S(1)}, u32[]{:S(2)}, u32[]{:S(2)}) collective-permute-start(bf16[64,768]{1,0:T(8,128)(2,1)S(1)} %get-tuple-element.72.refs_0_), channel_id=1, source_target_pairs={{0,8},{4,12},{8,0},{12,4},{1,9},{5,13},{9,1},{13,5},{2,10},{6,14},... | collective-permute-start | bytes 294920 | tf_op jit(solution)/shard_map/ppermute | solution.py:48
  81.3 7.9 %collective-permute-start.33 = (bf16[64,768]{1,0:T(8,128)(2,1)S(1)}, bf16[64,768]{1,0:T(8,128)(2,1)S(1)}, u32[]{:S(2)}, u32[]{:S(2)}) collective-permute-start(bf16[64,768]{1,0:T(8,128)(2,1)S(1)} %get-tuple-element.72.refs_0_), channel_id=1, source_target_pairs={{0,12},{4,0},{8,4},{12,8},{1,13},{5,1},{9,5},{13,9},{2,14},{6,2},{... | collective-permute-start | bytes 294920 | tf_op jit(solution)/shard_map/ppermute | solution.py:48
  (11 other events, 33.4 us)

commit v3 on v1

v3 whole, which is shorter than its diff:
```python
import functools

import jax
import jax.numpy as jnp
from jax import lax
from jax.experimental import pallas as pl
from jax.experimental.pallas import tpu as pltpu
from jax.sharding import PartitionSpec as P

adapter_scale = 0.5
norm_eps = 1e-06
gelu_coef = 0.7978845608028654
f32 = jnp.float32
bf16 = jnp.bfloat16
LANES = 128
ORDER = [2, 3, 1]
OWN_GRANT = (64 * 1024 - 11400) * 1024


def gelu_value(pre_value):
    inner_arg = gelu_coef * (pre_value + 0.044715 * pre_value * pre_value * pre_value)
    return 0.5 * pre_value * (1.0 + jnp.tanh(inner_arg))


def dot(left, right):
    return jnp.dot(left, right, preferred_element_type=f32)


def dot_transposed(left, right):
    return lax.dot_general(left, right, (((1,), (1,)), ((), ())), preferred_element_type=f32)


def dot_rows(left, right):
    return lax.dot_general(left, right, (((0,), (0,)), ((), ())), preferred_element_type=f32)


def split_dot(product, left, right):
    high = left.astype(bf16)
    low = (left - high.astype(f32)).astype(bf16)
    return product(high, right) + product(low, right)


def swap(value, axis, distance):
    size = lax.axis_size(axis)
    return lax.ppermute(value, axis, [(i, i ^ distance) for i in range(size)])


def exchange(value, axis, kind):
    distance, size = 1, lax.axis_size(axis)
    while True:
        other = swap(value, axis, distance)
        distance *= 2
        if distance >= size:
            return value, other
        value = (value.astype(f32) + other.astype(f32)).astype(kind)


def call(body, outs, arrays, after=(), scratch=(), remote=(), scalars=(), grant=24 * 2**20):
    vmem = pl.BlockSpec(memory_space=pltpu.VMEM)
    specs = [pl.BlockSpec(memory_space=pltpu.SMEM)] * len(scalars)
    specs += [pl.BlockSpec(memory_space=pltpu.HBM)] * len(remote) + [vmem] * len(arrays)
    count = len(specs)
    specs += [pl.BlockSpec(memory_space=pl.ANY)] * len(after)
    total = len(specs)

    def kernel(*refs):
        body(*refs[:count], *refs[total:])

    return pl.pallas_call(
        kernel,
        out_shape=[jax.ShapeDtypeStruct(shape, kind) for shape, kind in outs],
        in_specs=specs,
        out_specs=[vmem] * len(outs),
        scratch_shapes=list(scratch),
        compiler_params=pltpu.CompilerParams(vmem_limit_bytes=grant),
        cost_estimate=pl.CostEstimate(flops=1024, bytes_accessed=1024, transcendentals=0),
        name=body.__name__,
    )(*scalars, *remote, *arrays, *after)


def cut(width):
    return width // 2 // LANES * LANES


def columns(width, step=512):
    return [slice(at, min(at + step, width)) for at in range(0, width, step)]


def rows_at(place, count):
    return pl.ds(pl.multiple_of(place * count, count), count)


def own_core():
    return lax.axis_index("sub")


def feature_block():
    return lax.axis_index("narrow") * lax.axis_size("sub") + lax.axis_index("sub")


def centred(x, mod):
    values = x[...].astype(f32)
    total = jnp.sum(values, axis=1, keepdims=True)
    rows = (values - total / x.shape[1]) * (1.0 + mod[1:2, :])
    return rows.astype(bf16), total, values


def split_rows(value):
    high = value.astype(bf16)
    return [high, (value - high.astype(f32)).astype(bf16)]


def order_rows(value):
    middle = value.shape[0] // 2
    low, high = value[:middle], value[middle:]
    own = own_core()
    return [jnp.where(own == 0, low, high), jnp.where(own == 0, high, low)]


def own_rows(
    step, x_hbm, cot_hbm, mod_hbm, second_hbm, weight_hbm,
    kept_left, kept_right, left, right, packed, factor, mod, weight, x, cot, table, sems,
):
    rows, features = x.shape
    rank = factor.shape[0]
    hidden = weight.shape[1]
    tiles = hidden // LANES
    block = feature_block()
    blocks = lax.axis_size("narrow") * lax.axis_size("sub")
    at = pl.ds(pl.multiple_of(block * features, LANES), features)
    copies = [
        pltpu.make_async_copy(mod_hbm, table, sems.at[0]),
        pltpu.make_async_copy(x_hbm, x, sems.at[1]),
        pltpu.make_async_copy(cot_hbm, cot, sems.at[2]),
        pltpu.make_async_copy(second_hbm.at[:, at], factor, sems.at[3]),
    ]
    pieces = up_columns(hidden)
    loads = [
        pltpu.make_async_copy(weight_hbm.at[:, piece], weight.at[:, piece], sems.at[4 + place])
        for place, piece in enumerate(pieces)
    ]
    for copy in copies + loads:
        copy.start()
    copies[0].wait()
    for kind in range(3):
        mod[kind : kind + 1, :] = table[kind, pl.ds(step[0], 1), :]
    copies[1].wait()
    normed, total, values = centred(x, mod)
    squares = jnp.sum(values * values, axis=1, keepdims=True)
    extra = split_rows(1.0 + mod[1:2, :]) + split_rows(mod[0:1, :])
    extra.append(jnp.zeros((16 - len(extra), features), bf16))
    left_rows = jnp.concatenate(order_rows(normed) + extra, axis=0)
    for copy in copies[2:]:
        copy.wait()
    back_rows = (mod[2:3, :] * cot[...].astype(f32)).astype(bf16)
    padded = jnp.concatenate([factor[...], jnp.zeros((LANES - rank, features), bf16)], axis=0)
    low = dot_transposed(back_rows, padded)
    lane = lax.broadcasted_iota(jnp.int32, (rows, LANES), 1)
    low = jnp.where(lane == rank + block, total, low)
    packed[:rows] = jnp.where(lane == rank + blocks, squares, low)
    packed[rows:] = jnp.zeros((packed.shape[0] - rows, LANES), f32)
    middle = rows // 2
    for piece, load in zip(pieces, loads):
        load.wait()
        product = dot(left_rows, weight[:, piece])
        store_product(piece, product[:rows].astype(bf16), middle, kept_left, kept_right, left, right)
        scale_row = product[rows : rows + 1] + product[rows + 1 : rows + 2]
        shift_row = product[rows + 2 : rows + 3] + product[rows + 3 : rows + 4]
        for tile in range((piece.stop - piece.start) // LANES):
            lanes = slice(tile * LANES, (tile + 1) * LANES)
            place = piece.start // LANES + tile
            packed[pl.ds(rows + block * tiles + place, 1), :] = scale_row[:, lanes]
            packed[rows + blocks * tiles + place : rows + blocks * tiles + place + 1, :] = shift_row[:, lanes]


def add_packed(left, right, out):
    out[...] = left[...] + right[...]


def unpack(left, right, stats, table):
    rows, tiles = stats.shape[0], table.shape[1] // LANES
    stats[...] = left[:rows] + right[:rows]
    count = (left.shape[0] - rows) // tiles
    for kind in range(count):
        for tile in range(tiles):
            at = slice(rows + kind * tiles + tile, rows + kind * tiles + tile + 1)
            table[kind : kind + 1, tile * LANES : (tile + 1) * LANES] = left[at] + right[at]


def store_product(at, product, count, kept_left, kept_right, left, right):
    if at.start < left.shape[1]:
        kept_left[:, at] = product[:count]
        left[:, at] = product[count:]
    else:
        to = slice(at.start - left.shape[1], at.stop - left.shape[1])
        kept_right[:, to] = product[:count]
        right[:, to] = product[count:]


def up_columns(width):
    middle = cut(width)
    return columns(middle) + [slice(at.start + middle, at.stop + middle) for at in columns(width - middle)]


def up_rows(x, mod, weight, kept_left, kept_right, left, right):
    count = x.shape[0]
    normed, _, _ = centred(x, mod)
    rows = jnp.concatenate(order_rows(normed), axis=0)
    for at in up_columns(weight.shape[1]):
        product = dot(rows, weight[:, at]).astype(bf16)
        store_product(at, product, count // 2, kept_left, kept_right, left, right)


def add_cores(kept_left, kept_right, left, right, out):
    middle = left.shape[1]
    out[:, :middle] = (kept_left[...].astype(f32) + left[...].astype(f32)).astype(bf16)
    out[:, middle:] = (kept_right[...].astype(f32) + right[...].astype(f32)).astype(bf16)


def gelu_rows(rank, features, mine, other, stats, table, left, right):
    width, count = left.shape[1], left.shape[0]
    blocks = lax.axis_size("narrow") * lax.axis_size("sub")
    rows = stats[pl.ds(pl.multiple_of(own_core() * count, 16), count), :]
    sums = [rows[:, rank + block : rank + block + 1] for block in range(blocks)]
    row_mean = sum(sums[1:], sums[0]) / (blocks * features)
    row_msq = rows[:, rank + blocks : rank + blocks + 1] / (blocks * features)
    inv_std = lax.rsqrt(row_msq - row_mean * row_mean + norm_eps)
    offsets = [value / features - row_mean for value in sums]
    for out, start in ((left, 0), (right, width)):
        for at in columns(out.shape[1]):
            source = slice(at.start + start, at.stop + start)
            value = mine[:, source].astype(f32) + other[:, source].astype(f32)
            for block in range(blocks):
                value = value + offsets[block] * table[block : block + 1, source]
            pre_act = inv_std * value + table[blocks : blocks + 1, source]
            out[:, at] = gelu_value(pre_act).astype(bf16)


def two_halves(own, other):
    return [jnp.concatenate([a[...], b[...]], axis=0) for a, b in zip(own, other)]


def low_product(activated, first):
    left, right = activated
    hidden = left.shape[1] + right.shape[1]
    base = lax.axis_index("loop") * hidden
    factor_left = first[:, pl.ds(pl.multiple_of(base, LANES), left.shape[1])]
    factor_right = first[:, pl.ds(pl.multiple_of(base + left.shape[1], LANES), right.shape[1])]
    return dot_transposed(left, factor_left) + dot_transposed(right, factor_right)


def down_product(activated, weight, at):
    left, right = activated
    middle = left.shape[1]
    return dot(left, weight[:middle, at]) + dot(right, weight[middle:, at])


def store_rows(out, at, value):
    middle = value.shape[0] // 2
    own = own_core()
    out[rows_at(own, middle), at] = value[:middle].astype(out.dtype)
    out[rows_at(1 - own, middle), at] = value[middle:].astype(out.dtype)


def down_rows(left, right, other_left, other_right, weight, first, out):
    activated = two_halves((left, right), (other_left, other_right))
    features = weight.shape[1]
    low = low_product(activated, first)
    low = jnp.concatenate([low, jnp.zeros((low.shape[0], LANES - low.shape[1]), f32)], axis=1)
    store_rows(out, slice(features, features + LANES), low)
    for at in columns(features, 256):
        store_rows(out, at, down_product(activated, weight, at))


def stat_rows(stats, count):
    own = own_core()
    return [
        stats[pl.ds(pl.multiple_of(place * count, 16), count), :].astype(bf16)
        for place in (own, 1 - own)
    ]


def first_gradient_rows(*refs):
    blocks, out = refs[:-1], refs[-1]
    rank = out.shape[0]
    middle = blocks[0].shape[1]
    factors = []
    for at in range(0, len(blocks), 5):
        factors += stat_rows(blocks[at + 4], blocks[at].shape[0])
    factors = jnp.concatenate(factors, axis=0)
    for half, base in ((0, 0), (1, middle)):
        for at in columns(blocks[half].shape[1]):
            right = []
            for place in range(0, len(blocks), 5):
                right += [blocks[place + half][:, at], blocks[place + 2 + half][:, at]]
            product = dot_rows(factors, jnp.concatenate(right, axis=0))
            out[:, slice(at.start + base, at.stop + base)] = adapter_scale * product[:rank]


def second_gradient_part(left, right, other_left, other_right, first, cot, mod, *refs):
    received, (out, low_total, low) = refs[:-3], refs[-3:]
    activated = two_halves((left, right), (other_left, other_right))
    rank = first.shape[0]
    features = cot.shape[1]
    lanes = slice(features, features + rank)
    back_rows = (mod[2:3, :] * cot[...].astype(f32)).astype(bf16)
    store_rows(low, slice(0, rank), low_product(activated, first))
    sums = low[...]
    for value in received:
        sums = sums + value[:, lanes].astype(f32)
    low_total[...] = sums
    out[...] = (adapter_scale * split_dot(dot_rows, sums, back_rows)).astype(bf16)


def update_rows(left, right, other_left, other_right, weight, low_total, factor, mod, *refs):
    received, (out, total) = refs[:-2], refs[-2:]
    activated = two_halves((left, right), (other_left, other_right))
    features = factor.shape[1]
    for at in columns(features, 256):
        store_rows(total, at, down_product(activated, weight, at))
    base = total[...] + adapter_scale * split_dot(dot, low_total[...], factor[...])
    for value in received:
        base = base + value[:, :features].astype(f32)
    out[...] = (mod[2:3, :] * base).astype(bf16)


def add_four(own, one, two, three, out):
    out[...] = (own[...].astype(f32) + one[...].astype(f32)) + (
        two[...].astype(f32) + three[...].astype(f32)
    )


def per_device(
    block_input_rows,
    frozen_up_weight,
    frozen_down_weight,
    down_first_factor,
    down_second_factor,
    modulation,
    timestep_index,
    cotangent,
):
    loop_size = lax.axis_size("loop")
    wide_size = lax.axis_size("narrow") * lax.axis_size("sub")
    rows, features = block_input_rows.shape
    hidden = frozen_up_weight.shape[1]
    rank = down_first_factor.shape[1]
    blocks = wide_size
    middle = rows // 2
    wide = features + LANES
    first = down_first_factor.T
    part = cut(hidden)
    tiles = hidden // LANES
    dma = pltpu.SemaphoreType.DMA

    def swap_halves(left, right):
        return [swap(left, "sub", 1), swap(right, "sub", 1)]

    def halves(count):
        return [((count, part), bf16), ((count, hidden - part), bf16)]

    def named(body, *values):
        bound = functools.partial(body, *values)
        bound.__name__ = body.__name__
        return bound

    order = ORDER if loop_size == 4 else list(range(1, loop_size))
    raw = {k: swap(block_input_rows, "loop", k) for k in range(1, min(loop_size, 3))}
    for k in range(3, loop_size):
        raw[k] = swap(raw[2] if k == 3 else block_input_rows, "loop", 1 if k == 3 else k)

    length = -(-(rows + (blocks + 1) * tiles) // 8) * 8
    *kept, left, right, packed, second, mod = call(
        own_rows,
        [
            *halves(middle),
            *halves(middle),
            ((length, LANES), f32),
            ((rank, features), bf16),
            ((8, features), f32),
        ],
        [],
        scratch=[
            pltpu.VMEM((features, hidden), bf16),
            pltpu.VMEM((rows, features), bf16),
            pltpu.VMEM((rows, features), bf16),
            pltpu.VMEM((3, modulation.shape[0], features), f32),
            dma((4 + len(up_columns(hidden)),)),
        ],
        scalars=[timestep_index],
        remote=[
            block_input_rows,
            cotangent,
            jnp.transpose(modulation, (1, 0, 2)),
            down_second_factor,
            frozen_up_weight,
        ],
        grant=OWN_GRANT,
    )
    (packed,) = call(add_packed, [((length, LANES), f32)], [packed, swap(packed, "sub", 1)])
    own_stats, table = call(
        unpack,
        [((rows, LANES), f32), ((-(-(blocks + 1) // 8) * 8, hidden), f32)],
        list(exchange(packed, "narrow", f32)),
    )
    stats = [swap(own_stats, "loop", k) for k in order] + [own_stats]
    pairs = []
    activated = []
    received = []

    def multiply(place, after):
        *kept, left, right = call(
            up_rows,
            [*halves(middle), *halves(middle)],
            [raw[order[place]], mod, frozen_up_weight],
            after,
        )
        return [*kept, *swap_halves(left, right)]

    def add(parts, after):
        (value,) = call(add_cores, [((middle, hidden), bf16)], parts, after)
        pairs.append(exchange(value, "narrow", bf16))
        return [value]

    def activate(after):
        place = len(activated)
        left, right = call(
            named(gelu_rows, rank, features),
            halves(middle),
            [*pairs[place], stats[place], table],
            after,
        )
        activated.append([left, right, *swap_halves(left, right)])
        return [left]

    def down(place, after):
        operands = [*activated[place], frozen_down_weight, first]
        (joined,) = call(down_rows, [((rows, wide), bf16)], operands, after + received[-1:])
        received.append(swap(joined, "loop", order[place]))
        return [joined]

    own_parts = [*kept, *swap_halves(left, right)]
    last = len(order)
    after = [packed]
    for place in range(last):
        if place >= 2:
            after = activate(after) + stats[1:-1]
        parts = multiply(place, after)
        after = parts[:1]
        if place == 0:
            after = after + [own_stats]
        if place >= 2:
            after = down(place - 2, after)
        after = add(parts, after)
    after = add(own_parts, after)
    for place in (last - 2, last - 1):
        after = activate(after)
        after = down(place, after)
    after = activate(after)
    own = activated[last]
    contribution, low_total = call(
        second_gradient_part,
        [((rank, features), bf16), ((rows, rank), f32)],
        [*own, first, cotangent, mod, *received],
        after,
        scratch=[pltpu.VMEM((rows, rank), f32)],
    )
    (block_update,) = call(
        update_rows,
        [((rows, features), bf16)],
        [*own, frozen_down_weight, low_total, second, mod, *received],
        scratch=[pltpu.VMEM((rows, features), f32)],
    )
    gathered = []
    for parts, rows_of in zip(activated, stats):
        gathered += [*parts, rows_of]
    (first_gradient,) = call(first_gradient_rows, [((rank, hidden), f32)], gathered, [low_total])
    if loop_size == 4:
        terms = [swap(contribution, "loop", k) for k in (1, 2, 3)]
        (second_gradient,) = call(
            add_four, [((rank, features), f32)], [contribution, *terms], [block_update]
        )
    else:
        second_gradient = lax.psum(contribution, "loop").astype(f32)
    return (block_update, first_gradient.T, second_gradient)


def solution(mesh):
    in_specs = (
        P(("groups", "loop"), ("narrow", "sub")),
        P(("narrow", "sub"), "loop"),
        P("loop", ("narrow", "sub")),
        P(),
        P(),
        P(None, None, ("narrow", "sub")),
        P("groups"),
        P(("groups", "loop"), ("narrow", "sub")),
    )
    out_specs = (
        P(("groups", "loop"), ("narrow", "sub")),
        P(("groups", "loop"), None),
        P("groups", ("narrow", "sub")),
    )
    return jax.shard_map(
        per_device, mesh=mesh, in_specs=in_specs, out_specs=out_specs, check_vma=False
    )
```

time: 104 us -> 86.6 us (0.83)
  matrix products: 29.9 us -> 0 us
  Pallas kernels: 0 us -> 16.9 us
  waiting for transfers between devices: 26.8 us -> 34.8 us
  other arithmetic: 7.78 us -> 0.01 us
  starting transfers between devices: 34.9 us -> 31.2 us
    dot_general x19 -> x0, matrix products: 29.9 us -> none  [the longest x12 21.2 us: dot(): return jnp.dot(left, right, preferred_element_type=f32)]
    ppermute x14 -> x34, waiting for transfers between devices: 6.52 us -> 34.8 us  [swap(): return lax.ppermute(value, axis, [(i, i ^ distance) for i in range(size)])]
    ppermute x9 -> x0, starting transfers between devices: 24 us -> none  [shift(): lax.ppermute(value, axis, [(i, (i + distance) % size) for i in range(size)])]
    ppermute x14 -> x34, starting transfers between devices: 10.9 us -> 31.2 us  [swap(): return lax.ppermute(value, axis, [(i, i ^ distance) for i in range(size)])]
    ppermute x9 -> x0, waiting for transfers between devices: 20.3 us -> none  [shift(): lax.ppermute(value, axis, [(i, (i + distance) % size) for i in range(size)])]
    pallas_call x0 -> x21, Pallas kernels: none -> 16.9 us  [call(): pl.pallas_call(kernel, out_shape=[jax.ShapeDtypeStruct(shape, kind) for s...]
    convert_element_type x11 -> x0, other arithmetic: 4.92 us -> none  [the longest x4 3.31 us: per_device(): own_half = gelu_value(pre_act).astype(bf16)]
    add x5 -> x0, other arithmetic: 1.61 us -> none  [the longest x1 0.82 us: per_device(): 1.0 + mod_scale]
  transfers between devices with their start and end apart: 23 -> 34, of which waited for: 11 -> 16; matrix products, arithmetic and copies ran while one was open for 32% -> 0% of each run, Pallas kernels for 0% -> 17%
where the time goes in v3:
time: 86.6 us; the launch traced here: 86.4 us
  waiting for transfers between devices  34.8 us (40%)
  starting transfers between devices  31.2 us (36%)
  Pallas kernels  16.9 us (20%)
  local copies, waits for them, and re-layouts  1.84 us (2%)
  between operations  1.57 us (2%)
    ppermute x34, waiting for transfers between devices, swap(): return lax.ppermute(value, axis, [(i, i ^ distance) for i in range(size)])  34.8 us
    ppermute x34, starting transfers between devices, swap(): return lax.ppermute(value, axis, [(i, i ^ distance) for i in range(size)])  31.2 us
    pallas_call x21, Pallas kernels, call(): pl.pallas_call(kernel, out_shape=[jax.ShapeDtypeStruct(shape, kind) for s...  16.9 us
    unnamed x16, local copies, waits for them, and re-layouts  1.84 us
  transfers between devices with their start and end apart: 34, of which 16 were waited for; matrix products, arithmetic and copies ran while one was open for 0% of the time, Pallas kernels for 17%

profile of v3, /device:TPU:0, one launch (start us, length us, event | category | flops | bytes accessed | tf_op | source)
XLA Modules:
  0.0 86.4 jit_solution(12571581345951877004)
XLA Ops:
  0.6 4.1 %collective-permute-start.3 = (bf16[128,768]{1,0:T(8,128)(2,1)}, bf16[128,768]{1,0:T(8,128)(2,1)S(1)}, u32[]{:S(2)}, u32[]{:S(2)}) collective-permute-start(bf16[128,768]{1,0:T(8,128)(2,1)} %refs_1_.1), channel_id=1, source_target_pairs={{0,8},{4,12},{8,0},{12,4},{1,9},{5,13},{9,1},{13,5},{2,10},{6,14},... | collective-permute-start | bytes 589832 | tf_op jit(solution)/shard_map/ppermute | solution.py:45
  5.4 0.9 %copy-done.4 = f32[8,3,768]{2,0,1:T(8,128)S(1)} copy-done((f32[8,3,768]{2,0,1:T(8,128)S(1)}, f32[8,3,768]{2,0,1:T(8,128)}, u32[]{:S(2)}) %copy-start.4) | copy-done | bytes 73752
  6.3 3.3 %own_rows.1 = (bf16[64,1536]{1,0:T(8,128)(2,1)S(1)}, bf16[64,1536]{1,0:T(8,128)(2,1)S(1)}, bf16[64,1536]{1,0:T(8,128)(2,1)S(1)}, bf16[64,1536]{1,0:T(8,128)(2,1)...) custom-call(s32[1]{0:T(128)S(6)} %copy.11.refs_0_, bf16[128,768]{1,0:T(8,128)(2,1)} %refs_1_.1, ...), custom_call_target="tpu_custom_call" | custom-call | flops 1024 | bytes 1024 | tf_op jit(solution)/shard_map/own_rows/pallas_call | solution.py:69
  9.7 1.3 %collective-permute-done.4.refs_1_ = f32[248,128]{1,0:T(8,128)S(1)} collective-permute-done((f32[248,128]{1,0:T(8,128)S(1)}, f32[248,128]{1,0:T(8,128)S(1)}, u32[]{:S(2)}, u32[]{:S(2)}) %collective-permute-start.4) | collective-permute-done | bytes 127008 | tf_op jit(solution)/shard_map/ppermute | solution.py:45
  11.0 3.0 %collective-permute-done.3.refs_0_ = bf16[128,768]{1,0:T(8,128)(2,1)S(1)} collective-permute-done((bf16[128,768]{1,0:T(8,128)(2,1)}, bf16[128,768]{1,0:T(8,128)(2,1)S(1)}, u32[]{:S(2)}, u32[]{:S(2)}) %collective-permute-start.3) | collective-permute-done | bytes 196640 | tf_op jit(solution)/shard_map/ppermute | solution.py:45
  14.1 0.9 up_rows.3
  15.5 1.5 %collective-permute-start.7 = (f32[248,128]{1,0:T(8,128)S(1)}, f32[248,128]{1,0:T(8,128)S(1)}, u32[]{:S(2)}, u32[]{:S(2)}) collective-permute-start(f32[248,128]{1,0:T(8,128)S(1)} %add_packed.1.refs_3_.refs_0_), channel_id=1, source_target_pairs={{0,2},{2,0},{1,3},{3,1},{4,6},{6,4},{5,7},{7,5},{8,10},{10,8},{9,1... | collective-permute-start | bytes 380936 | tf_op jit(solution)/shard_map/ppermute | solution.py:45
  17.8 3.1 %collective-permute-done.7.refs_1_ = f32[248,128]{1,0:T(8,128)S(1)} collective-permute-done((f32[248,128]{1,0:T(8,128)S(1)}, f32[248,128]{1,0:T(8,128)S(1)}, u32[]{:S(2)}, u32[]{:S(2)}) %collective-permute-start.7) | collective-permute-done | bytes 127008 | tf_op jit(solution)/shard_map/ppermute | solution.py:45
  21.1 1.6 %collective-permute-start.8 = (bf16[64,3072]{1,0:T(8,128)(2,1)S(1)}, bf16[64,3072]{1,0:T(8,128)(2,1)S(1)}, u32[]{:S(2)}, u32[]{:S(2)}) collective-permute-start(bf16[64,3072]{1,0:T(8,128)(2,1)S(1)} %add_cores.4.refs_3_.refs_0_), channel_id=1, source_target_pairs={{0,2},{2,0},{1,3},{3,1},{4,6},{6,4},{5,7},{7,5},{8,10},{10,8},{9,1... | collective-permute-start | bytes 1179656 | tf_op jit(solution)/shard_map/ppermute | solution.py:45
  22.7 0.9 %collective-permute-done.10.refs_0_ = bf16[128,768]{1,0:T(8,128)(2,1)S(1)} collective-permute-done((bf16[128,768]{1,0:T(8,128)(2,1)S(1)}, bf16[128,768]{1,0:T(8,128)(2,1)S(1)}, u32[]{:S(2)}, u32[]{:S(2)}) %collective-permute-start.10) | collective-permute-done | bytes 196640 | tf_op jit(solution)/shard_map/ppermute | solution.py:45
  23.7 0.9 up_rows.4
  25.9 3.3 %collective-permute-start.9 = (f32[128,128]{1,0:T(8,128)S(1)}, f32[128,128]{1,0:T(8,128)S(1)}, u32[]{:S(2)}, u32[]{:S(2)}) collective-permute-start(f32[128,128]{1,0:T(8,128)S(1)} %get-tuple-element.44.refs_5_.refs_2_.refs_19_), channel_id=1, source_target_pairs={{0,8},{4,12},{8,0},{12,4},{1,9},{5,13},{9,1},{13,5},{2,10},{6,14},... | collective-permute-start | bytes 196616 | tf_op jit(solution)/shard_map/ppermute | solution.py:45
  29.9 2.8 %collective-permute-done.9.refs_2_.refs_4_ = f32[128,128]{1,0:T(8,128)S(1)} collective-permute-done((f32[128,128]{1,0:T(8,128)S(1)}, f32[128,128]{1,0:T(8,128)S(1)}, u32[]{:S(2)}, u32[]{:S(2)}) %collective-permute-start.9) | collective-permute-done | bytes 65568 | tf_op jit(solution)/shard_map/ppermute | solution.py:45
  34.6 2.7 %collective-permute-done.13.refs_4_.refs_2_.refs_9_ = f32[128,128]{1,0:T(8,128)S(1)} collective-permute-done((f32[128,128]{1,0:T(8,128)S(1)}, f32[128,128]{1,0:T(8,128)S(1)}, u32[]{:S(2)}, u32[]{:S(2)}) %collective-permute-start.13) | collective-permute-done | bytes 65568 | tf_op jit(solution)/shard_map/ppermute | solution.py:45
  37.3 0.9 up_rows.5
  39.2 1.0 %down_rows.3.refs_4_ = bf16[128,896]{1,0:T(8,128)(2,1)S(1)} custom-call(bf16[64,1536]{1,0:T(8,128)(2,1)S(1)} %get-tuple-element.50.refs_3_.refs_0_, bf16[64,1536]{1,0:T(8,128)(2,1)S(1)} %get-tuple-element.55.refs_1_, bf16[64,1536]{1,0:T(8,128)(2,1)S(1)} %collective-permute-done.17.refs_2_, bf16[64,1536]{1,0:T(8,128)(2,1)S(1)} %collective-permute-done.18.refs_3_, ...), custom_call_target="tpu_custom_call" | custom-call | flops 1024 | bytes 1024 | tf_op jit(solution)/shard_map/down_rows/pallas_call | solution.py:69
  41.0 1.6 %collective-permute-start.24 = (bf16[128,896]{1,0:T(8,128)(2,1)S(1)}, bf16[128,896]{1,0:T(8,128)(2,1)S(1)}, u32[]{:S(2)}, u32[]{:S(2)}) collective-permute-start(bf16[128,896]{1,0:T(8,128)(2,1)S(1)} %down_rows.3.refs_4_), channel_id=1, source_target_pairs={{0,8},{4,12},{8,0},{12,4},{1,9},{5,13},{9,1},{13,5},{2,10},{6,14},... | collective-permute-start | bytes 688136 | tf_op jit(solution)/shard_map/ppermute | solution.py:45
  42.7 3.4 %collective-permute-done.21.refs_1_ = bf16[64,3072]{1,0:T(8,128)(2,1)S(1)} collective-permute-done((bf16[64,3072]{1,0:T(8,128)(2,1)S(1)}, bf16[64,3072]{1,0:T(8,128)(2,1)S(1)}, u32[]{:S(2)}, u32[]{:S(2)}) %collective-permute-start.21) | collective-permute-done | bytes 393248 | tf_op jit(solution)/shard_map/ppermute | solution.py:45
  48.7 5.4 %collective-permute-done.24.refs_7_.refs_8_ = bf16[128,896]{1,0:T(8,128)(2,1)S(1)} collective-permute-done((bf16[128,896]{1,0:T(8,128)(2,1)S(1)}, bf16[128,896]{1,0:T(8,128)(2,1)S(1)}, u32[]{:S(2)}, u32[]{:S(2)}) %collective-permute-start.24) | collective-permute-done | bytes 229408 | tf_op jit(solution)/shard_map/ppermute | solution.py:45
  54.1 1.0 %down_rows.4.refs_4_ = bf16[128,896]{1,0:T(8,128)(2,1)S(1)} custom-call(bf16[64,1536]{1,0:T(8,128)(2,1)S(1)} %get-tuple-element.56.refs_0_.refs_6_.refs_5_, bf16[64,1536]{1,0:T(8,128)(2,1)S(1)} %get-tuple-element.57.refs_1_.refs_6_, bf16[64,1536]{1,0:T(8,128)(2,1)S(1)} %collective-permute-done.22.refs_2_.refs_7_, ...), custom_call_target="tpu_custom_call" | custom-call | flops 1024 | bytes 1024 | tf_op jit(solution)/shard_map/down_rows/pallas_call | solution.py:69
  55.1 2.6 %collective-permute-start.27 = (bf16[128,896]{1,0:T(8,128)(2,1)S(1)}, bf16[128,896]{1,0:T(8,128)(2,1)S(1)}, u32[]{:S(2)}, u32[]{:S(2)}) collective-permute-start(bf16[128,896]{1,0:T(8,128)(2,1)S(1)} %down_rows.4.refs_4_), channel_id=1, source_target_pairs={{0,12},{4,8},{8,4},{12,0},{1,13},{5,9},{9,5},{13,1},{2,14},{6,10},... | collective-permute-start | bytes 688136 | tf_op jit(solution)/shard_map/ppermute | solution.py:45
  59.0 4.5 %collective-permute-done.27.refs_7_.refs_8_.refs_9_ = bf16[128,896]{1,0:T(8,128)(2,1)S(1)} collective-permute-done((bf16[128,896]{1,0:T(8,128)(2,1)S(1)}, bf16[128,896]{1,0:T(8,128)(2,1)S(1)}, u32[]{:S(2)}, u32[]{:S(2)}) %collective-permute-start.27) | collective-permute-done | bytes 229408 | tf_op jit(solution)/shard_map/ppermute | solution.py:45
  63.5 1.0 %down_rows.5.refs_4_ = bf16[128,896]{1,0:T(8,128)(2,1)S(1)} custom-call(bf16[64,1536]{1,0:T(8,128)(2,1)S(1)} %get-tuple-element.58.refs_0_.refs_6_.refs_10_, bf16[64,1536]{1,0:T(8,128)(2,1)S(1)} %get-tuple-element.59.refs_1_.refs_11_, bf16[64,1536]{1,0:T(8,128)(2,1)S(1)} %collective-permute-done.25.refs_2_.refs_12_, ...), custom_call_target="tpu_custom_call" | custom-call | flops 1024 | bytes 1024 | tf_op jit(solution)/shard_map/down_rows/pallas_call | solution.py:69
  64.5 3.8 %collective-permute-start.30 = (bf16[128,896]{1,0:T(8,128)(2,1)S(1)}, bf16[128,896]{1,0:T(8,128)(2,1)S(1)}, u32[]{:S(2)}, u32[]{:S(2)}) collective-permute-start(bf16[128,896]{1,0:T(8,128)(2,1)S(1)} %down_rows.5.refs_4_), channel_id=1, source_target_pairs={{0,4},{4,0},{8,12},{12,8},{1,5},{5,1},{9,13},{13,9},{2,6},{6,2},{1... | collective-permute-start | bytes 688136 | tf_op jit(solution)/shard_map/ppermute | solution.py:45
  69.7 0.9 %collective-permute-done.28.refs_2_.refs_17_ = bf16[64,1536]{1,0:T(8,128)(2,1)S(1)} collective-permute-done((bf16[64,1536]{1,0:T(8,128)(2,1)S(1)}, bf16[64,1536]{1,0:T(8,128)(2,1)S(1)}, u32[]{:S(2)}, u32[]{:S(2)}) %collective-permute-start.28) | collective-permute-done | bytes 196640 | tf_op jit(solution)/shard_map/ppermute | solution.py:45
  70.9 2.4 %collective-permute-done.30.refs_9_.refs_10_ = bf16[128,896]{1,0:T(8,128)(2,1)S(1)} collective-permute-done((bf16[128,896]{1,0:T(8,128)(2,1)S(1)}, bf16[128,896]{1,0:T(8,128)(2,1)S(1)}, u32[]{:S(2)}, u32[]{:S(2)}) %collective-permute-start.30) | collective-permute-done | bytes 229408 | tf_op jit(solution)/shard_map/ppermute | solution.py:45
  74.0 1.8 %collective-permute-start.31 = (bf16[64,768]{1,0:T(8,128)(2,1)S(1)}, bf16[64,768]{1,0:T(8,128)(2,1)S(1)}, u32[]{:S(2)}, u32[]{:S(2)}) collective-permute-start(bf16[64,768]{1,0:T(8,128)(2,1)S(1)} %get-tuple-element.64.refs_0_), channel_id=1, source_target_pairs={{0,4},{4,0},{8,12},{12,8},{1,5},{5,1},{9,13},{13,9},{2,6},{6,2},{1... | collective-permute-start | bytes 294920 | tf_op jit(solution)/shard_map/ppermute | solution.py:45
  76.1 2.4 %collective-permute-start.33 = (bf16[64,768]{1,0:T(8,128)(2,1)S(1)}, bf16[64,768]{1,0:T(8,128)(2,1)S(1)}, u32[]{:S(2)}, u32[]{:S(2)}) collective-permute-start(bf16[64,768]{1,0:T(8,128)(2,1)S(1)} %get-tuple-element.64.refs_0_), channel_id=1, source_target_pairs={{0,12},{4,8},{8,4},{12,0},{1,13},{5,9},{9,5},{13,1},{2,14},{6,10},... | collective-permute-start | bytes 294920 | tf_op jit(solution)/shard_map/ppermute | solution.py:45
  78.5 1.5 %first_gradient_rows.1 = f32[64,3072]{1,0:T(8,128)} custom-call(bf16[64,1536]{1,0:T(8,128)(2,1)S(1)} %get-tuple-element.50.refs_3_.refs_0_, bf16[64,1536]{1,0:T(8,128)(2,1)S(1)} %get-tuple-element.55.refs_1_, bf16[64,1536]{1,0:T(8,128)(2,1)S(1)} %collective-permute-done.17.refs_2_, bf16[64,1536]{1,0:T(8,128)(2,1)S(1)} %collective-permute-done.18.refs_3_, ...), custom_call_target="tpu_custom_call" | custom-call | flops 1024 | bytes 1024 | tf_op jit(solution)/shard_map/first_gradient_rows/pallas_call | solution.py:69
  79.9 1.6 %update_rows.1.refs_4_ = bf16[128,768]{1,0:T(8,128)(2,1)} custom-call(bf16[64,1536]{1,0:T(8,128)(2,1)S(1)} %get-tuple-element.60.refs_0_.refs_10_.refs_15_, bf16[64,1536]{1,0:T(8,128)(2,1)S(1)} %get-tuple-element.61.refs_1_.refs_16_, bf16[64,1536]{1,0:T(8,128)(2,1)S(1)} %collective-permute-done.28.refs_2_.refs_17_, ...), custom_call_target="tpu_custom_call" | custom-call | flops 1024 | bytes 1024 | tf_op jit(solution)/shard_map/update_rows/pallas_call | solution.py:69
  81.6 3.1 %collective-permute-done.32.refs_2_ = bf16[64,768]{1,0:T(8,128)(2,1)S(1)} collective-permute-done((bf16[64,768]{1,0:T(8,128)(2,1)S(1)}, bf16[64,768]{1,0:T(8,128)(2,1)S(1)}, u32[]{:S(2)}, u32[]{:S(2)}) %collective-permute-start.32) | collective-permute-done | bytes 98336 | tf_op jit(solution)/shard_map/ppermute | solution.py:45
  84.7 0.9 %copy-done.2 = bf16[128,768]{1,0:T(8,128)(2,1)S(1)} copy-done((bf16[128,768]{1,0:T(8,128)(2,1)S(1)}, bf16[128,768]{1,0:T(8,128)(2,1)}, u32[]{:S(2)}) %copy-start.2) | copy-done | bytes 196632
  (74 shorter events, 14.7 us)
Async XLA Ops:
  0.6 13.4 %collective-permute-start.3 = (bf16[128,768]{1,0:T(8,128)(2,1)}, bf16[128,768]{1,0:T(8,128)(2,1)S(1)}, u32[]{:S(2)}, u32[]{:S(2)}) collective-permute-start(bf16[128,768]{1,0:T(8,128)(2,1)} %refs_1_.1), channel_id=1, source_target_pairs={{0,8},{4,12},{8,0},{12,4},{1,9},{5,13},{9,1},{13,5},{2,10},{6,14},... | collective-permute-start | bytes 589832 | tf_op jit(solution)/shard_map/ppermute | solution.py:45
  14.9 6.0 %collective-permute-start.5 = (bf16[64,1536]{1,0:T(8,128)(2,1)S(1)}, bf16[64,1536]{1,0:T(8,128)(2,1)S(1)}, u32[]{:S(2)}, u32[]{:S(2)}) collective-permute-start(bf16[64,1536]{1,0:T(8,128)(2,1)S(1)} %get-tuple-element.42), channel_id=1, source_target_pairs={{0,1},{1,0},{2,3},{3,2},{4,5},{5,4},{6,7},{7,6},{8,9},{9,8},{10,11... | collective-permute-start | bytes 589832 | tf_op jit(solution)/shard_map/ppermute | solution.py:45
  15.0 6.0 %collective-permute-start.6 = (bf16[64,1536]{1,0:T(8,128)(2,1)S(1)}, bf16[64,1536]{1,0:T(8,128)(2,1)S(1)}, u32[]{:S(2)}, u32[]{:S(2)}) collective-permute-start(bf16[64,1536]{1,0:T(8,128)(2,1)S(1)} %get-tuple-element.43), channel_id=1, source_target_pairs={{0,1},{1,0},{2,3},{3,2},{4,5},{5,4},{6,7},{7,6},{8,9},{9,8},{10,11... | collective-permute-start | bytes 589832 | tf_op jit(solution)/shard_map/ppermute | solution.py:45
  15.5 5.4 %collective-permute-start.7 = (f32[248,128]{1,0:T(8,128)S(1)}, f32[248,128]{1,0:T(8,128)S(1)}, u32[]{:S(2)}, u32[]{:S(2)}) collective-permute-start(f32[248,128]{1,0:T(8,128)S(1)} %add_packed.1.refs_3_.refs_0_), channel_id=1, source_target_pairs={{0,2},{2,0},{1,3},{3,1},{4,6},{6,4},{5,7},{7,5},{8,10},{10,8},{9,1... | collective-permute-start | bytes 380936 | tf_op jit(solution)/shard_map/ppermute | solution.py:45
  17.1 6.6 %collective-permute-start.10 = (bf16[128,768]{1,0:T(8,128)(2,1)S(1)}, bf16[128,768]{1,0:T(8,128)(2,1)S(1)}, u32[]{:S(2)}, u32[]{:S(2)}) collective-permute-start(bf16[128,768]{1,0:T(8,128)(2,1)S(1)} %collective-permute-done.3.refs_0_), channel_id=1, source_target_pairs={{0,4},{4,0},{8,12},{12,8},{1,5},{5,1},{9,13},{13,9},{2,6},{6,2},{1... | collective-permute-start | bytes 589832 | tf_op jit(solution)/shard_map/ppermute | solution.py:45
  21.1 11.5 %collective-permute-start.8 = (bf16[64,3072]{1,0:T(8,128)(2,1)S(1)}, bf16[64,3072]{1,0:T(8,128)(2,1)S(1)}, u32[]{:S(2)}, u32[]{:S(2)}) collective-permute-start(bf16[64,3072]{1,0:T(8,128)(2,1)S(1)} %add_cores.4.refs_3_.refs_0_), channel_id=1, source_target_pairs={{0,2},{2,0},{1,3},{3,1},{4,6},{6,4},{5,7},{7,5},{8,10},{10,8},{9,1... | collective-permute-start | bytes 1179656 | tf_op jit(solution)/shard_map/ppermute | solution.py:45
  24.5 4.6 %collective-permute-start.11 = (bf16[64,1536]{1,0:T(8,128)(2,1)S(1)}, bf16[64,1536]{1,0:T(8,128)(2,1)S(1)}, u32[]{:S(2)}, u32[]{:S(2)}) collective-permute-start(bf16[64,1536]{1,0:T(8,128)(2,1)S(1)} %get-tuple-element.48), channel_id=1, source_target_pairs={{0,1},{1,0},{2,3},{3,2},{4,5},{5,4},{6,7},{7,6},{8,9},{9,8},{10,11... | collective-permute-start | bytes 589832 | tf_op jit(solution)/shard_map/ppermute | solution.py:45
  24.6 4.9 %collective-permute-start.12 = (bf16[64,1536]{1,0:T(8,128)(2,1)S(1)}, bf16[64,1536]{1,0:T(8,128)(2,1)S(1)}, u32[]{:S(2)}, u32[]{:S(2)}) collective-permute-start(bf16[64,1536]{1,0:T(8,128)(2,1)S(1)} %get-tuple-element.49), channel_id=1, source_target_pairs={{0,1},{1,0},{2,3},{3,2},{4,5},{5,4},{6,7},{7,6},{8,9},{9,8},{10,11... | collective-permute-start | bytes 589832 | tf_op jit(solution)/shard_map/ppermute | solution.py:45
  25.1 9.0 %collective-permute-start.2 = (bf16[128,768]{1,0:T(8,128)(2,1)S(1)}, bf16[128,768]{1,0:T(8,128)(2,1)S(1)}, u32[]{:S(2)}, u32[]{:S(2)}) collective-permute-start(bf16[128,768]{1,0:T(8,128)(2,1)S(1)} %copy-done.5), channel_id=1, source_target_pairs={{0,4},{4,0},{8,12},{12,8},{1,5},{5,1},{9,13},{13,9},{2,6},{6,2},{1... | collective-permute-start | bytes 589832 | tf_op jit(solution)/shard_map/ppermute | solution.py:45
  25.9 6.7 %collective-permute-start.9 = (f32[128,128]{1,0:T(8,128)S(1)}, f32[128,128]{1,0:T(8,128)S(1)}, u32[]{:S(2)}, u32[]{:S(2)}) collective-permute-start(f32[128,128]{1,0:T(8,128)S(1)} %get-tuple-element.44.refs_5_.refs_2_.refs_19_), channel_id=1, source_target_pairs={{0,8},{4,12},{8,0},{12,4},{1,9},{5,13},{9,1},{13,5},{2,10},{6,14},... | collective-permute-start | bytes 196616 | tf_op jit(solution)/shard_map/ppermute | solution.py:45
  29.2 8.1 %collective-permute-start.13 = (f32[128,128]{1,0:T(8,128)S(1)}, f32[128,128]{1,0:T(8,128)S(1)}, u32[]{:S(2)}, u32[]{:S(2)}) collective-permute-start(f32[128,128]{1,0:T(8,128)S(1)} %get-tuple-element.44.refs_5_.refs_2_.refs_19_), channel_id=1, source_target_pairs={{0,12},{4,8},{8,4},{12,0},{1,13},{5,9},{9,5},{13,1},{2,14},{6,10},... | collective-permute-start | bytes 196616 | tf_op jit(solution)/shard_map/ppermute | solution.py:45
  29.6 7.7 %collective-permute-start.14 = (f32[128,128]{1,0:T(8,128)S(1)}, f32[128,128]{1,0:T(8,128)S(1)}, u32[]{:S(2)}, u32[]{:S(2)}) collective-permute-start(f32[128,128]{1,0:T(8,128)S(1)} %get-tuple-element.44.refs_5_.refs_2_.refs_19_), channel_id=1, source_target_pairs={{0,4},{4,0},{8,12},{12,8},{1,5},{5,1},{9,13},{13,9},{2,6},{6,2},{1... | collective-permute-start | bytes 196616 | tf_op jit(solution)/shard_map/ppermute | solution.py:45
  33.4 5.3 %collective-permute-start.17 = (bf16[64,1536]{1,0:T(8,128)(2,1)S(1)}, bf16[64,1536]{1,0:T(8,128)(2,1)S(1)}, u32[]{:S(2)}, u32[]{:S(2)}) collective-permute-start(bf16[64,1536]{1,0:T(8,128)(2,1)S(1)} %get-tuple-element.50.refs_3_.refs_0_), channel_id=1, source_target_pairs={{0,1},{1,0},{2,3},{3,2},{4,5},{5,4},{6,7},{7,6},{8,9},{9,8},{10,11... | collective-permute-start | bytes 589832 | tf_op jit(solution)/shard_map/ppermute | solution.py:45
  33.5 5.3 %collective-permute-start.18 = (bf16[64,1536]{1,0:T(8,128)(2,1)S(1)}, bf16[64,1536]{1,0:T(8,128)(2,1)S(1)}, u32[]{:S(2)}, u32[]{:S(2)}) collective-permute-start(bf16[64,1536]{1,0:T(8,128)(2,1)S(1)} %get-tuple-element.55.refs_1_), channel_id=1, source_target_pairs={{0,1},{1,0},{2,3},{3,2},{4,5},{5,4},{6,7},{7,6},{8,9},{9,8},{10,11... | collective-permute-start | bytes 589832 | tf_op jit(solution)/shard_map/ppermute | solution.py:45
  34.1 12.0 %collective-permute-start.21 = (bf16[64,3072]{1,0:T(8,128)(2,1)S(1)}, bf16[64,3072]{1,0:T(8,128)(2,1)S(1)}, u32[]{:S(2)}, u32[]{:S(2)}) collective-permute-start(bf16[64,3072]{1,0:T(8,128)(2,1)S(1)} %add_cores.5.refs_4_.refs_0_), channel_id=1, source_target_pairs={{0,2},{2,0},{1,3},{3,1},{4,6},{6,4},{5,7},{7,5},{8,10},{10,8},{9,1... | collective-permute-start | bytes 1179656 | tf_op jit(solution)/shard_map/ppermute | solution.py:45
  38.1 2.1 %collective-permute-start.15 = (bf16[64,1536]{1,0:T(8,128)(2,1)S(1)}, bf16[64,1536]{1,0:T(8,128)(2,1)S(1)}, u32[]{:S(2)}, u32[]{:S(2)}) collective-permute-start(bf16[64,1536]{1,0:T(8,128)(2,1)S(1)} %get-tuple-element.53), channel_id=1, source_target_pairs={{0,1},{1,0},{2,3},{3,2},{4,5},{5,4},{6,7},{7,6},{8,9},{9,8},{10,11... | collective-permute-start | bytes 589832 | tf_op jit(solution)/shard_map/ppermute | solution.py:45
  38.2 2.0 %collective-permute-start.16 = (bf16[64,1536]{1,0:T(8,128)(2,1)S(1)}, bf16[64,1536]{1,0:T(8,128)(2,1)S(1)}, u32[]{:S(2)}, u32[]{:S(2)}) collective-permute-start(bf16[64,1536]{1,0:T(8,128)(2,1)S(1)} %get-tuple-element.54), channel_id=1, source_target_pairs={{0,1},{1,0},{2,3},{3,2},{4,5},{5,4},{6,7},{7,6},{8,9},{9,8},{10,11... | collective-permute-start | bytes 589832 | tf_op jit(solution)/shard_map/ppermute | solution.py:45
  38.7 3.9 %collective-permute-start = (bf16[64,1536]{1,0:T(8,128)(2,1)S(1)}, bf16[64,1536]{1,0:T(8,128)(2,1)S(1)}, u32[]{:S(2)}, u32[]{:S(2)}) collective-permute-start(bf16[64,1536]{1,0:T(8,128)(2,1)S(1)} %get-tuple-element.36), channel_id=1, source_target_pairs={{0,1},{1,0},{2,3},{3,2},{4,5},{5,4},{6,7},{7,6},{8,9},{9,8},{10,11... | collective-permute-start | bytes 589832 | tf_op jit(solution)/shard_map/ppermute | solution.py:45
  38.8 3.8 %collective-permute-start.1 = (bf16[64,1536]{1,0:T(8,128)(2,1)S(1)}, bf16[64,1536]{1,0:T(8,128)(2,1)S(1)}, u32[]{:S(2)}, u32[]{:S(2)}) collective-permute-start(bf16[64,1536]{1,0:T(8,128)(2,1)S(1)} %get-tuple-element.37), channel_id=1, source_target_pairs={{0,1},{1,0},{2,3},{3,2},{4,5},{5,4},{6,7},{7,6},{8,9},{9,8},{10,11... | collective-permute-start | bytes 589832 | tf_op jit(solution)/shard_map/ppermute | solution.py:45
  40.4 17.3 %collective-permute-start.20 = (bf16[64,3072]{1,0:T(8,128)(2,1)S(1)}, bf16[64,3072]{1,0:T(8,128)(2,1)S(1)}, u32[]{:S(2)}, u32[]{:S(2)}) collective-permute-start(bf16[64,3072]{1,0:T(8,128)(2,1)S(1)} %add_cores.6.refs_4_.refs_0_), channel_id=1, source_target_pairs={{0,2},{2,0},{1,3},{3,1},{4,6},{6,4},{5,7},{7,5},{8,10},{10,8},{9,1... | collective-permute-start | bytes 1179656 | tf_op jit(solution)/shard_map/ppermute | solution.py:45
  41.0 13.1 %collective-permute-start.24 = (bf16[128,896]{1,0:T(8,128)(2,1)S(1)}, bf16[128,896]{1,0:T(8,128)(2,1)S(1)}, u32[]{:S(2)}, u32[]{:S(2)}) collective-permute-start(bf16[128,896]{1,0:T(8,128)(2,1)S(1)} %down_rows.3.refs_4_), channel_id=1, source_target_pairs={{0,8},{4,12},{8,0},{12,4},{1,9},{5,13},{9,1},{13,5},{2,10},{6,14},... | collective-permute-start | bytes 688136 | tf_op jit(solution)/shard_map/ppermute | solution.py:45
  46.9 1.5 %collective-permute-start.22 = (bf16[64,1536]{1,0:T(8,128)(2,1)S(1)}, bf16[64,1536]{1,0:T(8,128)(2,1)S(1)}, u32[]{:S(2)}, u32[]{:S(2)}) collective-permute-start(bf16[64,1536]{1,0:T(8,128)(2,1)S(1)} %get-tuple-element.56.refs_0_.refs_6_.refs_5_), channel_id=1, source_target_pairs={{0,1},{1,0},{2,3},{3,2},{4,5},{5,4},{6,7},{7,6},{8,9},{9,8},{10,11... | collective-permute-start | bytes 589832 | tf_op jit(solution)/shard_map/ppermute | solution.py:45
  47.0 1.7 %collective-permute-start.23 = (bf16[64,1536]{1,0:T(8,128)(2,1)S(1)}, bf16[64,1536]{1,0:T(8,128)(2,1)S(1)}, u32[]{:S(2)}, u32[]{:S(2)}) collective-permute-start(bf16[64,1536]{1,0:T(8,128)(2,1)S(1)} %get-tuple-element.57.refs_1_.refs_6_), channel_id=1, source_target_pairs={{0,1},{1,0},{2,3},{3,2},{4,5},{5,4},{6,7},{7,6},{8,9},{9,8},{10,11... | collective-permute-start | bytes 589832 | tf_op jit(solution)/shard_map/ppermute | solution.py:45
  47.5 20.9 %collective-permute-start.19 = (bf16[64,3072]{1,0:T(8,128)(2,1)S(1)}, bf16[64,3072]{1,0:T(8,128)(2,1)S(1)}, u32[]{:S(2)}, u32[]{:S(2)}) collective-permute-start(bf16[64,3072]{1,0:T(8,128)(2,1)S(1)} %add_cores.7.refs_4_.refs_0_), channel_id=1, source_target_pairs={{0,2},{2,0},{1,3},{3,1},{4,6},{6,4},{5,7},{7,5},{8,10},{10,8},{9,1... | collective-permute-start | bytes 1179656 | tf_op jit(solution)/shard_map/ppermute | solution.py:45
  55.1 8.5 %collective-permute-start.27 = (bf16[128,896]{1,0:T(8,128)(2,1)S(1)}, bf16[128,896]{1,0:T(8,128)(2,1)S(1)}, u32[]{:S(2)}, u32[]{:S(2)}) collective-permute-start(bf16[128,896]{1,0:T(8,128)(2,1)S(1)} %down_rows.4.refs_4_), channel_id=1, source_target_pairs={{0,12},{4,8},{8,4},{12,0},{1,13},{5,9},{9,5},{13,1},{2,14},{6,10},... | collective-permute-start | bytes 688136 | tf_op jit(solution)/shard_map/ppermute | solution.py:45
  58.5 5.1 %collective-permute-start.25 = (bf16[64,1536]{1,0:T(8,128)(2,1)S(1)}, bf16[64,1536]{1,0:T(8,128)(2,1)S(1)}, u32[]{:S(2)}, u32[]{:S(2)}) collective-permute-start(bf16[64,1536]{1,0:T(8,128)(2,1)S(1)} %get-tuple-element.58.refs_0_.refs_6_.refs_10_), channel_id=1, source_target_pairs={{0,1},{1,0},{2,3},{3,2},{4,5},{5,4},{6,7},{7,6},{8,9},{9,8},{10,11... | collective-permute-start | bytes 589832 | tf_op jit(solution)/shard_map/ppermute | solution.py:45
  58.5 5.0 %collective-permute-start.26 = (bf16[64,1536]{1,0:T(8,128)(2,1)S(1)}, bf16[64,1536]{1,0:T(8,128)(2,1)S(1)}, u32[]{:S(2)}, u32[]{:S(2)}) collective-permute-start(bf16[64,1536]{1,0:T(8,128)(2,1)S(1)} %get-tuple-element.59.refs_1_.refs_11_), channel_id=1, source_target_pairs={{0,1},{1,0},{2,3},{3,2},{4,5},{5,4},{6,7},{7,6},{8,9},{9,8},{10,11... | collective-permute-start | bytes 589832 | tf_op jit(solution)/shard_map/ppermute | solution.py:45
  64.5 8.8 %collective-permute-start.30 = (bf16[128,896]{1,0:T(8,128)(2,1)S(1)}, bf16[128,896]{1,0:T(8,128)(2,1)S(1)}, u32[]{:S(2)}, u32[]{:S(2)}) collective-permute-start(bf16[128,896]{1,0:T(8,128)(2,1)S(1)} %down_rows.5.refs_4_), channel_id=1, source_target_pairs={{0,4},{4,0},{8,12},{12,8},{1,5},{5,1},{9,13},{13,9},{2,6},{6,2},{1... | collective-permute-start | bytes 688136 | tf_op jit(solution)/shard_map/ppermute | solution.py:45
  69.2 1.7 %collective-permute-start.29 = (bf16[64,1536]{1,0:T(8,128)(2,1)S(1)}, bf16[64,1536]{1,0:T(8,128)(2,1)S(1)}, u32[]{:S(2)}, u32[]{:S(2)}) collective-permute-start(bf16[64,1536]{1,0:T(8,128)(2,1)S(1)} %get-tuple-element.61.refs_1_.refs_16_), channel_id=1, source_target_pairs={{0,1},{1,0},{2,3},{3,2},{4,5},{5,4},{6,7},{7,6},{8,9},{9,8},{10,11... | collective-permute-start | bytes 589832 | tf_op jit(solution)/shard_map/ppermute | solution.py:45
  74.0 7.6 %collective-permute-start.31 = (bf16[64,768]{1,0:T(8,128)(2,1)S(1)}, bf16[64,768]{1,0:T(8,128)(2,1)S(1)}, u32[]{:S(2)}, u32[]{:S(2)}) collective-permute-start(bf16[64,768]{1,0:T(8,128)(2,1)S(1)} %get-tuple-element.64.refs_0_), channel_id=1, source_target_pairs={{0,4},{4,0},{8,12},{12,8},{1,5},{5,1},{9,13},{13,9},{2,6},{6,2},{1... | collective-permute-start | bytes 294920 | tf_op jit(solution)/shard_map/ppermute | solution.py:45
  75.8 8.9 %collective-permute-start.32 = (bf16[64,768]{1,0:T(8,128)(2,1)S(1)}, bf16[64,768]{1,0:T(8,128)(2,1)S(1)}, u32[]{:S(2)}, u32[]{:S(2)}) collective-permute-start(bf16[64,768]{1,0:T(8,128)(2,1)S(1)} %get-tuple-element.64.refs_0_), channel_id=1, source_target_pairs={{0,8},{4,12},{8,0},{12,4},{1,9},{5,13},{9,1},{13,5},{2,10},{6,14},... | collective-permute-start | bytes 294920 | tf_op jit(solution)/shard_map/ppermute | solution.py:45
  76.1 8.6 %collective-permute-start.33 = (bf16[64,768]{1,0:T(8,128)(2,1)S(1)}, bf16[64,768]{1,0:T(8,128)(2,1)S(1)}, u32[]{:S(2)}, u32[]{:S(2)}) collective-permute-start(bf16[64,768]{1,0:T(8,128)(2,1)S(1)} %get-tuple-element.64.refs_0_), channel_id=1, source_target_pairs={{0,12},{4,8},{8,4},{12,0},{1,13},{5,9},{9,5},{13,1},{2,14},{6,10},... | collective-permute-start | bytes 294920 | tf_op jit(solution)/shard_map/ppermute | solution.py:45
  (10 other events, 83.0 us)

commit v4 on v3

v4 whole, which is shorter than its diff:
```python
import functools

import jax
import jax.numpy as jnp
from jax import lax
from jax.experimental import pallas as pl
from jax.experimental.pallas import tpu as pltpu
from jax.sharding import PartitionSpec as P

adapter_scale = 0.5
norm_eps = 1e-06
gelu_coef = 0.7978845608028654
f32 = jnp.float32
bf16 = jnp.bfloat16
LANES = 128
TOUCHES = 2
ORDER = [2, 3, 1]
OWN_PIECES = 3
UP_PIECES = (4, 2, 2)
OWN_PLACE = 0
GELU_PIECES = 2
OWN_GRANT = (64 * 1024 - 11440) * 1024


def gelu_value(pre_value):
    inner_arg = gelu_coef * (pre_value + 0.044715 * pre_value * pre_value * pre_value)
    return 0.5 * pre_value * (1.0 + jnp.tanh(inner_arg))


def dot(left, right):
    return jnp.dot(left, right, preferred_element_type=f32)


def dot_transposed(left, right):
    return lax.dot_general(left, right, (((1,), (1,)), ((), ())), preferred_element_type=f32)


def dot_rows(left, right):
    return lax.dot_general(left, right, (((0,), (0,)), ((), ())), preferred_element_type=f32)


def split_dot(product, left, right):
    high = left.astype(bf16)
    low = (left - high.astype(f32)).astype(bf16)
    return product(high, right) + product(low, right)


def swap(value, axis, distance):
    size = lax.axis_size(axis)
    return lax.ppermute(value, axis, [(i, i ^ distance) for i in range(size)])


def exchange(value, axis, kind):
    distance, size = 1, lax.axis_size(axis)
    while True:
        other = swap(value, axis, distance)
        distance *= 2
        if distance >= size:
            return value, other
        value = (value.astype(f32) + other.astype(f32)).astype(kind)


def call(body, outs, arrays, after=(), scratch=(), remote=(), scalars=(), grant=24 * 2**20):
    vmem = pl.BlockSpec(memory_space=pltpu.VMEM)
    specs = [pl.BlockSpec(memory_space=pltpu.SMEM)] * len(scalars)
    specs += [pl.BlockSpec(memory_space=pltpu.HBM)] * len(remote) + [vmem] * len(arrays)
    count = len(specs)
    specs += [pl.BlockSpec(memory_space=pl.ANY)] * len(after)
    total = len(specs)

    def kernel(*refs):
        body(*refs[:count], *refs[total:])

    results = pl.pallas_call(
        kernel,
        out_shape=[jax.ShapeDtypeStruct(shape, kind) for shape, kind in outs],
        in_specs=specs,
        out_specs=[vmem] * len(outs),
        scratch_shapes=list(scratch),
        compiler_params=pltpu.CompilerParams(vmem_limit_bytes=grant),
        cost_estimate=pl.CostEstimate(flops=1024, bytes_accessed=1024, transcendentals=0),
        name=body.__name__,
    )(*scalars, *remote, *arrays, *after)
    return list(results)


def pieces(width, count):
    tiles = width // LANES
    count = min(count, tiles)
    return [(tiles * (k + 1) // count - tiles * k // count) * LANES for k in range(count)]


def bases(arrays):
    at = 0
    for array in arrays:
        yield array, at
        at += array.shape[1]


def unit_pieces(arrays):
    for place, (array, base) in enumerate(bases(arrays)):
        yield array, base, array.shape[1] - (LANES if place == len(arrays) - 1 else 0)


def columns(width, step=512):
    return [slice(at, min(at + step, width)) for at in range(0, width, step)]


def rows_at(place, count):
    return pl.ds(pl.multiple_of(place * count, count), count)


def own_core():
    return lax.axis_index("sub")


def feature_block():
    return lax.axis_index("narrow") * lax.axis_size("sub") + lax.axis_index("sub")


def centred(x, mod):
    values = x[...].astype(f32)
    total = jnp.sum(values, axis=1, keepdims=True)
    rows = (values - total / x.shape[1]) * (1.0 + mod[1:2, :])
    return rows.astype(bf16), total, values


def three_terms(value):
    high = value.astype(bf16).astype(f32)
    middle = (value - high).astype(bf16).astype(f32)
    return [high, middle, value - high - middle]


def sum_lanes(values, total):
    squares = jnp.sum(values * values, axis=1, keepdims=True)
    lane = lax.broadcasted_iota(jnp.int32, (values.shape[0], LANES), 1) - 8 * feature_block()
    lanes = jnp.zeros((values.shape[0], LANES), f32)
    for place, term in enumerate(three_terms(total) + three_terms(squares)):
        lanes = jnp.where(lane == place, term, lanes)
    return lanes.astype(bf16)


def split_rows(value):
    high = value.astype(bf16)
    return [high, (value - high.astype(f32)).astype(bf16)]


def order_rows(value):
    middle = value.shape[0] // 2
    low, high = value[:middle], value[middle:]
    own = own_core()
    return [jnp.where(own == 0, low, high), jnp.where(own == 0, high, low)]


def own_rows(step, x_hbm, cot_hbm, mod_hbm, second_hbm, weight_hbm, *refs):
    *parts, packed, factor, mod, weight, x, cot, table, sems = refs
    kept, sent = parts[: len(parts) // 2], parts[len(parts) // 2 :]
    rows, features = x.shape
    rank = factor.shape[0]
    hidden = weight.shape[1]
    tiles = hidden // LANES
    block = feature_block()
    blocks = lax.axis_size("narrow") * lax.axis_size("sub")
    at = pl.ds(pl.multiple_of(block * features, LANES), features)
    copies = [
        pltpu.make_async_copy(mod_hbm, table, sems.at[0]),
        pltpu.make_async_copy(x_hbm, x, sems.at[1]),
        pltpu.make_async_copy(cot_hbm, cot, sems.at[2]),
        pltpu.make_async_copy(second_hbm.at[:, at], factor, sems.at[3]),
    ]
    loads = []
    for _, base, width in unit_pieces(kept):
        at = slice(base, base + width)
        loads.append(pltpu.make_async_copy(weight_hbm.at[:, at], weight.at[:, at], sems.at[4 + len(loads)]))
    for copy in copies + loads:
        copy.start()
    copies[0].wait()
    for kind in range(3):
        mod[kind : kind + 1, :] = table[kind, pl.ds(step[0], 1), :]
    copies[1].wait()
    normed, total, values = centred(x, mod)
    lanes = jnp.concatenate(order_rows(sum_lanes(values, total)), axis=0)
    extra = split_rows(1.0 + mod[1:2, :]) + split_rows(mod[0:1, :])
    extra.append(jnp.zeros((16 - len(extra), features), bf16))
    left_rows = jnp.concatenate(order_rows(normed) + extra, axis=0)
    for copy in copies[2:]:
        copy.wait()
    back_rows = (mod[2:3, :] * cot[...].astype(f32)).astype(bf16)
    padded = jnp.concatenate([jnp.zeros((LANES - rank, features), bf16), factor[...]], axis=0)
    packed[:rows] = dot_transposed(back_rows, padded)
    packed[rows:] = jnp.zeros((packed.shape[0] - rows, LANES), f32)
    middle = rows // 2
    kept[-1][:, -LANES:] = lanes[:middle]
    sent[-1][:, -LANES:] = lanes[middle:]
    for (piece, base, width), other, load in zip(unit_pieces(kept), sent, loads):
        load.wait()
        for at in columns(width):
            product = dot(left_rows, weight[:, base + at.start : base + at.stop])
            piece[:, at] = product[:middle].astype(bf16)
            other[:, at] = product[middle:rows].astype(bf16)
            scale_row = product[rows : rows + 1] + product[rows + 1 : rows + 2]
            shift_row = product[rows + 2 : rows + 3] + product[rows + 3 : rows + 4]
            for tile in range((at.stop - at.start) // LANES):
                lanes = slice(tile * LANES, (tile + 1) * LANES)
                place = rows + (base + at.start) // LANES + tile
                packed[pl.ds(place + block * tiles, 1), :] = scale_row[:, lanes]
                packed[place + blocks * tiles : place + blocks * tiles + 1, :] = shift_row[:, lanes]


def add_packed(left, right, out):
    out[...] = left[...] + right[...]


def unpack(left, right, low_back, table):
    rows, tiles = low_back.shape[0], table.shape[1] // LANES
    low_back[...] = (left[:rows] + right[:rows]).astype(bf16)
    count = (left.shape[0] - rows) // tiles
    for kind in range(count):
        for tile in range(tiles):
            at = slice(rows + kind * tiles + tile, rows + kind * tiles + tile + 1)
            table[kind : kind + 1, tile * LANES : (tile + 1) * LANES] = left[at] + right[at]


def up_rows(x, mod, weight, *parts):
    kept, sent = parts[: len(parts) // 2], parts[len(parts) // 2 :]
    middle = x.shape[0] // 2
    normed, total, values = centred(x, mod)
    rows = jnp.concatenate(order_rows(normed), axis=0)
    lanes = jnp.concatenate(order_rows(sum_lanes(values, total)), axis=0)
    kept[-1][:, -LANES:] = lanes[:middle]
    sent[-1][:, -LANES:] = lanes[middle:]
    for (piece, base, width), other in zip(unit_pieces(kept), sent):
        for at in columns(width):
            product = dot(rows, weight[:, base + at.start : base + at.stop]).astype(bf16)
            piece[:, at] = product[:middle]
            other[:, at] = product[middle:]


def add_cores(*refs):
    *parts, out = refs
    kept, received = parts[: len(parts) // 2], parts[len(parts) // 2 :]
    for (piece, base), other in zip(bases(kept), received):
        total = piece[...].astype(f32) + other[...].astype(f32)
        out[:, base : base + piece.shape[1]] = total.astype(bf16)


def touch(out):
    out[...] = jnp.zeros_like(out)


def gelu_rows(features, mine, other, table, *parts):
    blocks = lax.axis_size("narrow") * lax.axis_size("sub")
    lanes = mine[:, -LANES:].astype(f32) + other[:, -LANES:].astype(f32)

    def term(place):
        return lanes[:, place : place + 1] + lanes[:, place + 1 : place + 2] + lanes[:, place + 2 : place + 3]

    sums = [term(8 * block) for block in range(blocks)]
    squares = [term(8 * block + 3) for block in range(blocks)]
    row_mean = sum(sums[1:], sums[0]) / (blocks * features)
    row_msq = sum(squares[1:], squares[0]) / (blocks * features)
    inv_std = lax.rsqrt(row_msq - row_mean * row_mean + norm_eps)
    offsets = [value / features - row_mean for value in sums]
    for out, start in bases(parts):
        for at in columns(out.shape[1]):
            source = slice(at.start + start, at.stop + start)
            value = mine[:, source].astype(f32) + other[:, source].astype(f32)
            for block in range(blocks):
                value = value + offsets[block] * table[block : block + 1, source]
            pre_act = inv_std * value + table[blocks : blocks + 1, source]
            out[:, at] = gelu_value(pre_act).astype(bf16)


def both_cores(parts):
    count = len(parts) // 2
    return [jnp.concatenate([a[...], b[...]], axis=0) for a, b in zip(parts[:count], parts[count:])]


def low_product(activated, first):
    hidden = sum(piece.shape[1] for piece in activated)
    place = lax.axis_index("loop") * hidden
    terms = []
    for piece, base in bases(activated):
        at = pl.ds(pl.multiple_of(place + base, LANES), piece.shape[1])
        terms.append(dot_transposed(piece, first[:, at]))
    return sum(terms[1:], terms[0])


def down_product(activated, weight, at):
    terms = [dot(piece, weight[base : base + piece.shape[1], at]) for piece, base in bases(activated)]
    return sum(terms[1:], terms[0])


def store_rows(out, at, value):
    middle = value.shape[0] // 2
    own = own_core()
    out[rows_at(own, middle), at] = value[:middle].astype(out.dtype)
    out[rows_at(1 - own, middle), at] = value[middle:].astype(out.dtype)


def down_rows(weight, first, low_back, *refs):
    *parts, out = refs
    activated = both_cores(parts)
    features = weight.shape[1]
    low = low_product(activated, first)
    low = jnp.concatenate([low, jnp.zeros((low.shape[0], LANES - low.shape[1]), f32)], axis=1)
    last = slice(features, features + LANES)
    store_rows(out, last, low)
    out[:, last] = (out[:, last].astype(f32) + low_back[...].astype(f32)).astype(bf16)
    for at in columns(features, 256):
        store_rows(out, at, down_product(activated, weight, at))


def first_gradient_rows(count, *refs):
    *blocks, out = refs
    rank = out.shape[0]
    stride = 2 * count + 1
    places = range(0, len(blocks), stride)
    own = own_core()
    factors = []
    for at in places:
        middle = blocks[at].shape[0]
        low_back = blocks[at + stride - 1]
        factors += [low_back[rows_at(core, middle), -LANES:] for core in (own, 1 - own)]
    factors = jnp.concatenate(factors, axis=0)
    for which, (piece, base) in enumerate(bases(blocks[:count])):
        for at in columns(piece.shape[1]):
            right = []
            for place in places:
                right += [blocks[place + which][:, at], blocks[place + count + which][:, at]]
            product = dot_rows(factors, jnp.concatenate(right, axis=0))
            out[:, slice(at.start + base, at.stop + base)] = adapter_scale * product[LANES - rank :]


def second_gradient_part(terms, first, cot, mod, *refs):
    *arrays, out, low_total, low = refs
    received, parts = arrays[:terms], arrays[terms:]
    rank, features = first.shape[0], cot.shape[1]
    back_rows = (mod[2:3, :] * cot[...].astype(f32)).astype(bf16)
    store_rows(low, slice(0, rank), low_product(both_cores(parts), first))
    sums = low[...]
    for value in received:
        sums = sums + value[:, features : features + rank].astype(f32)
    low_total[...] = sums
    out[...] = (adapter_scale * split_dot(dot_rows, sums, back_rows)).astype(bf16)


def update_rows(terms, weight, low_total, factor, mod, *refs):
    *arrays, out, total = refs
    received, parts = arrays[:terms], arrays[terms:]
    activated = both_cores(parts)
    features = factor.shape[1]
    for at in columns(features, 256):
        store_rows(total, at, down_product(activated, weight, at))
    base = total[...] + adapter_scale * split_dot(dot, low_total[...], factor[...])
    for value in received:
        base = base + value[:, :features].astype(f32)
    out[...] = (mod[2:3, :] * base).astype(bf16)


def add_four(own, one, two, three, out):
    out[...] = (own[...].astype(f32) + one[...].astype(f32)) + (
        two[...].astype(f32) + three[...].astype(f32)
    )


def per_device(
    block_input_rows,
    frozen_up_weight,
    frozen_down_weight,
    down_first_factor,
    down_second_factor,
    modulation,
    timestep_index,
    cotangent,
):
    loop_size = lax.axis_size("loop")
    wide_size = lax.axis_size("narrow") * lax.axis_size("sub")
    rows, features = block_input_rows.shape
    hidden = frozen_up_weight.shape[1]
    rank = down_first_factor.shape[1]
    blocks = wide_size
    middle = rows // 2
    wide = features + LANES
    first = down_first_factor.T
    tiles = hidden // LANES
    dma = pltpu.SemaphoreType.DMA

    def swap_all(parts):
        return [swap(part, "sub", 1) for part in parts]

    def cut(count, extra=0):
        widths = pieces(hidden, count)
        widths[-1] += extra
        return [((middle, width), bf16) for width in widths]

    def named(body, *values):
        bound = functools.partial(body, *values)
        bound.__name__ = body.__name__
        return bound

    order = ORDER if loop_size == 4 else list(range(1, loop_size))
    raw = {k: swap(block_input_rows, "loop", k) for k in range(1, min(loop_size, 3))}
    for k in range(3, loop_size):
        raw[k] = swap(raw[2] if k == 3 else block_input_rows, "loop", 1 if k == 3 else k)

    length = -(-(rows + (blocks + 1) * tiles) // 8) * 8
    *own_parts, packed, second, mod = call(
        own_rows,
        [
            *(2 * cut(OWN_PIECES, LANES)),
            ((length, LANES), f32),
            ((rank, features), bf16),
            ((8, features), f32),
        ],
        [],
        scratch=[
            pltpu.VMEM((features, hidden), bf16),
            pltpu.VMEM((rows, features), bf16),
            pltpu.VMEM((rows, features), bf16),
            pltpu.VMEM((3, modulation.shape[0], features), f32),
            dma((4 + OWN_PIECES,)),
        ],
        scalars=[timestep_index],
        remote=[
            block_input_rows,
            cotangent,
            jnp.transpose(modulation, (1, 0, 2)),
            down_second_factor,
            frozen_up_weight,
        ],
        grant=OWN_GRANT,
    )
    (packed,) = call(add_packed, [((length, LANES), f32)], [packed, swap(packed, "sub", 1)])
    low_back, table = call(
        unpack,
        [((rows, LANES), bf16), ((-(-(blocks + 1) // 8) * 8, hidden), f32)],
        list(exchange(packed, "narrow", f32)),
    )
    pairs = []
    activated = []
    received = []

    def cores(parts):
        count = len(parts) // 2
        return parts[:count] + swap_all(parts[count:])

    def multiply(place, after):
        return call(
            up_rows, 2 * cut(UP_PIECES[min(place, 2)], LANES), [raw[order[place]], mod, frozen_up_weight], after
        )

    def add(parts, after):
        (value,) = call(add_cores, [((middle, hidden + LANES), bf16)], cores(parts), after)
        pairs.append(exchange(value, "narrow", bf16))
        return [value]

    def activate(after):
        place = len(activated)
        parts = call(
            named(gelu_rows, features),
            cut(GELU_PIECES),
            [*pairs[place], table],
            after,
        )
        activated.append([*parts, *swap_all(parts)])
        return parts[:1]

    def down(place, after):
        operands = [frozen_down_weight, first, low_back, *activated[place]]
        (joined,) = call(down_rows, [((rows, wide), bf16)], operands, after)
        received.append(swap(joined, "loop", order[place]))
        return [joined]

    def wait(after):
        return call(touch, [((8, LANES), f32)], [], after)

    last = len(order)
    after = [packed]
    for place in range(last):
        if place >= 2:
            after = activate(after)
        parts = multiply(place, after)
        after = parts[:1]
        if place == 0:
            after = after + [table]
        if place >= 2:
            after = down(place - 2, after)
        after = add(parts, after)
        if place == OWN_PLACE:
            after = add(own_parts, after)
            own_pair = pairs.pop()
    after = activate(after)
    after = wait(after + received[-1:])
    if OWN_PLACE > 2:
        after = add(own_parts, after)
        own_pair = pairs.pop()
    else:
        for _ in range(TOUCHES):
            after = wait(after)
    after = down(last - 2, after)
    after = activate(after)
    after = wait(down(last - 1, after) + received[-2:-1])
    pairs.append(own_pair)
    after = activate(after)
    own = activated[last]
    contribution, low_total = call(
        named(second_gradient_part, last),
        [((rank, features), bf16), ((rows, rank), f32)],
        [first, cotangent, mod, *received, *own],
        after,
        scratch=[pltpu.VMEM((rows, rank), f32)],
    )
    (block_update,) = call(
        named(update_rows, last),
        [((rows, features), bf16)],
        [frozen_down_weight, low_total, second, mod, *received, *own],
        scratch=[pltpu.VMEM((rows, features), f32)],
    )
    gathered = []
    for parts, rows_of in zip(activated, received + [low_back]):
        gathered += [*parts, rows_of]
    (first_gradient,) = call(
        named(first_gradient_rows, len(cut(GELU_PIECES))),
        [((rank, hidden), f32)],
        gathered,
        [low_total],
    )
    if loop_size == 4:
        terms = [swap(contribution, "loop", k) for k in (1, 2, 3)]
        (second_gradient,) = call(
            add_four,
            [((rank, features), f32)],
            [contribution, *terms],
            [low_total],
        )
    else:
        second_gradient = lax.psum(contribution, "loop").astype(f32)
    return (block_update, first_gradient.T, second_gradient)


def solution(mesh):
    in_specs = (
        P(("groups", "loop"), ("narrow", "sub")),
        P(("narrow", "sub"), "loop"),
        P("loop", ("narrow", "sub")),
        P(),
        P(),
        P(None, None, ("narrow", "sub")),
        P("groups"),
        P(("groups", "loop"), ("narrow", "sub")),
    )
    out_specs = (
        P(("groups", "loop"), ("narrow", "sub")),
        P(("groups", "loop"), None),
        P("groups", ("narrow", "sub")),
    )
    return jax.shard_map(
        per_device, mesh=mesh, in_specs=in_specs, out_specs=out_specs, check_vma=False
    )
```

time: 86.6 us -> 79.3 us (0.916)
  waiting for transfers between devices: 34.8 us -> 30 us
  starting transfers between devices: 31.2 us -> 29.4 us
  local copies, waits for them, and re-layouts: 1.84 us -> 0.91 us
    ppermute x34, waiting for transfers between devices: 34.8 us -> 30 us  [swap(): return lax.ppermute(value, axis, [(i, i ^ distance) for i in range(size)])]
    ppermute x34, starting transfers between devices: 31.2 us -> 29.4 us  [swap(): return lax.ppermute(value, axis, [(i, i ^ distance) for i in range(size)])]
    unnamed x16 -> x14, local copies, waits for them, and re-layouts: 1.84 us -> 0.91 us
    pallas_call x21 -> x25, Pallas kernels: 16.9 us -> 17.2 us  [call(): pl.pallas_call(kernel, out_shape=[jax.ShapeDtypeStruct(shape, kind) for s...]
  transfers between devices with their start and end apart: 34 -> 34, of which waited for: 16 -> 20; matrix products, arithmetic and copies ran while one was open for 0% -> 0% of each run, Pallas kernels for 17% -> 19%
where the time goes in v4:
time: 79.3 us; the launch traced here: 79.1 us
  waiting for transfers between devices  30 us (38%)
  starting transfers between devices  29.4 us (37%)
  Pallas kernels  17.2 us (22%)
  between operations  1.59 us (2%)
  local copies, waits for them, and re-layouts  0.91 us (1%)
    ppermute x34, waiting for transfers between devices, swap(): return lax.ppermute(value, axis, [(i, i ^ distance) for i in range(size)])  30 us
    ppermute x34, starting transfers between devices, swap(): return lax.ppermute(value, axis, [(i, i ^ distance) for i in range(size)])  29.4 us
    pallas_call x25, Pallas kernels, call(): pl.pallas_call(kernel, out_shape=[jax.ShapeDtypeStruct(shape, kind) for s...  17.2 us
  transfers between devices with their start and end apart: 34, of which 20 were waited for; matrix products, arithmetic and copies ran while one was open for 0% of the time, Pallas kernels for 19%

profile of v4, /device:TPU:0, one launch (start us, length us, event | category | flops | bytes accessed | tf_op | source)
XLA Modules:
  0.0 79.1 jit_solution(18061390921156177397)
XLA Ops:
  0.6 4.1 %collective-permute-start.2 = (bf16[128,768]{1,0:T(8,128)(2,1)}, bf16[128,768]{1,0:T(8,128)(2,1)S(1)}, u32[]{:S(2)}, u32[]{:S(2)}) collective-permute-start(bf16[128,768]{1,0:T(8,128)(2,1)} %refs_1_.2), channel_id=1, source_target_pairs={{0,8},{4,12},{8,0},{12,4},{1,9},{5,13},{9,1},{13,5},{2,10},{6,14},... | collective-permute-start | bytes 589832 | tf_op jit(solution)/shard_map/ppermute | solution.py:50
  6.3 3.2 %own_rows.1 = (bf16[64,1024]{1,0:T(8,128)(2,1)S(1)}, bf16[64,1024]{1,0:T(8,128)(2,1)S(1)}, bf16[64,1152]{1,0:T(8,128)(2,1)S(1)}, bf16[64,1024]{1,0:T(8,128)(2,1)...) custom-call(s32[1]{0:T(128)S(6)} %copy.11.refs_0_, ...), custom_call_target="tpu_custom_call" | custom-call | flops 1024 | bytes 1024 | tf_op jit(solution)/shard_map/own_rows/pallas_call | solution.py:74
  9.5 1.3 %collective-permute-done.refs_1_ = f32[248,128]{1,0:T(8,128)S(1)} collective-permute-done((f32[248,128]{1,0:T(8,128)S(1)}, f32[248,128]{1,0:T(8,128)S(1)}, u32[]{:S(2)}, u32[]{:S(2)}) %collective-permute-start) | collective-permute-done | bytes 127008 | tf_op jit(solution)/shard_map/ppermute | solution.py:50
  10.9 1.6 %collective-permute-start.1 = (f32[248,128]{1,0:T(8,128)S(1)}, f32[248,128]{1,0:T(8,128)S(1)}, u32[]{:S(2)}, u32[]{:S(2)}) collective-permute-start(f32[248,128]{1,0:T(8,128)S(1)} %add_packed.1.refs_0_.refs_3_), channel_id=1, source_target_pairs={{0,2},{2,0},{1,3},{3,1},{4,6},{6,4},{5,7},{7,5},{8,10},{10,8},{9,1... | collective-permute-start | bytes 380936 | tf_op jit(solution)/shard_map/ppermute | solution.py:50
  12.4 1.6 %collective-permute-done.2.refs_0_ = bf16[128,768]{1,0:T(8,128)(2,1)S(1)} collective-permute-done((bf16[128,768]{1,0:T(8,128)(2,1)}, bf16[128,768]{1,0:T(8,128)(2,1)S(1)}, u32[]{:S(2)}, u32[]{:S(2)}) %collective-permute-start.2) | collective-permute-done | bytes 196640 | tf_op jit(solution)/shard_map/ppermute | solution.py:50
  16.4 1.6 %collective-permute-start.8 = (bf16[128,768]{1,0:T(8,128)(2,1)S(1)}, bf16[128,768]{1,0:T(8,128)(2,1)S(1)}, u32[]{:S(2)}, u32[]{:S(2)}) collective-permute-start(bf16[128,768]{1,0:T(8,128)(2,1)S(1)} %collective-permute-done.2.refs_0_), channel_id=1, source_target_pairs={{0,4},{4,0},{8,12},{12,8},{1,5},{5,1},{9,13},{13,9},{2,6},{6,2},{1... | collective-permute-start | bytes 589832 | tf_op jit(solution)/shard_map/ppermute | solution.py:50
  18.2 1.6 %collective-permute-start.7 = (bf16[64,3200]{1,0:T(8,128)(2,1)S(1)}, bf16[64,3200]{1,0:T(8,128)(2,1)S(1)}, u32[]{:S(2)}, u32[]{:S(2)}) collective-permute-start(bf16[64,3200]{1,0:T(8,128)(2,1)S(1)} %add_cores.4.refs_6_.refs_0_), channel_id=1, source_target_pairs={{0,2},{2,0},{1,3},{3,1},{4,6},{6,4},{5,7},{7,5},{8,10},{10,8},{9,1... | collective-permute-start | bytes 1228808 | tf_op jit(solution)/shard_map/ppermute | solution.py:50
  20.3 1.0 %collective-permute-done.9.refs_3_ = bf16[64,1024]{1,0:T(8,128)(2,1)S(1)} collective-permute-done((bf16[64,1024]{1,0:T(8,128)(2,1)S(1)}, bf16[64,1024]{1,0:T(8,128)(2,1)S(1)}, u32[]{:S(2)}, u32[]{:S(2)}) %collective-permute-start.9) | collective-permute-done | bytes 131104 | tf_op jit(solution)/shard_map/ppermute | solution.py:50
  21.7 1.2 %collective-permute-done.8.refs_0_ = bf16[128,768]{1,0:T(8,128)(2,1)S(1)} collective-permute-done((bf16[128,768]{1,0:T(8,128)(2,1)S(1)}, bf16[128,768]{1,0:T(8,128)(2,1)S(1)}, u32[]{:S(2)}, u32[]{:S(2)}) %collective-permute-start.8) | collective-permute-done | bytes 196640 | tf_op jit(solution)/shard_map/ppermute | solution.py:50
  24.5 1.1 %collective-permute-start.16 = (bf16[128,768]{1,0:T(8,128)(2,1)S(1)}, bf16[128,768]{1,0:T(8,128)(2,1)S(1)}, u32[]{:S(2)}, u32[]{:S(2)}) collective-permute-start(bf16[128,768]{1,0:T(8,128)(2,1)S(1)} %copy-done.4), channel_id=1, source_target_pairs={{0,4},{4,0},{8,12},{12,8},{1,5},{5,1},{9,13},{13,9},{2,6},{6,2},{1... | collective-permute-start | bytes 589832 | tf_op jit(solution)/shard_map/ppermute | solution.py:50
  25.8 3.1 %collective-permute-done.7.refs_1_ = bf16[64,3200]{1,0:T(8,128)(2,1)S(1)} collective-permute-done((bf16[64,3200]{1,0:T(8,128)(2,1)S(1)}, bf16[64,3200]{1,0:T(8,128)(2,1)S(1)}, u32[]{:S(2)}, u32[]{:S(2)}) %collective-permute-start.7) | collective-permute-done | bytes 409632 | tf_op jit(solution)/shard_map/ppermute | solution.py:50
  29.8 1.6 %collective-permute-done.16.refs_0_ = bf16[128,768]{1,0:T(8,128)(2,1)S(1)} collective-permute-done((bf16[128,768]{1,0:T(8,128)(2,1)S(1)}, bf16[128,768]{1,0:T(8,128)(2,1)S(1)}, u32[]{:S(2)}, u32[]{:S(2)}) %collective-permute-start.16) | collective-permute-done | bytes 196640 | tf_op jit(solution)/shard_map/ppermute | solution.py:50
  32.9 1.5 %collective-permute-start.18 = (bf16[64,3200]{1,0:T(8,128)(2,1)S(1)}, bf16[64,3200]{1,0:T(8,128)(2,1)S(1)}, u32[]{:S(2)}, u32[]{:S(2)}) collective-permute-start(bf16[64,3200]{1,0:T(8,128)(2,1)S(1)} %add_cores.6.refs_3_.refs_0_), channel_id=1, source_target_pairs={{0,2},{2,0},{1,3},{3,1},{4,6},{6,4},{5,7},{7,5},{8,10},{10,8},{9,1... | collective-permute-start | bytes 1228808 | tf_op jit(solution)/shard_map/ppermute | solution.py:50
  34.7 1.0 %down_rows.3.refs_4_ = bf16[128,896]{1,0:T(8,128)(2,1)S(1)} custom-call(bf16[3072,768]{1,0:T(8,128)(2,1)S(1)} %bitcast.4, bf16[64,12288]{1,0:T(8,128)(2,1)S(1)} %bitcast.5, bf16[128,128]{1,0:T(8,128)(2,1)S(1)} %get-tuple-element.42.refs_2_.refs_19_, bf16[64,1536]{1,0:T(8,128)(2,1)S(1)} %get-tuple-element.62.refs_3_.refs_0_, ...), custom_call_target="tpu_custom_call" | custom-call | flops 1024 | bytes 1024 | tf_op jit(solution)/shard_map/down_rows/pallas_call | solution.py:74
  36.0 1.1 %collective-permute-start.24 = (bf16[64,3200]{1,0:T(8,128)(2,1)S(1)}, bf16[64,3200]{1,0:T(8,128)(2,1)S(1)}, u32[]{:S(2)}, u32[]{:S(2)}) collective-permute-start(bf16[64,3200]{1,0:T(8,128)(2,1)S(1)} %add_cores.7.refs_3_.refs_0_), channel_id=1, source_target_pairs={{0,2},{2,0},{1,3},{3,1},{4,6},{6,4},{5,7},{7,5},{8,10},{10,8},{9,1... | collective-permute-start | bytes 1228808 | tf_op jit(solution)/shard_map/ppermute | solution.py:50
  37.1 2.3 %collective-permute-start.17 = (bf16[128,896]{1,0:T(8,128)(2,1)S(1)}, bf16[128,896]{1,0:T(8,128)(2,1)S(1)}, u32[]{:S(2)}, u32[]{:S(2)}) collective-permute-start(bf16[128,896]{1,0:T(8,128)(2,1)S(1)} %down_rows.3.refs_4_), channel_id=1, source_target_pairs={{0,8},{4,12},{8,0},{12,4},{1,9},{5,13},{9,1},{13,5},{2,10},{6,14},... | collective-permute-start | bytes 688136 | tf_op jit(solution)/shard_map/ppermute | solution.py:50
  39.4 5.8 %collective-permute-done.18.refs_1_ = bf16[64,3200]{1,0:T(8,128)(2,1)S(1)} collective-permute-done((bf16[64,3200]{1,0:T(8,128)(2,1)S(1)}, bf16[64,3200]{1,0:T(8,128)(2,1)S(1)}, u32[]{:S(2)}, u32[]{:S(2)}) %collective-permute-start.18) | collective-permute-done | bytes 409632 | tf_op jit(solution)/shard_map/ppermute | solution.py:50
  46.6 1.5 %collective-permute-start.28 = (bf16[64,3200]{1,0:T(8,128)(2,1)S(1)}, bf16[64,3200]{1,0:T(8,128)(2,1)S(1)}, u32[]{:S(2)}, u32[]{:S(2)}) collective-permute-start(bf16[64,3200]{1,0:T(8,128)(2,1)S(1)} %add_cores.5.refs_3_.refs_0_), channel_id=1, source_target_pairs={{0,2},{2,0},{1,3},{3,1},{4,6},{6,4},{5,7},{7,5},{8,10},{10,8},{9,1... | collective-permute-start | bytes 1228808 | tf_op jit(solution)/shard_map/ppermute | solution.py:50
  48.1 2.2 %collective-permute-done.17.refs_1_.refs_3_.refs_4_ = bf16[128,896]{1,0:T(8,128)(2,1)S(1)} collective-permute-done((bf16[128,896]{1,0:T(8,128)(2,1)S(1)}, bf16[128,896]{1,0:T(8,128)(2,1)S(1)}, u32[]{:S(2)}, u32[]{:S(2)}) %collective-permute-start.17) | collective-permute-done | bytes 229408 | tf_op jit(solution)/shard_map/ppermute | solution.py:50
  50.4 1.0 %down_rows.4.refs_3_ = bf16[128,896]{1,0:T(8,128)(2,1)S(1)} custom-call(bf16[3072,768]{1,0:T(8,128)(2,1)S(1)} %bitcast.4, bf16[64,12288]{1,0:T(8,128)(2,1)S(1)} %bitcast.6, bf16[128,128]{1,0:T(8,128)(2,1)S(1)} %get-tuple-element.42.refs_2_.refs_19_, bf16[64,1536]{1,0:T(8,128)(2,1)S(1)} %get-tuple-element.68.refs_0_.refs_3_.refs_5_, ...), custom_call_target="tpu_custom_call" | custom-call | flops 1024 | bytes 1024 | tf_op jit(solution)/shard_map/down_rows/pallas_call | solution.py:74
  51.4 3.3 %collective-permute-start.23 = (bf16[128,896]{1,0:T(8,128)(2,1)S(1)}, bf16[128,896]{1,0:T(8,128)(2,1)S(1)}, u32[]{:S(2)}, u32[]{:S(2)}) collective-permute-start(bf16[128,896]{1,0:T(8,128)(2,1)S(1)} %down_rows.4.refs_3_), channel_id=1, source_target_pairs={{0,12},{4,8},{8,4},{12,0},{1,13},{5,9},{9,5},{13,1},{2,14},{6,10},... | collective-permute-start | bytes 688136 | tf_op jit(solution)/shard_map/ppermute | solution.py:50
  56.1 0.9 %collective-permute-done.25.refs_5_.refs_12_ = bf16[64,1536]{1,0:T(8,128)(2,1)S(1)} collective-permute-done((bf16[64,1536]{1,0:T(8,128)(2,1)S(1)}, bf16[64,1536]{1,0:T(8,128)(2,1)S(1)}, u32[]{:S(2)}, u32[]{:S(2)}) %collective-permute-start.25) | collective-permute-done | bytes 196640 | tf_op jit(solution)/shard_map/ppermute | solution.py:50
  57.3 1.0 %down_rows.5.refs_0_ = bf16[128,896]{1,0:T(8,128)(2,1)S(1)} custom-call(bf16[3072,768]{1,0:T(8,128)(2,1)S(1)} %bitcast.4, bf16[64,12288]{1,0:T(8,128)(2,1)S(1)} %bitcast.7, bf16[128,128]{1,0:T(8,128)(2,1)S(1)} %get-tuple-element.42.refs_2_.refs_19_, bf16[64,1536]{1,0:T(8,128)(2,1)S(1)} %get-tuple-element.70.refs_3_.refs_7_.refs_10_, ...), custom_call_target="tpu_custom_call" | custom-call | flops 1024 | bytes 1024 | tf_op jit(solution)/shard_map/down_rows/pallas_call | solution.py:74
  58.8 1.7 %collective-permute-done.23.refs_1_.refs_4_.refs_5_.refs_9_ = bf16[128,896]{1,0:T(8,128)(2,1)S(1)} collective-permute-done((bf16[128,896]{1,0:T(8,128)(2,1)S(1)}, bf16[128,896]{1,0:T(8,128)(2,1)S(1)}, u32[]{:S(2)}, u32[]{:S(2)}) %collective-permute-start.23) | collective-permute-done | bytes 229408 | tf_op jit(solution)/shard_map/ppermute | solution.py:50
  60.6 1.7 %collective-permute-done.28.refs_1_ = bf16[64,3200]{1,0:T(8,128)(2,1)S(1)} collective-permute-done((bf16[64,3200]{1,0:T(8,128)(2,1)S(1)}, bf16[64,3200]{1,0:T(8,128)(2,1)S(1)}, u32[]{:S(2)}, u32[]{:S(2)}) %collective-permute-start.28) | collective-permute-done | bytes 409632 | tf_op jit(solution)/shard_map/ppermute | solution.py:50
  63.7 0.9 %collective-permute-done.29.refs_8_.refs_9_.refs_17_ = bf16[64,1536]{1,0:T(8,128)(2,1)S(1)} collective-permute-done((bf16[64,1536]{1,0:T(8,128)(2,1)S(1)}, bf16[64,1536]{1,0:T(8,128)(2,1)S(1)}, u32[]{:S(2)}, u32[]{:S(2)}) %collective-permute-start.29) | collective-permute-done | bytes 196640 | tf_op jit(solution)/shard_map/ppermute | solution.py:50
  64.9 1.2 %collective-permute-done.27.refs_5_.refs_6_.refs_14_ = bf16[128,896]{1,0:T(8,128)(2,1)S(1)} collective-permute-done((bf16[128,896]{1,0:T(8,128)(2,1)S(1)}, bf16[128,896]{1,0:T(8,128)(2,1)S(1)}, u32[]{:S(2)}, u32[]{:S(2)}) %collective-permute-start.27) | collective-permute-done | bytes 229408 | tf_op jit(solution)/shard_map/ppermute | solution.py:50
  66.8 3.2 %collective-permute-start.33 = (bf16[64,768]{1,0:T(8,128)(2,1)S(1)}, bf16[64,768]{1,0:T(8,128)(2,1)S(1)}, u32[]{:S(2)}, u32[]{:S(2)}) collective-permute-start(bf16[64,768]{1,0:T(8,128)(2,1)S(1)} %get-tuple-element.76.refs_0_), channel_id=1, source_target_pairs={{0,12},{4,8},{8,4},{12,0},{1,13},{5,9},{9,5},{13,1},{2,14},{6,10},... | collective-permute-start | bytes 294920 | tf_op jit(solution)/shard_map/ppermute | solution.py:50
  70.0 1.3 %collective-permute-start.31 = (bf16[64,768]{1,0:T(8,128)(2,1)S(1)}, bf16[64,768]{1,0:T(8,128)(2,1)S(1)}, u32[]{:S(2)}, u32[]{:S(2)}) collective-permute-start(bf16[64,768]{1,0:T(8,128)(2,1)S(1)} %get-tuple-element.76.refs_0_), channel_id=1, source_target_pairs={{0,4},{4,0},{8,12},{12,8},{1,5},{5,1},{9,13},{13,9},{2,6},{6,2},{1... | collective-permute-start | bytes 294920 | tf_op jit(solution)/shard_map/ppermute | solution.py:50
  71.3 1.5 %first_gradient_rows.1 = f32[64,3072]{1,0:T(8,128)} custom-call(bf16[64,1536]{1,0:T(8,128)(2,1)S(1)} %get-tuple-element.62.refs_3_.refs_0_, bf16[64,1536]{1,0:T(8,128)(2,1)S(1)} %get-tuple-element.63.refs_4_.refs_1_, bf16[64,1536]{1,0:T(8,128)(2,1)S(1)} %collective-permute-done.14.refs_5_.refs_2_, ...), custom_call_target="tpu_custom_call" | custom-call | flops 1024 | bytes 1024 | tf_op jit(solution)/shard_map/first_gradient_rows/pallas_call | solution.py:74
  72.8 1.6 %update_rows.1 = bf16[128,768]{1,0:T(8,128)(2,1)} custom-call(bf16[3072,768]{1,0:T(8,128)(2,1)S(1)} %bitcast.4, f32[128,64]{1,0:T(8,128)S(1)} %get-tuple-element.74.refs_1_.refs_20_.refs_4_, bf16[64,768]{1,0:T(8,128)(2,1)S(1)} %get-tuple-element.75.refs_2_, f32[8,768]{1,0:T(8,128)S(1)} %get-tuple-element.40.refs_1_.refs_2_.refs_3_, ...), custom_call_target="tpu_custom_call" | custom-call | flops 1024 | bytes 1024 | tf_op jit(solution)/shard_map/update_rows/pallas_call | solution.py:74
  74.4 4.0 %collective-permute-done.32.refs_2_ = bf16[64,768]{1,0:T(8,128)(2,1)S(1)} collective-permute-done((bf16[64,768]{1,0:T(8,128)(2,1)S(1)}, bf16[64,768]{1,0:T(8,128)(2,1)S(1)}, u32[]{:S(2)}, u32[]{:S(2)}) %collective-permute-start.32) | collective-permute-done | bytes 98336 | tf_op jit(solution)/shard_map/ppermute | solution.py:50
  (76 shorter events, 15.6 us)
Async XLA Ops:
  0.6 13.4 %collective-permute-start.2 = (bf16[128,768]{1,0:T(8,128)(2,1)}, bf16[128,768]{1,0:T(8,128)(2,1)S(1)}, u32[]{:S(2)}, u32[]{:S(2)}) collective-permute-start(bf16[128,768]{1,0:T(8,128)(2,1)} %refs_1_.2), channel_id=1, source_target_pairs={{0,8},{4,12},{8,0},{12,4},{1,9},{5,13},{9,1},{13,5},{2,10},{6,14},... | collective-permute-start | bytes 589832 | tf_op jit(solution)/shard_map/ppermute | solution.py:50
  10.9 5.5 %collective-permute-start.1 = (f32[248,128]{1,0:T(8,128)S(1)}, f32[248,128]{1,0:T(8,128)S(1)}, u32[]{:S(2)}, u32[]{:S(2)}) collective-permute-start(f32[248,128]{1,0:T(8,128)S(1)} %add_packed.1.refs_0_.refs_3_), channel_id=1, source_target_pairs={{0,2},{2,0},{1,3},{3,1},{4,6},{6,4},{5,7},{7,5},{8,10},{10,8},{9,1... | collective-permute-start | bytes 380936 | tf_op jit(solution)/shard_map/ppermute | solution.py:50
  15.0 3.1 %collective-permute-start.6 = (bf16[64,896]{1,0:T(8,128)(2,1)S(1)}, bf16[64,896]{1,0:T(8,128)(2,1)S(1)}, u32[]{:S(2)}, u32[]{:S(2)}) collective-permute-start(bf16[64,896]{1,0:T(8,128)(2,1)S(1)} %get-tuple-element.50), channel_id=1, source_target_pairs={{0,1},{1,0},{2,3},{3,2},{4,5},{5,4},{6,7},{7,6},{8,9},{9,8},{10,11... | collective-permute-start | bytes 344072 | tf_op jit(solution)/shard_map/ppermute | solution.py:50
  15.1 3.0 %collective-permute-start.3 = (bf16[64,768]{1,0:T(8,128)(2,1)S(1)}, bf16[64,768]{1,0:T(8,128)(2,1)S(1)}, u32[]{:S(2)}, u32[]{:S(2)}) collective-permute-start(bf16[64,768]{1,0:T(8,128)(2,1)S(1)} %get-tuple-element.47), channel_id=1, source_target_pairs={{0,1},{1,0},{2,3},{3,2},{4,5},{5,4},{6,7},{7,6},{8,9},{9,8},{10,11... | collective-permute-start | bytes 294920 | tf_op jit(solution)/shard_map/ppermute | solution.py:50
  15.6 2.5 %collective-permute-start.4 = (bf16[64,768]{1,0:T(8,128)(2,1)S(1)}, bf16[64,768]{1,0:T(8,128)(2,1)S(1)}, u32[]{:S(2)}, u32[]{:S(2)}) collective-permute-start(bf16[64,768]{1,0:T(8,128)(2,1)S(1)} %get-tuple-element.48), channel_id=1, source_target_pairs={{0,1},{1,0},{2,3},{3,2},{4,5},{5,4},{6,7},{7,6},{8,9},{9,8},{10,11... | collective-permute-start | bytes 294920 | tf_op jit(solution)/shard_map/ppermute | solution.py:50
  15.6 2.4 %collective-permute-start.5 = (bf16[64,768]{1,0:T(8,128)(2,1)S(1)}, bf16[64,768]{1,0:T(8,128)(2,1)S(1)}, u32[]{:S(2)}, u32[]{:S(2)}) collective-permute-start(bf16[64,768]{1,0:T(8,128)(2,1)S(1)} %get-tuple-element.49), channel_id=1, source_target_pairs={{0,1},{1,0},{2,3},{3,2},{4,5},{5,4},{6,7},{7,6},{8,9},{9,8},{10,11... | collective-permute-start | bytes 294920 | tf_op jit(solution)/shard_map/ppermute | solution.py:50
  16.4 6.6 %collective-permute-start.8 = (bf16[128,768]{1,0:T(8,128)(2,1)S(1)}, bf16[128,768]{1,0:T(8,128)(2,1)S(1)}, u32[]{:S(2)}, u32[]{:S(2)}) collective-permute-start(bf16[128,768]{1,0:T(8,128)(2,1)S(1)} %collective-permute-done.2.refs_0_), channel_id=1, source_target_pairs={{0,4},{4,0},{8,12},{12,8},{1,5},{5,1},{9,13},{13,9},{2,6},{6,2},{1... | collective-permute-start | bytes 589832 | tf_op jit(solution)/shard_map/ppermute | solution.py:50
  18.2 10.7 %collective-permute-start.7 = (bf16[64,3200]{1,0:T(8,128)(2,1)S(1)}, bf16[64,3200]{1,0:T(8,128)(2,1)S(1)}, u32[]{:S(2)}, u32[]{:S(2)}) collective-permute-start(bf16[64,3200]{1,0:T(8,128)(2,1)S(1)} %add_cores.4.refs_6_.refs_0_), channel_id=1, source_target_pairs={{0,2},{2,0},{1,3},{3,1},{4,6},{6,4},{5,7},{7,5},{8,10},{10,8},{9,1... | collective-permute-start | bytes 1228808 | tf_op jit(solution)/shard_map/ppermute | solution.py:50
  19.8 1.9 %collective-permute-start.11 = (bf16[64,1152]{1,0:T(8,128)(2,1)S(1)}, bf16[64,1152]{1,0:T(8,128)(2,1)S(1)}, u32[]{:S(2)}, u32[]{:S(2)}) collective-permute-start(bf16[64,1152]{1,0:T(8,128)(2,1)S(1)} %get-tuple-element.57), channel_id=1, source_target_pairs={{0,1},{1,0},{2,3},{3,2},{4,5},{5,4},{6,7},{7,6},{8,9},{9,8},{10,11... | collective-permute-start | bytes 442376 | tf_op jit(solution)/shard_map/ppermute | solution.py:50
  19.8 1.6 %collective-permute-start.9 = (bf16[64,1024]{1,0:T(8,128)(2,1)S(1)}, bf16[64,1024]{1,0:T(8,128)(2,1)S(1)}, u32[]{:S(2)}, u32[]{:S(2)}) collective-permute-start(bf16[64,1024]{1,0:T(8,128)(2,1)S(1)} %get-tuple-element.55), channel_id=1, source_target_pairs={{0,1},{1,0},{2,3},{3,2},{4,5},{5,4},{6,7},{7,6},{8,9},{9,8},{10,11... | collective-permute-start | bytes 393224 | tf_op jit(solution)/shard_map/ppermute | solution.py:50
  23.9 1.8 %collective-permute-start.13 = (bf16[64,1664]{1,0:T(8,128)(2,1)S(1)}, bf16[64,1664]{1,0:T(8,128)(2,1)S(1)}, u32[]{:S(2)}, u32[]{:S(2)}) collective-permute-start(bf16[64,1664]{1,0:T(8,128)(2,1)S(1)} %get-tuple-element.61), channel_id=1, source_target_pairs={{0,1},{1,0},{2,3},{3,2},{4,5},{5,4},{6,7},{7,6},{8,9},{9,8},{10,11... | collective-permute-start | bytes 638984 | tf_op jit(solution)/shard_map/ppermute | solution.py:50
  24.0 1.7 %collective-permute-start.12 = (bf16[64,1536]{1,0:T(8,128)(2,1)S(1)}, bf16[64,1536]{1,0:T(8,128)(2,1)S(1)}, u32[]{:S(2)}, u32[]{:S(2)}) collective-permute-start(bf16[64,1536]{1,0:T(8,128)(2,1)S(1)} %get-tuple-element.60), channel_id=1, source_target_pairs={{0,1},{1,0},{2,3},{3,2},{4,5},{5,4},{6,7},{7,6},{8,9},{9,8},{10,11... | collective-permute-start | bytes 589832 | tf_op jit(solution)/shard_map/ppermute | solution.py:50
  24.5 6.9 %collective-permute-start.16 = (bf16[128,768]{1,0:T(8,128)(2,1)S(1)}, bf16[128,768]{1,0:T(8,128)(2,1)S(1)}, u32[]{:S(2)}, u32[]{:S(2)}) collective-permute-start(bf16[128,768]{1,0:T(8,128)(2,1)S(1)} %copy-done.4), channel_id=1, source_target_pairs={{0,4},{4,0},{8,12},{12,8},{1,5},{5,1},{9,13},{13,9},{2,6},{6,2},{1... | collective-permute-start | bytes 589832 | tf_op jit(solution)/shard_map/ppermute | solution.py:50
  32.3 3.6 %collective-permute-start.20 = (bf16[64,1664]{1,0:T(8,128)(2,1)S(1)}, bf16[64,1664]{1,0:T(8,128)(2,1)S(1)}, u32[]{:S(2)}, u32[]{:S(2)}) collective-permute-start(bf16[64,1664]{1,0:T(8,128)(2,1)S(1)} %get-tuple-element.67), channel_id=1, source_target_pairs={{0,1},{1,0},{2,3},{3,2},{4,5},{5,4},{6,7},{7,6},{8,9},{9,8},{10,11... | collective-permute-start | bytes 638984 | tf_op jit(solution)/shard_map/ppermute | solution.py:50
  32.3 2.3 %collective-permute-start.15 = (bf16[64,1536]{1,0:T(8,128)(2,1)S(1)}, bf16[64,1536]{1,0:T(8,128)(2,1)S(1)}, u32[]{:S(2)}, u32[]{:S(2)}) collective-permute-start(bf16[64,1536]{1,0:T(8,128)(2,1)S(1)} %get-tuple-element.63.refs_4_.refs_1_), channel_id=1, source_target_pairs={{0,1},{1,0},{2,3},{3,2},{4,5},{5,4},{6,7},{7,6},{8,9},{9,8},{10,11... | collective-permute-start | bytes 589832 | tf_op jit(solution)/shard_map/ppermute | solution.py:50
  32.8 1.8 %collective-permute-start.14 = (bf16[64,1536]{1,0:T(8,128)(2,1)S(1)}, bf16[64,1536]{1,0:T(8,128)(2,1)S(1)}, u32[]{:S(2)}, u32[]{:S(2)}) collective-permute-start(bf16[64,1536]{1,0:T(8,128)(2,1)S(1)} %get-tuple-element.62.refs_3_.refs_0_), channel_id=1, source_target_pairs={{0,1},{1,0},{2,3},{3,2},{4,5},{5,4},{6,7},{7,6},{8,9},{9,8},{10,11... | collective-permute-start | bytes 589832 | tf_op jit(solution)/shard_map/ppermute | solution.py:50
  32.9 12.3 %collective-permute-start.18 = (bf16[64,3200]{1,0:T(8,128)(2,1)S(1)}, bf16[64,3200]{1,0:T(8,128)(2,1)S(1)}, u32[]{:S(2)}, u32[]{:S(2)}) collective-permute-start(bf16[64,3200]{1,0:T(8,128)(2,1)S(1)} %add_cores.6.refs_3_.refs_0_), channel_id=1, source_target_pairs={{0,2},{2,0},{1,3},{3,1},{4,6},{6,4},{5,7},{7,5},{8,10},{10,8},{9,1... | collective-permute-start | bytes 1228808 | tf_op jit(solution)/shard_map/ppermute | solution.py:50
  34.5 1.4 %collective-permute-start.19 = (bf16[64,1536]{1,0:T(8,128)(2,1)S(1)}, bf16[64,1536]{1,0:T(8,128)(2,1)S(1)}, u32[]{:S(2)}, u32[]{:S(2)}) collective-permute-start(bf16[64,1536]{1,0:T(8,128)(2,1)S(1)} %get-tuple-element.66), channel_id=1, source_target_pairs={{0,1},{1,0},{2,3},{3,2},{4,5},{5,4},{6,7},{7,6},{8,9},{9,8},{10,11... | collective-permute-start | bytes 589832 | tf_op jit(solution)/shard_map/ppermute | solution.py:50
  36.0 18.7 %collective-permute-start.24 = (bf16[64,3200]{1,0:T(8,128)(2,1)S(1)}, bf16[64,3200]{1,0:T(8,128)(2,1)S(1)}, u32[]{:S(2)}, u32[]{:S(2)}) collective-permute-start(bf16[64,3200]{1,0:T(8,128)(2,1)S(1)} %add_cores.7.refs_3_.refs_0_), channel_id=1, source_target_pairs={{0,2},{2,0},{1,3},{3,1},{4,6},{6,4},{5,7},{7,5},{8,10},{10,8},{9,1... | collective-permute-start | bytes 1228808 | tf_op jit(solution)/shard_map/ppermute | solution.py:50
  37.1 13.2 %collective-permute-start.17 = (bf16[128,896]{1,0:T(8,128)(2,1)S(1)}, bf16[128,896]{1,0:T(8,128)(2,1)S(1)}, u32[]{:S(2)}, u32[]{:S(2)}) collective-permute-start(bf16[128,896]{1,0:T(8,128)(2,1)S(1)} %down_rows.3.refs_4_), channel_id=1, source_target_pairs={{0,8},{4,12},{8,0},{12,4},{1,9},{5,13},{9,1},{13,5},{2,10},{6,14},... | collective-permute-start | bytes 688136 | tf_op jit(solution)/shard_map/ppermute | solution.py:50
  46.0 4.4 %collective-permute-start.22 = (bf16[64,1536]{1,0:T(8,128)(2,1)S(1)}, bf16[64,1536]{1,0:T(8,128)(2,1)S(1)}, u32[]{:S(2)}, u32[]{:S(2)}) collective-permute-start(bf16[64,1536]{1,0:T(8,128)(2,1)S(1)} %get-tuple-element.69.refs_4_.refs_6_), channel_id=1, source_target_pairs={{0,1},{1,0},{2,3},{3,2},{4,5},{5,4},{6,7},{7,6},{8,9},{9,8},{10,11... | collective-permute-start | bytes 589832 | tf_op jit(solution)/shard_map/ppermute | solution.py:50
  46.1 4.3 %collective-permute-start.21 = (bf16[64,1536]{1,0:T(8,128)(2,1)S(1)}, bf16[64,1536]{1,0:T(8,128)(2,1)S(1)}, u32[]{:S(2)}, u32[]{:S(2)}) collective-permute-start(bf16[64,1536]{1,0:T(8,128)(2,1)S(1)} %get-tuple-element.68.refs_0_.refs_3_.refs_5_), channel_id=1, source_target_pairs={{0,1},{1,0},{2,3},{3,2},{4,5},{5,4},{6,7},{7,6},{8,9},{9,8},{10,11... | collective-permute-start | bytes 589832 | tf_op jit(solution)/shard_map/ppermute | solution.py:50
  46.6 15.7 %collective-permute-start.28 = (bf16[64,3200]{1,0:T(8,128)(2,1)S(1)}, bf16[64,3200]{1,0:T(8,128)(2,1)S(1)}, u32[]{:S(2)}, u32[]{:S(2)}) collective-permute-start(bf16[64,3200]{1,0:T(8,128)(2,1)S(1)} %add_cores.5.refs_3_.refs_0_), channel_id=1, source_target_pairs={{0,2},{2,0},{1,3},{3,1},{4,6},{6,4},{5,7},{7,5},{8,10},{10,8},{9,1... | collective-permute-start | bytes 1228808 | tf_op jit(solution)/shard_map/ppermute | solution.py:50
  51.4 9.2 %collective-permute-start.23 = (bf16[128,896]{1,0:T(8,128)(2,1)S(1)}, bf16[128,896]{1,0:T(8,128)(2,1)S(1)}, u32[]{:S(2)}, u32[]{:S(2)}) collective-permute-start(bf16[128,896]{1,0:T(8,128)(2,1)S(1)} %down_rows.4.refs_3_), channel_id=1, source_target_pairs={{0,12},{4,8},{8,4},{12,0},{1,13},{5,9},{9,5},{13,1},{2,14},{6,10},... | collective-permute-start | bytes 688136 | tf_op jit(solution)/shard_map/ppermute | solution.py:50
  55.5 1.5 %collective-permute-start.25 = (bf16[64,1536]{1,0:T(8,128)(2,1)S(1)}, bf16[64,1536]{1,0:T(8,128)(2,1)S(1)}, u32[]{:S(2)}, u32[]{:S(2)}) collective-permute-start(bf16[64,1536]{1,0:T(8,128)(2,1)S(1)} %get-tuple-element.70.refs_3_.refs_7_.refs_10_), channel_id=1, source_target_pairs={{0,1},{1,0},{2,3},{3,2},{4,5},{5,4},{6,7},{7,6},{8,9},{9,8},{10,11... | collective-permute-start | bytes 589832 | tf_op jit(solution)/shard_map/ppermute | solution.py:50
  55.6 1.7 %collective-permute-start.26 = (bf16[64,1536]{1,0:T(8,128)(2,1)S(1)}, bf16[64,1536]{1,0:T(8,128)(2,1)S(1)}, u32[]{:S(2)}, u32[]{:S(2)}) collective-permute-start(bf16[64,1536]{1,0:T(8,128)(2,1)S(1)} %get-tuple-element.71.refs_4_.refs_11_), channel_id=1, source_target_pairs={{0,1},{1,0},{2,3},{3,2},{4,5},{5,4},{6,7},{7,6},{8,9},{9,8},{10,11... | collective-permute-start | bytes 589832 | tf_op jit(solution)/shard_map/ppermute | solution.py:50
  58.3 7.8 %collective-permute-start.27 = (bf16[128,896]{1,0:T(8,128)(2,1)S(1)}, bf16[128,896]{1,0:T(8,128)(2,1)S(1)}, u32[]{:S(2)}, u32[]{:S(2)}) collective-permute-start(bf16[128,896]{1,0:T(8,128)(2,1)S(1)} %down_rows.5.refs_0_), channel_id=1, source_target_pairs={{0,4},{4,0},{8,12},{12,8},{1,5},{5,1},{9,13},{13,9},{2,6},{6,2},{1... | collective-permute-start | bytes 688136 | tf_op jit(solution)/shard_map/ppermute | solution.py:50
  63.1 1.5 %collective-permute-start.29 = (bf16[64,1536]{1,0:T(8,128)(2,1)S(1)}, bf16[64,1536]{1,0:T(8,128)(2,1)S(1)}, u32[]{:S(2)}, u32[]{:S(2)}) collective-permute-start(bf16[64,1536]{1,0:T(8,128)(2,1)S(1)} %get-tuple-element.72.refs_6_.refs_10_.refs_7_.refs_15_), channel_id=1, source_target_pairs={{0,1},{1,0},{2,3},{3,2},{4,5},{5,4},{6,7},{7,6},{8,9},{9,8},{10,11... | collective-permute-start | bytes 589832 | tf_op jit(solution)/shard_map/ppermute | solution.py:50
  63.2 1.7 %collective-permute-start.30 = (bf16[64,1536]{1,0:T(8,128)(2,1)S(1)}, bf16[64,1536]{1,0:T(8,128)(2,1)S(1)}, u32[]{:S(2)}, u32[]{:S(2)}) collective-permute-start(bf16[64,1536]{1,0:T(8,128)(2,1)S(1)} %get-tuple-element.73.refs_7_.refs_8_.refs_16_), channel_id=1, source_target_pairs={{0,1},{1,0},{2,3},{3,2},{4,5},{5,4},{6,7},{7,6},{8,9},{9,8},{10,11... | collective-permute-start | bytes 589832 | tf_op jit(solution)/shard_map/ppermute | solution.py:50
  66.8 7.6 %collective-permute-start.33 = (bf16[64,768]{1,0:T(8,128)(2,1)S(1)}, bf16[64,768]{1,0:T(8,128)(2,1)S(1)}, u32[]{:S(2)}, u32[]{:S(2)}) collective-permute-start(bf16[64,768]{1,0:T(8,128)(2,1)S(1)} %get-tuple-element.76.refs_0_), channel_id=1, source_target_pairs={{0,12},{4,8},{8,4},{12,0},{1,13},{5,9},{9,5},{13,1},{2,14},{6,10},... | collective-permute-start | bytes 294920 | tf_op jit(solution)/shard_map/ppermute | solution.py:50
  70.0 8.4 %collective-permute-start.32 = (bf16[64,768]{1,0:T(8,128)(2,1)S(1)}, bf16[64,768]{1,0:T(8,128)(2,1)S(1)}, u32[]{:S(2)}, u32[]{:S(2)}) collective-permute-start(bf16[64,768]{1,0:T(8,128)(2,1)S(1)} %get-tuple-element.76.refs_0_), channel_id=1, source_target_pairs={{0,8},{4,12},{8,0},{12,4},{1,9},{5,13},{9,1},{13,5},{2,10},{6,14},... | collective-permute-start | bytes 294920 | tf_op jit(solution)/shard_map/ppermute | solution.py:50
  70.0 8.4 %collective-permute-start.31 = (bf16[64,768]{1,0:T(8,128)(2,1)S(1)}, bf16[64,768]{1,0:T(8,128)(2,1)S(1)}, u32[]{:S(2)}, u32[]{:S(2)}) collective-permute-start(bf16[64,768]{1,0:T(8,128)(2,1)S(1)} %get-tuple-element.76.refs_0_), channel_id=1, source_target_pairs={{0,4},{4,0},{8,12},{12,8},{1,5},{5,1},{9,13},{13,9},{2,6},{6,2},{1... | collective-permute-start | bytes 294920 | tf_op jit(solution)/shard_map/ppermute | solution.py:50
  (9 other events, 68.5 us)

commit v5 on v4

--- a/solution.py
+++ b/solution.py
@@ -312,7 +312,8 @@
 
 
 def first_gradient_rows(count, *refs):
-    *blocks, out = refs
+    *blocks, out, done = refs
+    done[...] = jnp.zeros_like(done)
     rank = out.shape[0]
     stride = 2 * count + 1
     places = range(0, len(blocks), stride)
@@ -333,7 +334,7 @@
 
 
 def second_gradient_part(terms, first, cot, mod, *refs):
-    *arrays, out, low_total, low = refs
+    *arrays, upper, lower, low_total, low = refs
     received, parts = arrays[:terms], arrays[terms:]
     rank, features = first.shape[0], cot.shape[1]
     back_rows = (mod[2:3, :] * cot[...].astype(f32)).astype(bf16)
@@ -342,7 +343,9 @@
     for value in received:
         sums = sums + value[:, features : features + rank].astype(f32)
     low_total[...] = sums
-    out[...] = (adapter_scale * split_dot(dot_rows, sums, back_rows)).astype(bf16)
+    product = (adapter_scale * split_dot(dot_rows, sums, back_rows)).astype(bf16)
+    upper[...] = product[: rank // 2]
+    lower[...] = product[rank // 2 :]
 
 
 def update_rows(terms, weight, low_total, factor, mod, *refs):
@@ -358,10 +361,14 @@
     out[...] = (mod[2:3, :] * base).astype(bf16)
 
 
-def add_four(own, one, two, three, out):
-    out[...] = (own[...].astype(f32) + one[...].astype(f32)) + (
-        two[...].astype(f32) + three[...].astype(f32)
-    )
+def add_pair(left, right, out):
+    out[...] = (left[...].astype(f32) + right[...].astype(f32)).astype(out.dtype)
+
+
+def add_halves(upper, upper_other, lower, lower_other, out):
+    middle = upper.shape[0]
+    out[:middle] = upper[...].astype(f32) + upper_other[...].astype(f32)
+    out[middle:] = lower[...].astype(f32) + lower_other[...].astype(f32)
 
 
 def per_device(
@@ -504,9 +511,9 @@
     pairs.append(own_pair)
     after = activate(after)
     own = activated[last]
-    contribution, low_total = call(
+    *contribution, low_total = call(
         named(second_gradient_part, last),
-        [((rank, features), bf16), ((rows, rank), f32)],
+        [*(2 * [((rank // 2, features), bf16)]), ((rows, rank), f32)],
         [first, cotangent, mod, *received, *own],
         after,
         scratch=[pltpu.VMEM((rows, rank), f32)],
@@ -520,22 +527,21 @@
     gathered = []
     for parts, rows_of in zip(activated, received + [low_back]):
         gathered += [*parts, rows_of]
-    (first_gradient,) = call(
+    first_gradient, done = call(
         named(first_gradient_rows, len(cut(GELU_PIECES))),
-        [((rank, hidden), f32)],
+        [((rank, hidden), f32), ((8, LANES), f32)],
         gathered,
         [low_total],
     )
     if loop_size == 4:
-        terms = [swap(contribution, "loop", k) for k in (1, 2, 3)]
-        (second_gradient,) = call(
-            add_four,
-            [((rank, features), f32)],
-            [contribution, *terms],
-            [low_total],
-        )
+        operands, after = [], [done]
+        for half in contribution:
+            after = call(add_pair, [(half.shape, bf16)], [half, swap(half, "loop", 1)], after)
+            operands += [after[0], swap(after[0], "loop", 2)]
+        (second_gradient,) = call(add_halves, [((rank, features), f32)], operands)
     else:
-        second_gradient = lax.psum(contribution, "loop").astype(f32)
+        halves = [lax.psum(half, "loop") for half in contribution]
+        second_gradient = jnp.concatenate(halves, axis=0).astype(f32)
     return (block_update, first_gradient.T, second_gradient)
 
 

time: 79.3 us -> 78.9 us (level)
  waiting for transfers between devices: 30 us -> 28.3 us
  starting transfers between devices: 29.4 us -> 30.6 us
    ppermute x34 -> x35, waiting for transfers between devices: 30 us -> 28.3 us  [swap(): return lax.ppermute(value, axis, [(i, i ^ distance) for i in range(size)])]
    ppermute x34 -> x35, starting transfers between devices: 29.4 us -> 30.6 us  [swap(): return lax.ppermute(value, axis, [(i, i ^ distance) for i in range(size)])]
    pallas_call x25 -> x27, Pallas kernels: 17.2 us -> 17.3 us  [call(): pl.pallas_call(kernel, out_shape=[jax.ShapeDtypeStruct(shape, kind) for s...]
  transfers between devices with their start and end apart: 34 -> 35, of which waited for: 20 -> 22; matrix products, arithmetic and copies ran while one was open for 0% -> 0% of each run, Pallas kernels for 19% -> 19%
where the time goes in v5:
time: 78.9 us; the launch traced here: 78.7 us
  starting transfers between devices  30.6 us (39%)
  waiting for transfers between devices  28.3 us (36%)
  Pallas kernels  17.3 us (22%)
  between operations  1.59 us (2%)
  local copies, waits for them, and re-layouts  0.91 us (1%)
    ppermute x35, starting transfers between devices, swap(): return lax.ppermute(value, axis, [(i, i ^ distance) for i in range(size)])  30.6 us
    ppermute x35, waiting for transfers between devices, swap(): return lax.ppermute(value, axis, [(i, i ^ distance) for i in range(size)])  28.3 us
    pallas_call x27, Pallas kernels, call(): pl.pallas_call(kernel, out_shape=[jax.ShapeDtypeStruct(shape, kind) for s...  17.3 us
  transfers between devices with their start and end apart: 35, of which 22 were waited for; matrix products, arithmetic and copies ran while one was open for 0% of the time, Pallas kernels for 19%

profile of v5, /device:TPU:0, one launch (start us, length us, event | category | flops | bytes accessed | tf_op | source)
XLA Modules:
  0.0 78.7 jit_solution(4353350756918729461)
XLA Ops:
  0.6 4.1 %collective-permute-start.2 = (bf16[128,768]{1,0:T(8,128)(2,1)}, bf16[128,768]{1,0:T(8,128)(2,1)S(1)}, u32[]{:S(2)}, u32[]{:S(2)}) collective-permute-start(bf16[128,768]{1,0:T(8,128)(2,1)} %refs_1_.2), channel_id=1, source_target_pairs={{0,8},{4,12},{8,0},{12,4},{1,9},{5,13},{9,1},{13,5},{2,10},{6,14},... | collective-permute-start | bytes 589832 | tf_op jit(solution)/shard_map/ppermute | solution.py:50
  6.3 3.2 %own_rows.1 = (bf16[64,1024]{1,0:T(8,128)(2,1)S(1)}, bf16[64,1024]{1,0:T(8,128)(2,1)S(1)}, bf16[64,1152]{1,0:T(8,128)(2,1)S(1)}, bf16[64,1024]{1,0:T(8,128)(2,1)...) custom-call(s32[1]{0:T(128)S(6)} %copy.11.refs_0_, ...), custom_call_target="tpu_custom_call" | custom-call | flops 1024 | bytes 1024 | tf_op jit(solution)/shard_map/own_rows/pallas_call | solution.py:74
  9.5 1.3 %collective-permute-done.refs_1_ = f32[248,128]{1,0:T(8,128)S(1)} collective-permute-done((f32[248,128]{1,0:T(8,128)S(1)}, f32[248,128]{1,0:T(8,128)S(1)}, u32[]{:S(2)}, u32[]{:S(2)}) %collective-permute-start) | collective-permute-done | bytes 127008 | tf_op jit(solution)/shard_map/ppermute | solution.py:50
  10.9 1.6 %collective-permute-start.1 = (f32[248,128]{1,0:T(8,128)S(1)}, f32[248,128]{1,0:T(8,128)S(1)}, u32[]{:S(2)}, u32[]{:S(2)}) collective-permute-start(f32[248,128]{1,0:T(8,128)S(1)} %add_packed.1.refs_0_.refs_3_), channel_id=1, source_target_pairs={{0,2},{2,0},{1,3},{3,1},{4,6},{6,4},{5,7},{7,5},{8,10},{10,8},{9,1... | collective-permute-start | bytes 380936 | tf_op jit(solution)/shard_map/ppermute | solution.py:50
  12.4 1.6 %collective-permute-done.2.refs_0_ = bf16[128,768]{1,0:T(8,128)(2,1)S(1)} collective-permute-done((bf16[128,768]{1,0:T(8,128)(2,1)}, bf16[128,768]{1,0:T(8,128)(2,1)S(1)}, u32[]{:S(2)}, u32[]{:S(2)}) %collective-permute-start.2) | collective-permute-done | bytes 196640 | tf_op jit(solution)/shard_map/ppermute | solution.py:50
  16.4 1.6 %collective-permute-start.8 = (bf16[128,768]{1,0:T(8,128)(2,1)S(1)}, bf16[128,768]{1,0:T(8,128)(2,1)S(1)}, u32[]{:S(2)}, u32[]{:S(2)}) collective-permute-start(bf16[128,768]{1,0:T(8,128)(2,1)S(1)} %collective-permute-done.2.refs_0_), channel_id=1, source_target_pairs={{0,4},{4,0},{8,12},{12,8},{1,5},{5,1},{9,13},{13,9},{2,6},{6,2},{1... | collective-permute-start | bytes 589832 | tf_op jit(solution)/shard_map/ppermute | solution.py:50
  18.2 1.6 %collective-permute-start.7 = (bf16[64,3200]{1,0:T(8,128)(2,1)S(1)}, bf16[64,3200]{1,0:T(8,128)(2,1)S(1)}, u32[]{:S(2)}, u32[]{:S(2)}) collective-permute-start(bf16[64,3200]{1,0:T(8,128)(2,1)S(1)} %add_cores.4.refs_6_.refs_0_), channel_id=1, source_target_pairs={{0,2},{2,0},{1,3},{3,1},{4,6},{6,4},{5,7},{7,5},{8,10},{10,8},{9,1... | collective-permute-start | bytes 1228808 | tf_op jit(solution)/shard_map/ppermute | solution.py:50
  20.3 1.0 %collective-permute-done.9.refs_3_ = bf16[64,1024]{1,0:T(8,128)(2,1)S(1)} collective-permute-done((bf16[64,1024]{1,0:T(8,128)(2,1)S(1)}, bf16[64,1024]{1,0:T(8,128)(2,1)S(1)}, u32[]{:S(2)}, u32[]{:S(2)}) %collective-permute-start.9) | collective-permute-done | bytes 131104 | tf_op jit(solution)/shard_map/ppermute | solution.py:50
  21.7 1.2 %collective-permute-done.8.refs_0_ = bf16[128,768]{1,0:T(8,128)(2,1)S(1)} collective-permute-done((bf16[128,768]{1,0:T(8,128)(2,1)S(1)}, bf16[128,768]{1,0:T(8,128)(2,1)S(1)}, u32[]{:S(2)}, u32[]{:S(2)}) %collective-permute-start.8) | collective-permute-done | bytes 196640 | tf_op jit(solution)/shard_map/ppermute | solution.py:50
  24.5 1.1 %collective-permute-start.16 = (bf16[128,768]{1,0:T(8,128)(2,1)S(1)}, bf16[128,768]{1,0:T(8,128)(2,1)S(1)}, u32[]{:S(2)}, u32[]{:S(2)}) collective-permute-start(bf16[128,768]{1,0:T(8,128)(2,1)S(1)} %copy-done.4), channel_id=1, source_target_pairs={{0,4},{4,0},{8,12},{12,8},{1,5},{5,1},{9,13},{13,9},{2,6},{6,2},{1... | collective-permute-start | bytes 589832 | tf_op jit(solution)/shard_map/ppermute | solution.py:50
  25.8 3.1 %collective-permute-done.7.refs_1_ = bf16[64,3200]{1,0:T(8,128)(2,1)S(1)} collective-permute-done((bf16[64,3200]{1,0:T(8,128)(2,1)S(1)}, bf16[64,3200]{1,0:T(8,128)(2,1)S(1)}, u32[]{:S(2)}, u32[]{:S(2)}) %collective-permute-start.7) | collective-permute-done | bytes 409632 | tf_op jit(solution)/shard_map/ppermute | solution.py:50
  29.8 1.6 %collective-permute-done.16.refs_0_ = bf16[128,768]{1,0:T(8,128)(2,1)S(1)} collective-permute-done((bf16[128,768]{1,0:T(8,128)(2,1)S(1)}, bf16[128,768]{1,0:T(8,128)(2,1)S(1)}, u32[]{:S(2)}, u32[]{:S(2)}) %collective-permute-start.16) | collective-permute-done | bytes 196640 | tf_op jit(solution)/shard_map/ppermute | solution.py:50
  32.9 1.5 %collective-permute-start.18 = (bf16[64,3200]{1,0:T(8,128)(2,1)S(1)}, bf16[64,3200]{1,0:T(8,128)(2,1)S(1)}, u32[]{:S(2)}, u32[]{:S(2)}) collective-permute-start(bf16[64,3200]{1,0:T(8,128)(2,1)S(1)} %add_cores.6.refs_3_.refs_0_), channel_id=1, source_target_pairs={{0,2},{2,0},{1,3},{3,1},{4,6},{6,4},{5,7},{7,5},{8,10},{10,8},{9,1... | collective-permute-start | bytes 1228808 | tf_op jit(solution)/shard_map/ppermute | solution.py:50
  34.7 1.0 %down_rows.3.refs_4_ = bf16[128,896]{1,0:T(8,128)(2,1)S(1)} custom-call(bf16[3072,768]{1,0:T(8,128)(2,1)S(1)} %bitcast.4, bf16[64,12288]{1,0:T(8,128)(2,1)S(1)} %bitcast.5, bf16[128,128]{1,0:T(8,128)(2,1)S(1)} %get-tuple-element.45.refs_2_.refs_19_, bf16[64,1536]{1,0:T(8,128)(2,1)S(1)} %get-tuple-element.65.refs_3_.refs_0_, ...), custom_call_target="tpu_custom_call" | custom-call | flops 1024 | bytes 1024 | tf_op jit(solution)/shard_map/down_rows/pallas_call | solution.py:74
  36.0 1.1 %collective-permute-start.24 = (bf16[64,3200]{1,0:T(8,128)(2,1)S(1)}, bf16[64,3200]{1,0:T(8,128)(2,1)S(1)}, u32[]{:S(2)}, u32[]{:S(2)}) collective-permute-start(bf16[64,3200]{1,0:T(8,128)(2,1)S(1)} %add_cores.7.refs_3_.refs_0_), channel_id=1, source_target_pairs={{0,2},{2,0},{1,3},{3,1},{4,6},{6,4},{5,7},{7,5},{8,10},{10,8},{9,1... | collective-permute-start | bytes 1228808 | tf_op jit(solution)/shard_map/ppermute | solution.py:50
  37.1 2.3 %collective-permute-start.17 = (bf16[128,896]{1,0:T(8,128)(2,1)S(1)}, bf16[128,896]{1,0:T(8,128)(2,1)S(1)}, u32[]{:S(2)}, u32[]{:S(2)}) collective-permute-start(bf16[128,896]{1,0:T(8,128)(2,1)S(1)} %down_rows.3.refs_4_), channel_id=1, source_target_pairs={{0,8},{4,12},{8,0},{12,4},{1,9},{5,13},{9,1},{13,5},{2,10},{6,14},... | collective-permute-start | bytes 688136 | tf_op jit(solution)/shard_map/ppermute | solution.py:50
  39.4 5.8 %collective-permute-done.18.refs_1_ = bf16[64,3200]{1,0:T(8,128)(2,1)S(1)} collective-permute-done((bf16[64,3200]{1,0:T(8,128)(2,1)S(1)}, bf16[64,3200]{1,0:T(8,128)(2,1)S(1)}, u32[]{:S(2)}, u32[]{:S(2)}) %collective-permute-start.18) | collective-permute-done | bytes 409632 | tf_op jit(solution)/shard_map/ppermute | solution.py:50
  46.6 1.5 %collective-permute-start.28 = (bf16[64,3200]{1,0:T(8,128)(2,1)S(1)}, bf16[64,3200]{1,0:T(8,128)(2,1)S(1)}, u32[]{:S(2)}, u32[]{:S(2)}) collective-permute-start(bf16[64,3200]{1,0:T(8,128)(2,1)S(1)} %add_cores.5.refs_3_.refs_0_), channel_id=1, source_target_pairs={{0,2},{2,0},{1,3},{3,1},{4,6},{6,4},{5,7},{7,5},{8,10},{10,8},{9,1... | collective-permute-start | bytes 1228808 | tf_op jit(solution)/shard_map/ppermute | solution.py:50
  48.2 2.2 %collective-permute-done.17.refs_1_.refs_3_.refs_4_ = bf16[128,896]{1,0:T(8,128)(2,1)S(1)} collective-permute-done((bf16[128,896]{1,0:T(8,128)(2,1)S(1)}, bf16[128,896]{1,0:T(8,128)(2,1)S(1)}, u32[]{:S(2)}, u32[]{:S(2)}) %collective-permute-start.17) | collective-permute-done | bytes 229408 | tf_op jit(solution)/shard_map/ppermute | solution.py:50
  50.4 1.0 %down_rows.4.refs_3_ = bf16[128,896]{1,0:T(8,128)(2,1)S(1)} custom-call(bf16[3072,768]{1,0:T(8,128)(2,1)S(1)} %bitcast.4, bf16[64,12288]{1,0:T(8,128)(2,1)S(1)} %bitcast.6, bf16[128,128]{1,0:T(8,128)(2,1)S(1)} %get-tuple-element.45.refs_2_.refs_19_, bf16[64,1536]{1,0:T(8,128)(2,1)S(1)} %get-tuple-element.71.refs_0_.refs_3_.refs_5_, ...), custom_call_target="tpu_custom_call" | custom-call | flops 1024 | bytes 1024 | tf_op jit(solution)/shard_map/down_rows/pallas_call | solution.py:74
  51.4 3.3 %collective-permute-start.23 = (bf16[128,896]{1,0:T(8,128)(2,1)S(1)}, bf16[128,896]{1,0:T(8,128)(2,1)S(1)}, u32[]{:S(2)}, u32[]{:S(2)}) collective-permute-start(bf16[128,896]{1,0:T(8,128)(2,1)S(1)} %down_rows.4.refs_3_), channel_id=1, source_target_pairs={{0,12},{4,8},{8,4},{12,0},{1,13},{5,9},{9,5},{13,1},{2,14},{6,10},... | collective-permute-start | bytes 688136 | tf_op jit(solution)/shard_map/ppermute | solution.py:50
  57.3 1.0 %down_rows.5.refs_0_ = bf16[128,896]{1,0:T(8,128)(2,1)S(1)} custom-call(bf16[3072,768]{1,0:T(8,128)(2,1)S(1)} %bitcast.4, bf16[64,12288]{1,0:T(8,128)(2,1)S(1)} %bitcast.7, bf16[128,128]{1,0:T(8,128)(2,1)S(1)} %get-tuple-element.45.refs_2_.refs_19_, bf16[64,1536]{1,0:T(8,128)(2,1)S(1)} %get-tuple-element.73.refs_3_.refs_7_.refs_10_, ...), custom_call_target="tpu_custom_call" | custom-call | flops 1024 | bytes 1024 | tf_op jit(solution)/shard_map/down_rows/pallas_call | solution.py:74
  58.8 1.7 %collective-permute-done.23.refs_1_.refs_4_.refs_5_.refs_9_ = bf16[128,896]{1,0:T(8,128)(2,1)S(1)} collective-permute-done((bf16[128,896]{1,0:T(8,128)(2,1)S(1)}, bf16[128,896]{1,0:T(8,128)(2,1)S(1)}, u32[]{:S(2)}, u32[]{:S(2)}) %collective-permute-start.23) | collective-permute-done | bytes 229408 | tf_op jit(solution)/shard_map/ppermute | solution.py:50
  60.6 1.7 %collective-permute-done.28.refs_1_ = bf16[64,3200]{1,0:T(8,128)(2,1)S(1)} collective-permute-done((bf16[64,3200]{1,0:T(8,128)(2,1)S(1)}, bf16[64,3200]{1,0:T(8,128)(2,1)S(1)}, u32[]{:S(2)}, u32[]{:S(2)}) %collective-permute-start.28) | collective-permute-done | bytes 409632 | tf_op jit(solution)/shard_map/ppermute | solution.py:50
  63.7 0.9 %collective-permute-done.29.refs_8_.refs_9_.refs_17_ = bf16[64,1536]{1,0:T(8,128)(2,1)S(1)} collective-permute-done((bf16[64,1536]{1,0:T(8,128)(2,1)S(1)}, bf16[64,1536]{1,0:T(8,128)(2,1)S(1)}, u32[]{:S(2)}, u32[]{:S(2)}) %collective-permute-start.29) | collective-permute-done | bytes 196640 | tf_op jit(solution)/shard_map/ppermute | solution.py:50
  64.9 1.2 %collective-permute-done.27.refs_5_.refs_6_.refs_14_ = bf16[128,896]{1,0:T(8,128)(2,1)S(1)} collective-permute-done((bf16[128,896]{1,0:T(8,128)(2,1)S(1)}, bf16[128,896]{1,0:T(8,128)(2,1)S(1)}, u32[]{:S(2)}, u32[]{:S(2)}) %collective-permute-start.27) | collective-permute-done | bytes 229408 | tf_op jit(solution)/shard_map/ppermute | solution.py:50
  66.9 1.1 %collective-permute-start.31 = (bf16[32,768]{1,0:T(8,128)(2,1)S(1)}, bf16[32,768]{1,0:T(8,128)(2,1)S(1)}, u32[]{:S(2)}, u32[]{:S(2)}) collective-permute-start(bf16[32,768]{1,0:T(8,128)(2,1)S(1)} %get-tuple-element.80.refs_0_), channel_id=1, source_target_pairs={{0,4},{4,0},{8,12},{12,8},{1,5},{5,1},{9,13},{13,9},{2,6},{6,2},{1... | collective-permute-start | bytes 147464 | tf_op jit(solution)/shard_map/ppermute | solution.py:50
  67.9 1.0 %collective-permute-start.33 = (bf16[32,768]{1,0:T(8,128)(2,1)S(1)}, bf16[32,768]{1,0:T(8,128)(2,1)S(1)}, u32[]{:S(2)}, u32[]{:S(2)}) collective-permute-start(bf16[32,768]{1,0:T(8,128)(2,1)S(1)} %get-tuple-element.82.refs_0_), channel_id=1, source_target_pairs={{0,4},{4,0},{8,12},{12,8},{1,5},{5,1},{9,13},{13,9},{2,6},{6,2},{1... | collective-permute-start | bytes 147464 | tf_op jit(solution)/shard_map/ppermute | solution.py:50
  69.0 1.5 %first_gradient_rows.1 = (f32[64,3072]{1,0:T(8,128)}, f32[8,128]{1,0:T(8,128)S(1)}) custom-call(bf16[64,1536]{1,0:T(8,128)(2,1)S(1)} %get-tuple-element.65.refs_3_.refs_0_, bf16[64,1536]{1,0:T(8,128)(2,1)S(1)} %get-tuple-element.66.refs_4_.refs_1_, bf16[64,1536]{1,0:T(8,128)(2,1)S(1)} %collective-permute-done.14.refs_5_.refs_2_, ...), custom_call_target="tpu_custom_call" | custom-call | flops 1024 | bytes 1024 | tf_op jit(solution)/shard_map/first_gradient_rows/pallas_call | solution.py:74
  71.4 1.6 %collective-permute-start.32 = (bf16[32,768]{1,0:T(8,128)(2,1)S(1)}, bf16[32,768]{1,0:T(8,128)(2,1)S(1)}, u32[]{:S(2)}, u32[]{:S(2)}) collective-permute-start(bf16[32,768]{1,0:T(8,128)(2,1)S(1)} %add_pair.2.refs_2_.refs_0_), channel_id=1, source_target_pairs={{0,8},{4,12},{8,0},{12,4},{1,9},{5,13},{9,1},{13,5},{2,10},{6,14},... | collective-permute-start | bytes 147464 | tf_op jit(solution)/shard_map/ppermute | solution.py:50
  73.0 2.0 %collective-permute-start.34 = (bf16[32,768]{1,0:T(8,128)(2,1)S(1)}, bf16[32,768]{1,0:T(8,128)(2,1)S(1)}, u32[]{:S(2)}, u32[]{:S(2)}) collective-permute-start(bf16[32,768]{1,0:T(8,128)(2,1)S(1)} %add_pair.3.refs_2_), channel_id=1, source_target_pairs={{0,8},{4,12},{8,0},{12,4},{1,9},{5,13},{9,1},{13,5},{2,10},{6,14},... | collective-permute-start | bytes 147464 | tf_op jit(solution)/shard_map/ppermute | solution.py:50
  75.0 1.6 %update_rows.1 = bf16[128,768]{1,0:T(8,128)(2,1)} custom-call(bf16[3072,768]{1,0:T(8,128)(2,1)S(1)} %bitcast.4, f32[128,64]{1,0:T(8,128)S(1)} %get-tuple-element.77.refs_1_.refs_20_, bf16[64,768]{1,0:T(8,128)(2,1)S(1)} %get-tuple-element.78.refs_2_, f32[8,768]{1,0:T(8,128)S(1)} %get-tuple-element.43.refs_1_.refs_2_.refs_3_, ...), custom_call_target="tpu_custom_call" | custom-call | flops 1024 | bytes 1024 | tf_op jit(solution)/shard_map/update_rows/pallas_call | solution.py:74
  (80 shorter events, 19.0 us)
Async XLA Ops:
  0.6 13.4 %collective-permute-start.2 = (bf16[128,768]{1,0:T(8,128)(2,1)}, bf16[128,768]{1,0:T(8,128)(2,1)S(1)}, u32[]{:S(2)}, u32[]{:S(2)}) collective-permute-start(bf16[128,768]{1,0:T(8,128)(2,1)} %refs_1_.2), channel_id=1, source_target_pairs={{0,8},{4,12},{8,0},{12,4},{1,9},{5,13},{9,1},{13,5},{2,10},{6,14},... | collective-permute-start | bytes 589832 | tf_op jit(solution)/shard_map/ppermute | solution.py:50
  10.9 5.5 %collective-permute-start.1 = (f32[248,128]{1,0:T(8,128)S(1)}, f32[248,128]{1,0:T(8,128)S(1)}, u32[]{:S(2)}, u32[]{:S(2)}) collective-permute-start(f32[248,128]{1,0:T(8,128)S(1)} %add_packed.1.refs_0_.refs_3_), channel_id=1, source_target_pairs={{0,2},{2,0},{1,3},{3,1},{4,6},{6,4},{5,7},{7,5},{8,10},{10,8},{9,1... | collective-permute-start | bytes 380936 | tf_op jit(solution)/shard_map/ppermute | solution.py:50
  15.0 3.1 %collective-permute-start.6 = (bf16[64,896]{1,0:T(8,128)(2,1)S(1)}, bf16[64,896]{1,0:T(8,128)(2,1)S(1)}, u32[]{:S(2)}, u32[]{:S(2)}) collective-permute-start(bf16[64,896]{1,0:T(8,128)(2,1)S(1)} %get-tuple-element.53), channel_id=1, source_target_pairs={{0,1},{1,0},{2,3},{3,2},{4,5},{5,4},{6,7},{7,6},{8,9},{9,8},{10,11... | collective-permute-start | bytes 344072 | tf_op jit(solution)/shard_map/ppermute | solution.py:50
  15.1 3.0 %collective-permute-start.3 = (bf16[64,768]{1,0:T(8,128)(2,1)S(1)}, bf16[64,768]{1,0:T(8,128)(2,1)S(1)}, u32[]{:S(2)}, u32[]{:S(2)}) collective-permute-start(bf16[64,768]{1,0:T(8,128)(2,1)S(1)} %get-tuple-element.50), channel_id=1, source_target_pairs={{0,1},{1,0},{2,3},{3,2},{4,5},{5,4},{6,7},{7,6},{8,9},{9,8},{10,11... | collective-permute-start | bytes 294920 | tf_op jit(solution)/shard_map/ppermute | solution.py:50
  15.6 2.5 %collective-permute-start.4 = (bf16[64,768]{1,0:T(8,128)(2,1)S(1)}, bf16[64,768]{1,0:T(8,128)(2,1)S(1)}, u32[]{:S(2)}, u32[]{:S(2)}) collective-permute-start(bf16[64,768]{1,0:T(8,128)(2,1)S(1)} %get-tuple-element.51), channel_id=1, source_target_pairs={{0,1},{1,0},{2,3},{3,2},{4,5},{5,4},{6,7},{7,6},{8,9},{9,8},{10,11... | collective-permute-start | bytes 294920 | tf_op jit(solution)/shard_map/ppermute | solution.py:50
  15.6 2.4 %collective-permute-start.5 = (bf16[64,768]{1,0:T(8,128)(2,1)S(1)}, bf16[64,768]{1,0:T(8,128)(2,1)S(1)}, u32[]{:S(2)}, u32[]{:S(2)}) collective-permute-start(bf16[64,768]{1,0:T(8,128)(2,1)S(1)} %get-tuple-element.52), channel_id=1, source_target_pairs={{0,1},{1,0},{2,3},{3,2},{4,5},{5,4},{6,7},{7,6},{8,9},{9,8},{10,11... | collective-permute-start | bytes 294920 | tf_op jit(solution)/shard_map/ppermute | solution.py:50
  16.4 6.6 %collective-permute-start.8 = (bf16[128,768]{1,0:T(8,128)(2,1)S(1)}, bf16[128,768]{1,0:T(8,128)(2,1)S(1)}, u32[]{:S(2)}, u32[]{:S(2)}) collective-permute-start(bf16[128,768]{1,0:T(8,128)(2,1)S(1)} %collective-permute-done.2.refs_0_), channel_id=1, source_target_pairs={{0,4},{4,0},{8,12},{12,8},{1,5},{5,1},{9,13},{13,9},{2,6},{6,2},{1... | collective-permute-start | bytes 589832 | tf_op jit(solution)/shard_map/ppermute | solution.py:50
  18.2 10.7 %collective-permute-start.7 = (bf16[64,3200]{1,0:T(8,128)(2,1)S(1)}, bf16[64,3200]{1,0:T(8,128)(2,1)S(1)}, u32[]{:S(2)}, u32[]{:S(2)}) collective-permute-start(bf16[64,3200]{1,0:T(8,128)(2,1)S(1)} %add_cores.4.refs_6_.refs_0_), channel_id=1, source_target_pairs={{0,2},{2,0},{1,3},{3,1},{4,6},{6,4},{5,7},{7,5},{8,10},{10,8},{9,1... | collective-permute-start | bytes 1228808 | tf_op jit(solution)/shard_map/ppermute | solution.py:50
  19.8 1.9 %collective-permute-start.11 = (bf16[64,1152]{1,0:T(8,128)(2,1)S(1)}, bf16[64,1152]{1,0:T(8,128)(2,1)S(1)}, u32[]{:S(2)}, u32[]{:S(2)}) collective-permute-start(bf16[64,1152]{1,0:T(8,128)(2,1)S(1)} %get-tuple-element.60), channel_id=1, source_target_pairs={{0,1},{1,0},{2,3},{3,2},{4,5},{5,4},{6,7},{7,6},{8,9},{9,8},{10,11... | collective-permute-start | bytes 442376 | tf_op jit(solution)/shard_map/ppermute | solution.py:50
  19.8 1.6 %collective-permute-start.9 = (bf16[64,1024]{1,0:T(8,128)(2,1)S(1)}, bf16[64,1024]{1,0:T(8,128)(2,1)S(1)}, u32[]{:S(2)}, u32[]{:S(2)}) collective-permute-start(bf16[64,1024]{1,0:T(8,128)(2,1)S(1)} %get-tuple-element.58), channel_id=1, source_target_pairs={{0,1},{1,0},{2,3},{3,2},{4,5},{5,4},{6,7},{7,6},{8,9},{9,8},{10,11... | collective-permute-start | bytes 393224 | tf_op jit(solution)/shard_map/ppermute | solution.py:50
  23.9 1.8 %collective-permute-start.13 = (bf16[64,1664]{1,0:T(8,128)(2,1)S(1)}, bf16[64,1664]{1,0:T(8,128)(2,1)S(1)}, u32[]{:S(2)}, u32[]{:S(2)}) collective-permute-start(bf16[64,1664]{1,0:T(8,128)(2,1)S(1)} %get-tuple-element.64), channel_id=1, source_target_pairs={{0,1},{1,0},{2,3},{3,2},{4,5},{5,4},{6,7},{7,6},{8,9},{9,8},{10,11... | collective-permute-start | bytes 638984 | tf_op jit(solution)/shard_map/ppermute | solution.py:50
  24.0 1.7 %collective-permute-start.12 = (bf16[64,1536]{1,0:T(8,128)(2,1)S(1)}, bf16[64,1536]{1,0:T(8,128)(2,1)S(1)}, u32[]{:S(2)}, u32[]{:S(2)}) collective-permute-start(bf16[64,1536]{1,0:T(8,128)(2,1)S(1)} %get-tuple-element.63), channel_id=1, source_target_pairs={{0,1},{1,0},{2,3},{3,2},{4,5},{5,4},{6,7},{7,6},{8,9},{9,8},{10,11... | collective-permute-start | bytes 589832 | tf_op jit(solution)/shard_map/ppermute | solution.py:50
  24.5 6.9 %collective-permute-start.16 = (bf16[128,768]{1,0:T(8,128)(2,1)S(1)}, bf16[128,768]{1,0:T(8,128)(2,1)S(1)}, u32[]{:S(2)}, u32[]{:S(2)}) collective-permute-start(bf16[128,768]{1,0:T(8,128)(2,1)S(1)} %copy-done.4), channel_id=1, source_target_pairs={{0,4},{4,0},{8,12},{12,8},{1,5},{5,1},{9,13},{13,9},{2,6},{6,2},{1... | collective-permute-start | bytes 589832 | tf_op jit(solution)/shard_map/ppermute | solution.py:50
  32.3 3.6 %collective-permute-start.20 = (bf16[64,1664]{1,0:T(8,128)(2,1)S(1)}, bf16[64,1664]{1,0:T(8,128)(2,1)S(1)}, u32[]{:S(2)}, u32[]{:S(2)}) collective-permute-start(bf16[64,1664]{1,0:T(8,128)(2,1)S(1)} %get-tuple-element.70), channel_id=1, source_target_pairs={{0,1},{1,0},{2,3},{3,2},{4,5},{5,4},{6,7},{7,6},{8,9},{9,8},{10,11... | collective-permute-start | bytes 638984 | tf_op jit(solution)/shard_map/ppermute | solution.py:50
  32.3 2.3 %collective-permute-start.15 = (bf16[64,1536]{1,0:T(8,128)(2,1)S(1)}, bf16[64,1536]{1,0:T(8,128)(2,1)S(1)}, u32[]{:S(2)}, u32[]{:S(2)}) collective-permute-start(bf16[64,1536]{1,0:T(8,128)(2,1)S(1)} %get-tuple-element.66.refs_4_.refs_1_), channel_id=1, source_target_pairs={{0,1},{1,0},{2,3},{3,2},{4,5},{5,4},{6,7},{7,6},{8,9},{9,8},{10,11... | collective-permute-start | bytes 589832 | tf_op jit(solution)/shard_map/ppermute | solution.py:50
  32.8 1.8 %collective-permute-start.14 = (bf16[64,1536]{1,0:T(8,128)(2,1)S(1)}, bf16[64,1536]{1,0:T(8,128)(2,1)S(1)}, u32[]{:S(2)}, u32[]{:S(2)}) collective-permute-start(bf16[64,1536]{1,0:T(8,128)(2,1)S(1)} %get-tuple-element.65.refs_3_.refs_0_), channel_id=1, source_target_pairs={{0,1},{1,0},{2,3},{3,2},{4,5},{5,4},{6,7},{7,6},{8,9},{9,8},{10,11... | collective-permute-start | bytes 589832 | tf_op jit(solution)/shard_map/ppermute | solution.py:50
  32.9 12.3 %collective-permute-start.18 = (bf16[64,3200]{1,0:T(8,128)(2,1)S(1)}, bf16[64,3200]{1,0:T(8,128)(2,1)S(1)}, u32[]{:S(2)}, u32[]{:S(2)}) collective-permute-start(bf16[64,3200]{1,0:T(8,128)(2,1)S(1)} %add_cores.6.refs_3_.refs_0_), channel_id=1, source_target_pairs={{0,2},{2,0},{1,3},{3,1},{4,6},{6,4},{5,7},{7,5},{8,10},{10,8},{9,1... | collective-permute-start | bytes 1228808 | tf_op jit(solution)/shard_map/ppermute | solution.py:50
  36.0 18.7 %collective-permute-start.24 = (bf16[64,3200]{1,0:T(8,128)(2,1)S(1)}, bf16[64,3200]{1,0:T(8,128)(2,1)S(1)}, u32[]{:S(2)}, u32[]{:S(2)}) collective-permute-start(bf16[64,3200]{1,0:T(8,128)(2,1)S(1)} %add_cores.7.refs_3_.refs_0_), channel_id=1, source_target_pairs={{0,2},{2,0},{1,3},{3,1},{4,6},{6,4},{5,7},{7,5},{8,10},{10,8},{9,1... | collective-permute-start | bytes 1228808 | tf_op jit(solution)/shard_map/ppermute | solution.py:50
  37.1 13.2 %collective-permute-start.17 = (bf16[128,896]{1,0:T(8,128)(2,1)S(1)}, bf16[128,896]{1,0:T(8,128)(2,1)S(1)}, u32[]{:S(2)}, u32[]{:S(2)}) collective-permute-start(bf16[128,896]{1,0:T(8,128)(2,1)S(1)} %down_rows.3.refs_4_), channel_id=1, source_target_pairs={{0,8},{4,12},{8,0},{12,4},{1,9},{5,13},{9,1},{13,5},{2,10},{6,14},... | collective-permute-start | bytes 688136 | tf_op jit(solution)/shard_map/ppermute | solution.py:50
  46.0 4.3 %collective-permute-start.22 = (bf16[64,1536]{1,0:T(8,128)(2,1)S(1)}, bf16[64,1536]{1,0:T(8,128)(2,1)S(1)}, u32[]{:S(2)}, u32[]{:S(2)}) collective-permute-start(bf16[64,1536]{1,0:T(8,128)(2,1)S(1)} %get-tuple-element.72.refs_4_.refs_6_), channel_id=1, source_target_pairs={{0,1},{1,0},{2,3},{3,2},{4,5},{5,4},{6,7},{7,6},{8,9},{9,8},{10,11... | collective-permute-start | bytes 589832 | tf_op jit(solution)/shard_map/ppermute | solution.py:50
  46.1 4.3 %collective-permute-start.21 = (bf16[64,1536]{1,0:T(8,128)(2,1)S(1)}, bf16[64,1536]{1,0:T(8,128)(2,1)S(1)}, u32[]{:S(2)}, u32[]{:S(2)}) collective-permute-start(bf16[64,1536]{1,0:T(8,128)(2,1)S(1)} %get-tuple-element.71.refs_0_.refs_3_.refs_5_), channel_id=1, source_target_pairs={{0,1},{1,0},{2,3},{3,2},{4,5},{5,4},{6,7},{7,6},{8,9},{9,8},{10,11... | collective-permute-start | bytes 589832 | tf_op jit(solution)/shard_map/ppermute | solution.py:50
  46.6 15.7 %collective-permute-start.28 = (bf16[64,3200]{1,0:T(8,128)(2,1)S(1)}, bf16[64,3200]{1,0:T(8,128)(2,1)S(1)}, u32[]{:S(2)}, u32[]{:S(2)}) collective-permute-start(bf16[64,3200]{1,0:T(8,128)(2,1)S(1)} %add_cores.5.refs_3_.refs_0_), channel_id=1, source_target_pairs={{0,2},{2,0},{1,3},{3,1},{4,6},{6,4},{5,7},{7,5},{8,10},{10,8},{9,1... | collective-permute-start | bytes 1228808 | tf_op jit(solution)/shard_map/ppermute | solution.py:50
  51.4 9.2 %collective-permute-start.23 = (bf16[128,896]{1,0:T(8,128)(2,1)S(1)}, bf16[128,896]{1,0:T(8,128)(2,1)S(1)}, u32[]{:S(2)}, u32[]{:S(2)}) collective-permute-start(bf16[128,896]{1,0:T(8,128)(2,1)S(1)} %down_rows.4.refs_3_), channel_id=1, source_target_pairs={{0,12},{4,8},{8,4},{12,0},{1,13},{5,9},{9,5},{13,1},{2,14},{6,10},... | collective-permute-start | bytes 688136 | tf_op jit(solution)/shard_map/ppermute | solution.py:50
  55.6 1.5 %collective-permute-start.25 = (bf16[64,1536]{1,0:T(8,128)(2,1)S(1)}, bf16[64,1536]{1,0:T(8,128)(2,1)S(1)}, u32[]{:S(2)}, u32[]{:S(2)}) collective-permute-start(bf16[64,1536]{1,0:T(8,128)(2,1)S(1)} %get-tuple-element.73.refs_3_.refs_7_.refs_10_), channel_id=1, source_target_pairs={{0,1},{1,0},{2,3},{3,2},{4,5},{5,4},{6,7},{7,6},{8,9},{9,8},{10,11... | collective-permute-start | bytes 589832 | tf_op jit(solution)/shard_map/ppermute | solution.py:50
  55.6 1.7 %collective-permute-start.26 = (bf16[64,1536]{1,0:T(8,128)(2,1)S(1)}, bf16[64,1536]{1,0:T(8,128)(2,1)S(1)}, u32[]{:S(2)}, u32[]{:S(2)}) collective-permute-start(bf16[64,1536]{1,0:T(8,128)(2,1)S(1)} %get-tuple-element.74.refs_4_.refs_11_), channel_id=1, source_target_pairs={{0,1},{1,0},{2,3},{3,2},{4,5},{5,4},{6,7},{7,6},{8,9},{9,8},{10,11... | collective-permute-start | bytes 589832 | tf_op jit(solution)/shard_map/ppermute | solution.py:50
  58.4 7.8 %collective-permute-start.27 = (bf16[128,896]{1,0:T(8,128)(2,1)S(1)}, bf16[128,896]{1,0:T(8,128)(2,1)S(1)}, u32[]{:S(2)}, u32[]{:S(2)}) collective-permute-start(bf16[128,896]{1,0:T(8,128)(2,1)S(1)} %down_rows.5.refs_0_), channel_id=1, source_target_pairs={{0,4},{4,0},{8,12},{12,8},{1,5},{5,1},{9,13},{13,9},{2,6},{6,2},{1... | collective-permute-start | bytes 688136 | tf_op jit(solution)/shard_map/ppermute | solution.py:50
  63.1 1.5 %collective-permute-start.29 = (bf16[64,1536]{1,0:T(8,128)(2,1)S(1)}, bf16[64,1536]{1,0:T(8,128)(2,1)S(1)}, u32[]{:S(2)}, u32[]{:S(2)}) collective-permute-start(bf16[64,1536]{1,0:T(8,128)(2,1)S(1)} %get-tuple-element.75.refs_6_.refs_10_.refs_7_.refs_15_), channel_id=1, source_target_pairs={{0,1},{1,0},{2,3},{3,2},{4,5},{5,4},{6,7},{7,6},{8,9},{9,8},{10,11... | collective-permute-start | bytes 589832 | tf_op jit(solution)/shard_map/ppermute | solution.py:50
  63.2 1.7 %collective-permute-start.30 = (bf16[64,1536]{1,0:T(8,128)(2,1)S(1)}, bf16[64,1536]{1,0:T(8,128)(2,1)S(1)}, u32[]{:S(2)}, u32[]{:S(2)}) collective-permute-start(bf16[64,1536]{1,0:T(8,128)(2,1)S(1)} %get-tuple-element.76.refs_7_.refs_8_.refs_16_), channel_id=1, source_target_pairs={{0,1},{1,0},{2,3},{3,2},{4,5},{5,4},{6,7},{7,6},{8,9},{9,8},{10,11... | collective-permute-start | bytes 589832 | tf_op jit(solution)/shard_map/ppermute | solution.py:50
  66.9 4.5 %collective-permute-start.31 = (bf16[32,768]{1,0:T(8,128)(2,1)S(1)}, bf16[32,768]{1,0:T(8,128)(2,1)S(1)}, u32[]{:S(2)}, u32[]{:S(2)}) collective-permute-start(bf16[32,768]{1,0:T(8,128)(2,1)S(1)} %get-tuple-element.80.refs_0_), channel_id=1, source_target_pairs={{0,4},{4,0},{8,12},{12,8},{1,5},{5,1},{9,13},{13,9},{2,6},{6,2},{1... | collective-permute-start | bytes 147464 | tf_op jit(solution)/shard_map/ppermute | solution.py:50
  67.9 5.0 %collective-permute-start.33 = (bf16[32,768]{1,0:T(8,128)(2,1)S(1)}, bf16[32,768]{1,0:T(8,128)(2,1)S(1)}, u32[]{:S(2)}, u32[]{:S(2)}) collective-permute-start(bf16[32,768]{1,0:T(8,128)(2,1)S(1)} %get-tuple-element.82.refs_0_), channel_id=1, source_target_pairs={{0,4},{4,0},{8,12},{12,8},{1,5},{5,1},{9,13},{13,9},{2,6},{6,2},{1... | collective-permute-start | bytes 147464 | tf_op jit(solution)/shard_map/ppermute | solution.py:50
  71.4 6.1 %collective-permute-start.32 = (bf16[32,768]{1,0:T(8,128)(2,1)S(1)}, bf16[32,768]{1,0:T(8,128)(2,1)S(1)}, u32[]{:S(2)}, u32[]{:S(2)}) collective-permute-start(bf16[32,768]{1,0:T(8,128)(2,1)S(1)} %add_pair.2.refs_2_.refs_0_), channel_id=1, source_target_pairs={{0,8},{4,12},{8,0},{12,4},{1,9},{5,13},{9,1},{13,5},{2,10},{6,14},... | collective-permute-start | bytes 147464 | tf_op jit(solution)/shard_map/ppermute | solution.py:50
  73.0 5.1 %collective-permute-start.34 = (bf16[32,768]{1,0:T(8,128)(2,1)S(1)}, bf16[32,768]{1,0:T(8,128)(2,1)S(1)}, u32[]{:S(2)}, u32[]{:S(2)}) collective-permute-start(bf16[32,768]{1,0:T(8,128)(2,1)S(1)} %add_pair.3.refs_2_), channel_id=1, source_target_pairs={{0,8},{4,12},{8,0},{12,4},{1,9},{5,13},{9,1},{13,5},{2,10},{6,14},... | collective-permute-start | bytes 147464 | tf_op jit(solution)/shard_map/ppermute | solution.py:50
  (10 other events, 70.0 us)

commit v6 on v5

--- a/solution.py
+++ b/solution.py
@@ -16,9 +16,9 @@
 TOUCHES = 2
 ORDER = [2, 3, 1]
 OWN_PIECES = 3
-UP_PIECES = (4, 2, 2)
+UP_PIECES = (4, 2, 3)
 OWN_PLACE = 0
-GELU_PIECES = 2
+GELU_PIECES = (4, 2, 2, 2)
 OWN_GRANT = (64 * 1024 - 11440) * 1024
 
 
@@ -311,26 +311,31 @@
         store_rows(out, at, down_product(activated, weight, at))
 
 
-def first_gradient_rows(count, *refs):
-    *blocks, out, done = refs
+def columns_of(parts, at):
+    for piece, base in bases(parts):
+        if base <= at.start < base + piece.shape[1]:
+            return piece[:, at.start - base : at.stop - base]
+
+
+def first_gradient_rows(counts, *refs):
+    *arrays, out, done = refs
     done[...] = jnp.zeros_like(done)
-    rank = out.shape[0]
-    stride = 2 * count + 1
-    places = range(0, len(blocks), stride)
+    rank, hidden = out.shape
     own = own_core()
-    factors = []
-    for at in places:
-        middle = blocks[at].shape[0]
-        low_back = blocks[at + stride - 1]
-        factors += [low_back[rows_at(core, middle), -LANES:] for core in (own, 1 - own)]
+    factors, mine, other = [], [], []
+    for count in counts:
+        block, arrays = arrays[: 2 * count + 1], arrays[2 * count + 1 :]
+        middle = block[0].shape[0]
+        factors += [block[-1][rows_at(core, middle), -LANES:] for core in (own, 1 - own)]
+        mine.append(block[:count])
+        other.append(block[count : 2 * count])
     factors = jnp.concatenate(factors, axis=0)
-    for which, (piece, base) in enumerate(bases(blocks[:count])):
-        for at in columns(piece.shape[1]):
-            right = []
-            for place in places:
-                right += [blocks[place + which][:, at], blocks[place + count + which][:, at]]
-            product = dot_rows(factors, jnp.concatenate(right, axis=0))
-            out[:, slice(at.start + base, at.stop + base)] = adapter_scale * product[LANES - rank :]
+    for at in columns(hidden, 256 if hidden % 1536 == 0 else LANES):
+        right = []
+        for parts in zip(mine, other):
+            right += [columns_of(piece, at) for piece in parts]
+        product = dot_rows(factors, jnp.concatenate(right, axis=0))
+        out[:, at] = adapter_scale * product[LANES - rank :]
 
 
 def second_gradient_part(terms, first, cot, mod, *refs):
@@ -466,7 +471,7 @@
         place = len(activated)
         parts = call(
             named(gelu_rows, features),
-            cut(GELU_PIECES),
+            cut(GELU_PIECES[min(place, 3)]),
             [*pairs[place], table],
             after,
         )
@@ -528,7 +533,7 @@
     for parts, rows_of in zip(activated, received + [low_back]):
         gathered += [*parts, rows_of]
     first_gradient, done = call(
-        named(first_gradient_rows, len(cut(GELU_PIECES))),
+        named(first_gradient_rows, [len(parts) // 2 for parts in activated]),
         [((rank, hidden), f32), ((8, LANES), f32)],
         gathered,
         [low_total],

time: 78.9 us -> 79.2 us (level)
    ppermute x35 -> x38, waiting for transfers between devices: 28.3 us -> 28.5 us  [swap(): return lax.ppermute(value, axis, [(i, i ^ distance) for i in range(size)])]
    ppermute x35 -> x38, starting transfers between devices: 30.6 us -> 30.4 us  [swap(): return lax.ppermute(value, axis, [(i, i ^ distance) for i in range(size)])]
  transfers between devices with their start and end apart: 35 -> 38, of which waited for: 22 -> 20; matrix products, arithmetic and copies ran while one was open for 0% -> 0% of each run, Pallas kernels for 19% -> 20%
where the time goes in v6:
time: 79.2 us; the launch traced here: 79 us
  starting transfers between devices  30.4 us (38%)
  waiting for transfers between devices  28.5 us (36%)
  Pallas kernels  17.5 us (22%)
  between operations  1.61 us (2%)
  local copies, waits for them, and re-layouts  0.91 us (1%)
    ppermute x38, starting transfers between devices, swap(): return lax.ppermute(value, axis, [(i, i ^ distance) for i in range(size)])  30.4 us
    ppermute x38, waiting for transfers between devices, swap(): return lax.ppermute(value, axis, [(i, i ^ distance) for i in range(size)])  28.5 us
    pallas_call x27, Pallas kernels, call(): pl.pallas_call(kernel, out_shape=[jax.ShapeDtypeStruct(shape, kind) for s...  17.5 us
  transfers between devices with their start and end apart: 38, of which 20 were waited for; matrix products, arithmetic and copies ran while one was open for 0% of the time, Pallas kernels for 20%

profile of v6, /device:TPU:0, one launch (start us, length us, event | category | flops | bytes accessed | tf_op | source)
XLA Modules:
  0.0 79.0 jit_solution(7886170926910141796)
XLA Ops:
  0.6 4.1 %collective-permute-start.2 = (bf16[128,768]{1,0:T(8,128)(2,1)}, bf16[128,768]{1,0:T(8,128)(2,1)S(1)}, u32[]{:S(2)}, u32[]{:S(2)}) collective-permute-start(bf16[128,768]{1,0:T(8,128)(2,1)} %refs_1_.2), channel_id=1, source_target_pairs={{0,8},{4,12},{8,0},{12,4},{1,9},{5,13},{9,1},{13,5},{2,10},{6,14},... | collective-permute-start | bytes 589832 | tf_op jit(solution)/shard_map/ppermute | solution.py:50
  6.3 3.2 %own_rows.1 = (bf16[64,1024]{1,0:T(8,128)(2,1)S(1)}, bf16[64,1024]{1,0:T(8,128)(2,1)S(1)}, bf16[64,1152]{1,0:T(8,128)(2,1)S(1)}, bf16[64,1024]{1,0:T(8,128)(2,1)...) custom-call(s32[1]{0:T(128)S(6)} %copy.11.refs_0_, ...), custom_call_target="tpu_custom_call" | custom-call | flops 1024 | bytes 1024 | tf_op jit(solution)/shard_map/own_rows/pallas_call | solution.py:74
  9.5 1.3 %collective-permute-done.refs_1_ = f32[248,128]{1,0:T(8,128)S(1)} collective-permute-done((f32[248,128]{1,0:T(8,128)S(1)}, f32[248,128]{1,0:T(8,128)S(1)}, u32[]{:S(2)}, u32[]{:S(2)}) %collective-permute-start) | collective-permute-done | bytes 127008 | tf_op jit(solution)/shard_map/ppermute | solution.py:50
  10.9 1.6 %collective-permute-start.1 = (f32[248,128]{1,0:T(8,128)S(1)}, f32[248,128]{1,0:T(8,128)S(1)}, u32[]{:S(2)}, u32[]{:S(2)}) collective-permute-start(f32[248,128]{1,0:T(8,128)S(1)} %add_packed.1.refs_0_.refs_3_), channel_id=1, source_target_pairs={{0,2},{2,0},{1,3},{3,1},{4,6},{6,4},{5,7},{7,5},{8,10},{10,8},{9,1... | collective-permute-start | bytes 380936 | tf_op jit(solution)/shard_map/ppermute | solution.py:50
  12.4 1.6 %collective-permute-done.2.refs_0_ = bf16[128,768]{1,0:T(8,128)(2,1)S(1)} collective-permute-done((bf16[128,768]{1,0:T(8,128)(2,1)}, bf16[128,768]{1,0:T(8,128)(2,1)S(1)}, u32[]{:S(2)}, u32[]{:S(2)}) %collective-permute-start.2) | collective-permute-done | bytes 196640 | tf_op jit(solution)/shard_map/ppermute | solution.py:50
  16.4 1.6 %collective-permute-start.8 = (bf16[128,768]{1,0:T(8,128)(2,1)S(1)}, bf16[128,768]{1,0:T(8,128)(2,1)S(1)}, u32[]{:S(2)}, u32[]{:S(2)}) collective-permute-start(bf16[128,768]{1,0:T(8,128)(2,1)S(1)} %collective-permute-done.2.refs_0_), channel_id=1, source_target_pairs={{0,4},{4,0},{8,12},{12,8},{1,5},{5,1},{9,13},{13,9},{2,6},{6,2},{1... | collective-permute-start | bytes 589832 | tf_op jit(solution)/shard_map/ppermute | solution.py:50
  18.2 1.6 %collective-permute-start.7 = (bf16[64,3200]{1,0:T(8,128)(2,1)S(1)}, bf16[64,3200]{1,0:T(8,128)(2,1)S(1)}, u32[]{:S(2)}, u32[]{:S(2)}) collective-permute-start(bf16[64,3200]{1,0:T(8,128)(2,1)S(1)} %add_cores.4.refs_6_.refs_0_), channel_id=1, source_target_pairs={{0,2},{2,0},{1,3},{3,1},{4,6},{6,4},{5,7},{7,5},{8,10},{10,8},{9,1... | collective-permute-start | bytes 1228808 | tf_op jit(solution)/shard_map/ppermute | solution.py:50
  20.3 1.0 %collective-permute-done.9.refs_3_ = bf16[64,1024]{1,0:T(8,128)(2,1)S(1)} collective-permute-done((bf16[64,1024]{1,0:T(8,128)(2,1)S(1)}, bf16[64,1024]{1,0:T(8,128)(2,1)S(1)}, u32[]{:S(2)}, u32[]{:S(2)}) %collective-permute-start.9) | collective-permute-done | bytes 131104 | tf_op jit(solution)/shard_map/ppermute | solution.py:50
  21.7 1.2 %collective-permute-done.8.refs_0_ = bf16[128,768]{1,0:T(8,128)(2,1)S(1)} collective-permute-done((bf16[128,768]{1,0:T(8,128)(2,1)S(1)}, bf16[128,768]{1,0:T(8,128)(2,1)S(1)}, u32[]{:S(2)}, u32[]{:S(2)}) %collective-permute-start.8) | collective-permute-done | bytes 196640 | tf_op jit(solution)/shard_map/ppermute | solution.py:50
  24.5 1.1 %collective-permute-start.18 = (bf16[128,768]{1,0:T(8,128)(2,1)S(1)}, bf16[128,768]{1,0:T(8,128)(2,1)S(1)}, u32[]{:S(2)}, u32[]{:S(2)}) collective-permute-start(bf16[128,768]{1,0:T(8,128)(2,1)S(1)} %copy-done.4), channel_id=1, source_target_pairs={{0,4},{4,0},{8,12},{12,8},{1,5},{5,1},{9,13},{13,9},{2,6},{6,2},{1... | collective-permute-start | bytes 589832 | tf_op jit(solution)/shard_map/ppermute | solution.py:50
  25.8 3.1 %collective-permute-done.7.refs_1_ = bf16[64,3200]{1,0:T(8,128)(2,1)S(1)} collective-permute-done((bf16[64,3200]{1,0:T(8,128)(2,1)S(1)}, bf16[64,3200]{1,0:T(8,128)(2,1)S(1)}, u32[]{:S(2)}, u32[]{:S(2)}) %collective-permute-start.7) | collective-permute-done | bytes 409632 | tf_op jit(solution)/shard_map/ppermute | solution.py:50
  30.4 1.5 %collective-permute-start.20 = (bf16[64,3200]{1,0:T(8,128)(2,1)S(1)}, bf16[64,3200]{1,0:T(8,128)(2,1)S(1)}, u32[]{:S(2)}, u32[]{:S(2)}) collective-permute-start(bf16[64,3200]{1,0:T(8,128)(2,1)S(1)} %add_cores.6.refs_3_.refs_0_), channel_id=1, source_target_pairs={{0,2},{2,0},{1,3},{3,1},{4,6},{6,4},{5,7},{7,5},{8,10},{10,8},{9,1... | collective-permute-start | bytes 1228808 | tf_op jit(solution)/shard_map/ppermute | solution.py:50
  34.0 1.0 %collective-permute-done.14.refs_7_.refs_4_ = bf16[64,768]{1,0:T(8,128)(2,1)S(1)} collective-permute-done((bf16[64,768]{1,0:T(8,128)(2,1)S(1)}, bf16[64,768]{1,0:T(8,128)(2,1)S(1)}, u32[]{:S(2)}, u32[]{:S(2)}) %collective-permute-start.14) | collective-permute-done | bytes 98336 | tf_op jit(solution)/shard_map/ppermute | solution.py:50
  35.0 1.0 %down_rows.3.refs_6_ = bf16[128,896]{1,0:T(8,128)(2,1)S(1)} custom-call(bf16[3072,768]{1,0:T(8,128)(2,1)S(1)} %bitcast.4, bf16[64,12288]{1,0:T(8,128)(2,1)S(1)} %bitcast.5, bf16[128,128]{1,0:T(8,128)(2,1)S(1)} %get-tuple-element.49.refs_2_.refs_23_, bf16[64,768]{1,0:T(8,128)(2,1)S(1)} %get-tuple-element.69.refs_3_.refs_0_, ...), custom_call_target="tpu_custom_call" | custom-call | flops 1024 | bytes 1024 | tf_op jit(solution)/shard_map/down_rows/pallas_call | solution.py:74
  37.1 2.3 %collective-permute-start.19 = (bf16[128,896]{1,0:T(8,128)(2,1)S(1)}, bf16[128,896]{1,0:T(8,128)(2,1)S(1)}, u32[]{:S(2)}, u32[]{:S(2)}) collective-permute-start(bf16[128,896]{1,0:T(8,128)(2,1)S(1)} %down_rows.3.refs_6_), channel_id=1, source_target_pairs={{0,8},{4,12},{8,0},{12,4},{1,9},{5,13},{9,1},{13,5},{2,10},{6,14},... | collective-permute-start | bytes 688136 | tf_op jit(solution)/shard_map/ppermute | solution.py:50
  39.4 3.3 %collective-permute-done.20.refs_1_ = bf16[64,3200]{1,0:T(8,128)(2,1)S(1)} collective-permute-done((bf16[64,3200]{1,0:T(8,128)(2,1)S(1)}, bf16[64,3200]{1,0:T(8,128)(2,1)S(1)}, u32[]{:S(2)}, u32[]{:S(2)}) %collective-permute-start.20) | collective-permute-done | bytes 409632 | tf_op jit(solution)/shard_map/ppermute | solution.py:50
  44.2 1.5 %collective-permute-start.31 = (bf16[64,3200]{1,0:T(8,128)(2,1)S(1)}, bf16[64,3200]{1,0:T(8,128)(2,1)S(1)}, u32[]{:S(2)}, u32[]{:S(2)}) collective-permute-start(bf16[64,3200]{1,0:T(8,128)(2,1)S(1)} %add_cores.5.refs_3_.refs_0_), channel_id=1, source_target_pairs={{0,2},{2,0},{1,3},{3,1},{4,6},{6,4},{5,7},{7,5},{8,10},{10,8},{9,1... | collective-permute-start | bytes 1228808 | tf_op jit(solution)/shard_map/ppermute | solution.py:50
  45.7 4.8 %collective-permute-done.19.refs_1_.refs_3_.refs_4_.refs_8_ = bf16[128,896]{1,0:T(8,128)(2,1)S(1)} collective-permute-done((bf16[128,896]{1,0:T(8,128)(2,1)S(1)}, bf16[128,896]{1,0:T(8,128)(2,1)S(1)}, u32[]{:S(2)}, u32[]{:S(2)}) %collective-permute-start.19) | collective-permute-done | bytes 229408 | tf_op jit(solution)/shard_map/ppermute | solution.py:50
  50.5 1.0 %down_rows.4.refs_3_ = bf16[128,896]{1,0:T(8,128)(2,1)S(1)} custom-call(bf16[3072,768]{1,0:T(8,128)(2,1)S(1)} %bitcast.4, bf16[64,12288]{1,0:T(8,128)(2,1)S(1)} %bitcast.6, bf16[128,128]{1,0:T(8,128)(2,1)S(1)} %get-tuple-element.49.refs_2_.refs_23_, bf16[64,1536]{1,0:T(8,128)(2,1)S(1)} %get-tuple-element.79.refs_0_.refs_3_.refs_9_, ...), custom_call_target="tpu_custom_call" | custom-call | flops 1024 | bytes 1024 | tf_op jit(solution)/shard_map/down_rows/pallas_call | solution.py:74
  51.5 3.3 %collective-permute-start.26 = (bf16[128,896]{1,0:T(8,128)(2,1)S(1)}, bf16[128,896]{1,0:T(8,128)(2,1)S(1)}, u32[]{:S(2)}, u32[]{:S(2)}) collective-permute-start(bf16[128,896]{1,0:T(8,128)(2,1)S(1)} %down_rows.4.refs_3_), channel_id=1, source_target_pairs={{0,12},{4,8},{8,4},{12,0},{1,13},{5,9},{9,5},{13,1},{2,14},{6,10},... | collective-permute-start | bytes 688136 | tf_op jit(solution)/shard_map/ppermute | solution.py:50
  57.5 1.0 %down_rows.5.refs_0_ = bf16[128,896]{1,0:T(8,128)(2,1)S(1)} custom-call(bf16[3072,768]{1,0:T(8,128)(2,1)S(1)} %bitcast.4, bf16[64,12288]{1,0:T(8,128)(2,1)S(1)} %bitcast.7, bf16[128,128]{1,0:T(8,128)(2,1)S(1)} %get-tuple-element.49.refs_2_.refs_23_, bf16[64,1536]{1,0:T(8,128)(2,1)S(1)} %get-tuple-element.81.refs_3_.refs_7_.refs_14_, ...), custom_call_target="tpu_custom_call" | custom-call | flops 1024 | bytes 1024 | tf_op jit(solution)/shard_map/down_rows/pallas_call | solution.py:74
  58.6 2.4 %collective-permute-done.26.refs_1_.refs_4_.refs_5_.refs_13_ = bf16[128,896]{1,0:T(8,128)(2,1)S(1)} collective-permute-done((bf16[128,896]{1,0:T(8,128)(2,1)S(1)}, bf16[128,896]{1,0:T(8,128)(2,1)S(1)}, u32[]{:S(2)}, u32[]{:S(2)}) %collective-permute-start.26) | collective-permute-done | bytes 229408 | tf_op jit(solution)/shard_map/ppermute | solution.py:50
  61.0 1.0 %gelu_rows.7 = (bf16[64,1536]{1,0:T(8,128)(2,1)S(1)}, bf16[64,1536]{1,0:T(8,128)(2,1)S(1)}) custom-call(bf16[64,3200]{1,0:T(8,128)(2,1)S(1)} %add_cores.5.refs_3_.refs_0_, bf16[64,3200]{1,0:T(8,128)(2,1)S(1)} %collective-permute-done.31.refs_1_, f32[8,3072]{1,0:T(8,128)S(1)} %get-tuple-element.58.refs_9_.refs_2_, f32[8,128]{1,0:T(8,128)S(1)} %touch.7.refs_3_), custom_call_target="tpu_custom_call" | custom-call | flops 1024 | bytes 1024 | tf_op jit(solution)/shard_map/gelu_rows/pallas_call | solution.py:74
  63.8 2.5 %collective-permute-done.30.refs_5_.refs_6_.refs_18_ = bf16[128,896]{1,0:T(8,128)(2,1)S(1)} collective-permute-done((bf16[128,896]{1,0:T(8,128)(2,1)S(1)}, bf16[128,896]{1,0:T(8,128)(2,1)S(1)}, u32[]{:S(2)}, u32[]{:S(2)}) %collective-permute-start.30) | collective-permute-done | bytes 229408 | tf_op jit(solution)/shard_map/ppermute | solution.py:50
  67.0 1.1 %collective-permute-start.34 = (bf16[32,768]{1,0:T(8,128)(2,1)S(1)}, bf16[32,768]{1,0:T(8,128)(2,1)S(1)}, u32[]{:S(2)}, u32[]{:S(2)}) collective-permute-start(bf16[32,768]{1,0:T(8,128)(2,1)S(1)} %get-tuple-element.88.refs_0_), channel_id=1, source_target_pairs={{0,4},{4,0},{8,12},{12,8},{1,5},{5,1},{9,13},{13,9},{2,6},{6,2},{1... | collective-permute-start | bytes 147464 | tf_op jit(solution)/shard_map/ppermute | solution.py:50
  68.1 1.0 %collective-permute-start.36 = (bf16[32,768]{1,0:T(8,128)(2,1)S(1)}, bf16[32,768]{1,0:T(8,128)(2,1)S(1)}, u32[]{:S(2)}, u32[]{:S(2)}) collective-permute-start(bf16[32,768]{1,0:T(8,128)(2,1)S(1)} %get-tuple-element.90.refs_0_), channel_id=1, source_target_pairs={{0,4},{4,0},{8,12},{12,8},{1,5},{5,1},{9,13},{13,9},{2,6},{6,2},{1... | collective-permute-start | bytes 147464 | tf_op jit(solution)/shard_map/ppermute | solution.py:50
  69.1 1.5 %first_gradient_rows.1 = (f32[64,3072]{1,0:T(8,128)}, f32[8,128]{1,0:T(8,128)S(1)}) custom-call(bf16[64,768]{1,0:T(8,128)(2,1)S(1)} %get-tuple-element.69.refs_3_.refs_0_, bf16[64,768]{1,0:T(8,128)(2,1)S(1)} %get-tuple-element.70.refs_4_.refs_1_, bf16[64,768]{1,0:T(8,128)(2,1)S(1)} %get-tuple-element.71.refs_5_.refs_2_, ...), custom_call_target="tpu_custom_call" | custom-call | flops 1024 | bytes 1024 | tf_op jit(solution)/shard_map/first_gradient_rows/pallas_call | solution.py:74
  70.6 1.1 %collective-permute-done.34.refs_1_ = bf16[32,768]{1,0:T(8,128)(2,1)S(1)} collective-permute-done((bf16[32,768]{1,0:T(8,128)(2,1)S(1)}, bf16[32,768]{1,0:T(8,128)(2,1)S(1)}, u32[]{:S(2)}, u32[]{:S(2)}) %collective-permute-start.34) | collective-permute-done | bytes 49184 | tf_op jit(solution)/shard_map/ppermute | solution.py:50
  71.7 1.0 %collective-permute-start.35 = (bf16[32,768]{1,0:T(8,128)(2,1)S(1)}, bf16[32,768]{1,0:T(8,128)(2,1)S(1)}, u32[]{:S(2)}, u32[]{:S(2)}) collective-permute-start(bf16[32,768]{1,0:T(8,128)(2,1)S(1)} %add_pair.2.refs_2_.refs_0_), channel_id=1, source_target_pairs={{0,8},{4,12},{8,0},{12,4},{1,9},{5,13},{9,1},{13,5},{2,10},{6,14},... | collective-permute-start | bytes 147464 | tf_op jit(solution)/shard_map/ppermute | solution.py:50
  72.7 2.1 %collective-permute-start.37 = (bf16[32,768]{1,0:T(8,128)(2,1)S(1)}, bf16[32,768]{1,0:T(8,128)(2,1)S(1)}, u32[]{:S(2)}, u32[]{:S(2)}) collective-permute-start(bf16[32,768]{1,0:T(8,128)(2,1)S(1)} %add_pair.3.refs_2_), channel_id=1, source_target_pairs={{0,8},{4,12},{8,0},{12,4},{1,9},{5,13},{9,1},{13,5},{2,10},{6,14},... | collective-permute-start | bytes 147464 | tf_op jit(solution)/shard_map/ppermute | solution.py:50
  74.7 1.6 %update_rows.1 = bf16[128,768]{1,0:T(8,128)(2,1)} custom-call(bf16[3072,768]{1,0:T(8,128)(2,1)S(1)} %bitcast.4, f32[128,64]{1,0:T(8,128)S(1)} %get-tuple-element.85.refs_1_.refs_24_, bf16[64,768]{1,0:T(8,128)(2,1)S(1)} %get-tuple-element.86.refs_2_, f32[8,768]{1,0:T(8,128)S(1)} %get-tuple-element.47.refs_1_.refs_2_.refs_3_, ...), custom_call_target="tpu_custom_call" | custom-call | flops 1024 | bytes 1024 | tf_op jit(solution)/shard_map/update_rows/pallas_call | solution.py:74
  76.4 1.4 %collective-permute-done.35.refs_1_ = bf16[32,768]{1,0:T(8,128)(2,1)S(1)} collective-permute-done((bf16[32,768]{1,0:T(8,128)(2,1)S(1)}, bf16[32,768]{1,0:T(8,128)(2,1)S(1)}, u32[]{:S(2)}, u32[]{:S(2)}) %collective-permute-start.35) | collective-permute-done | bytes 49184 | tf_op jit(solution)/shard_map/ppermute | solution.py:50
  (86 shorter events, 18.5 us)
Async XLA Ops:
  0.6 13.4 %collective-permute-start.2 = (bf16[128,768]{1,0:T(8,128)(2,1)}, bf16[128,768]{1,0:T(8,128)(2,1)S(1)}, u32[]{:S(2)}, u32[]{:S(2)}) collective-permute-start(bf16[128,768]{1,0:T(8,128)(2,1)} %refs_1_.2), channel_id=1, source_target_pairs={{0,8},{4,12},{8,0},{12,4},{1,9},{5,13},{9,1},{13,5},{2,10},{6,14},... | collective-permute-start | bytes 589832 | tf_op jit(solution)/shard_map/ppermute | solution.py:50
  10.9 5.5 %collective-permute-start.1 = (f32[248,128]{1,0:T(8,128)S(1)}, f32[248,128]{1,0:T(8,128)S(1)}, u32[]{:S(2)}, u32[]{:S(2)}) collective-permute-start(f32[248,128]{1,0:T(8,128)S(1)} %add_packed.1.refs_0_.refs_3_), channel_id=1, source_target_pairs={{0,2},{2,0},{1,3},{3,1},{4,6},{6,4},{5,7},{7,5},{8,10},{10,8},{9,1... | collective-permute-start | bytes 380936 | tf_op jit(solution)/shard_map/ppermute | solution.py:50
  15.0 3.1 %collective-permute-start.6 = (bf16[64,896]{1,0:T(8,128)(2,1)S(1)}, bf16[64,896]{1,0:T(8,128)(2,1)S(1)}, u32[]{:S(2)}, u32[]{:S(2)}) collective-permute-start(bf16[64,896]{1,0:T(8,128)(2,1)S(1)} %get-tuple-element.57), channel_id=1, source_target_pairs={{0,1},{1,0},{2,3},{3,2},{4,5},{5,4},{6,7},{7,6},{8,9},{9,8},{10,11... | collective-permute-start | bytes 344072 | tf_op jit(solution)/shard_map/ppermute | solution.py:50
  15.1 3.0 %collective-permute-start.3 = (bf16[64,768]{1,0:T(8,128)(2,1)S(1)}, bf16[64,768]{1,0:T(8,128)(2,1)S(1)}, u32[]{:S(2)}, u32[]{:S(2)}) collective-permute-start(bf16[64,768]{1,0:T(8,128)(2,1)S(1)} %get-tuple-element.54), channel_id=1, source_target_pairs={{0,1},{1,0},{2,3},{3,2},{4,5},{5,4},{6,7},{7,6},{8,9},{9,8},{10,11... | collective-permute-start | bytes 294920 | tf_op jit(solution)/shard_map/ppermute | solution.py:50
  15.6 2.5 %collective-permute-start.4 = (bf16[64,768]{1,0:T(8,128)(2,1)S(1)}, bf16[64,768]{1,0:T(8,128)(2,1)S(1)}, u32[]{:S(2)}, u32[]{:S(2)}) collective-permute-start(bf16[64,768]{1,0:T(8,128)(2,1)S(1)} %get-tuple-element.55), channel_id=1, source_target_pairs={{0,1},{1,0},{2,3},{3,2},{4,5},{5,4},{6,7},{7,6},{8,9},{9,8},{10,11... | collective-permute-start | bytes 294920 | tf_op jit(solution)/shard_map/ppermute | solution.py:50
  15.6 2.4 %collective-permute-start.5 = (bf16[64,768]{1,0:T(8,128)(2,1)S(1)}, bf16[64,768]{1,0:T(8,128)(2,1)S(1)}, u32[]{:S(2)}, u32[]{:S(2)}) collective-permute-start(bf16[64,768]{1,0:T(8,128)(2,1)S(1)} %get-tuple-element.56), channel_id=1, source_target_pairs={{0,1},{1,0},{2,3},{3,2},{4,5},{5,4},{6,7},{7,6},{8,9},{9,8},{10,11... | collective-permute-start | bytes 294920 | tf_op jit(solution)/shard_map/ppermute | solution.py:50
  16.4 6.6 %collective-permute-start.8 = (bf16[128,768]{1,0:T(8,128)(2,1)S(1)}, bf16[128,768]{1,0:T(8,128)(2,1)S(1)}, u32[]{:S(2)}, u32[]{:S(2)}) collective-permute-start(bf16[128,768]{1,0:T(8,128)(2,1)S(1)} %collective-permute-done.2.refs_0_), channel_id=1, source_target_pairs={{0,4},{4,0},{8,12},{12,8},{1,5},{5,1},{9,13},{13,9},{2,6},{6,2},{1... | collective-permute-start | bytes 589832 | tf_op jit(solution)/shard_map/ppermute | solution.py:50
  18.2 10.7 %collective-permute-start.7 = (bf16[64,3200]{1,0:T(8,128)(2,1)S(1)}, bf16[64,3200]{1,0:T(8,128)(2,1)S(1)}, u32[]{:S(2)}, u32[]{:S(2)}) collective-permute-start(bf16[64,3200]{1,0:T(8,128)(2,1)S(1)} %add_cores.4.refs_6_.refs_0_), channel_id=1, source_target_pairs={{0,2},{2,0},{1,3},{3,1},{4,6},{6,4},{5,7},{7,5},{8,10},{10,8},{9,1... | collective-permute-start | bytes 1228808 | tf_op jit(solution)/shard_map/ppermute | solution.py:50
  19.8 1.9 %collective-permute-start.11 = (bf16[64,1152]{1,0:T(8,128)(2,1)S(1)}, bf16[64,1152]{1,0:T(8,128)(2,1)S(1)}, u32[]{:S(2)}, u32[]{:S(2)}) collective-permute-start(bf16[64,1152]{1,0:T(8,128)(2,1)S(1)} %get-tuple-element.64), channel_id=1, source_target_pairs={{0,1},{1,0},{2,3},{3,2},{4,5},{5,4},{6,7},{7,6},{8,9},{9,8},{10,11... | collective-permute-start | bytes 442376 | tf_op jit(solution)/shard_map/ppermute | solution.py:50
  23.9 1.8 %collective-permute-start.13 = (bf16[64,1664]{1,0:T(8,128)(2,1)S(1)}, bf16[64,1664]{1,0:T(8,128)(2,1)S(1)}, u32[]{:S(2)}, u32[]{:S(2)}) collective-permute-start(bf16[64,1664]{1,0:T(8,128)(2,1)S(1)} %get-tuple-element.68), channel_id=1, source_target_pairs={{0,1},{1,0},{2,3},{3,2},{4,5},{5,4},{6,7},{7,6},{8,9},{9,8},{10,11... | collective-permute-start | bytes 638984 | tf_op jit(solution)/shard_map/ppermute | solution.py:50
  24.0 1.7 %collective-permute-start.12 = (bf16[64,1536]{1,0:T(8,128)(2,1)S(1)}, bf16[64,1536]{1,0:T(8,128)(2,1)S(1)}, u32[]{:S(2)}, u32[]{:S(2)}) collective-permute-start(bf16[64,1536]{1,0:T(8,128)(2,1)S(1)} %get-tuple-element.67), channel_id=1, source_target_pairs={{0,1},{1,0},{2,3},{3,2},{4,5},{5,4},{6,7},{7,6},{8,9},{9,8},{10,11... | collective-permute-start | bytes 589832 | tf_op jit(solution)/shard_map/ppermute | solution.py:50
  24.5 7.5 %collective-permute-start.18 = (bf16[128,768]{1,0:T(8,128)(2,1)S(1)}, bf16[128,768]{1,0:T(8,128)(2,1)S(1)}, u32[]{:S(2)}, u32[]{:S(2)}) collective-permute-start(bf16[128,768]{1,0:T(8,128)(2,1)S(1)} %copy-done.4), channel_id=1, source_target_pairs={{0,4},{4,0},{8,12},{12,8},{1,5},{5,1},{9,13},{13,9},{2,6},{6,2},{1... | collective-permute-start | bytes 589832 | tf_op jit(solution)/shard_map/ppermute | solution.py:50
  29.8 3.3 %collective-permute-start.15 = (bf16[64,768]{1,0:T(8,128)(2,1)S(1)}, bf16[64,768]{1,0:T(8,128)(2,1)S(1)}, u32[]{:S(2)}, u32[]{:S(2)}) collective-permute-start(bf16[64,768]{1,0:T(8,128)(2,1)S(1)} %get-tuple-element.70.refs_4_.refs_1_), channel_id=1, source_target_pairs={{0,1},{1,0},{2,3},{3,2},{4,5},{5,4},{6,7},{7,6},{8,9},{9,8},{10,11... | collective-permute-start | bytes 294920 | tf_op jit(solution)/shard_map/ppermute | solution.py:50
  29.9 3.6 %collective-permute-start.16 = (bf16[64,768]{1,0:T(8,128)(2,1)S(1)}, bf16[64,768]{1,0:T(8,128)(2,1)S(1)}, u32[]{:S(2)}, u32[]{:S(2)}) collective-permute-start(bf16[64,768]{1,0:T(8,128)(2,1)S(1)} %get-tuple-element.71.refs_5_.refs_2_), channel_id=1, source_target_pairs={{0,1},{1,0},{2,3},{3,2},{4,5},{5,4},{6,7},{7,6},{8,9},{9,8},{10,11... | collective-permute-start | bytes 294920 | tf_op jit(solution)/shard_map/ppermute | solution.py:50
  30.4 3.3 %collective-permute-start.17 = (bf16[64,768]{1,0:T(8,128)(2,1)S(1)}, bf16[64,768]{1,0:T(8,128)(2,1)S(1)}, u32[]{:S(2)}, u32[]{:S(2)}) collective-permute-start(bf16[64,768]{1,0:T(8,128)(2,1)S(1)} %get-tuple-element.72.refs_6_.refs_3_), channel_id=1, source_target_pairs={{0,1},{1,0},{2,3},{3,2},{4,5},{5,4},{6,7},{7,6},{8,9},{9,8},{10,11... | collective-permute-start | bytes 294920 | tf_op jit(solution)/shard_map/ppermute | solution.py:50
  30.4 12.3 %collective-permute-start.20 = (bf16[64,3200]{1,0:T(8,128)(2,1)S(1)}, bf16[64,3200]{1,0:T(8,128)(2,1)S(1)}, u32[]{:S(2)}, u32[]{:S(2)}) collective-permute-start(bf16[64,3200]{1,0:T(8,128)(2,1)S(1)} %add_cores.6.refs_3_.refs_0_), channel_id=1, source_target_pairs={{0,2},{2,0},{1,3},{3,1},{4,6},{6,4},{5,7},{7,5},{8,10},{10,8},{9,1... | collective-permute-start | bytes 1228808 | tf_op jit(solution)/shard_map/ppermute | solution.py:50
  32.9 3.1 %collective-permute-start.23 = (bf16[64,1152]{1,0:T(8,128)(2,1)S(1)}, bf16[64,1152]{1,0:T(8,128)(2,1)S(1)}, u32[]{:S(2)}, u32[]{:S(2)}) collective-permute-start(bf16[64,1152]{1,0:T(8,128)(2,1)S(1)} %get-tuple-element.78), channel_id=1, source_target_pairs={{0,1},{1,0},{2,3},{3,2},{4,5},{5,4},{6,7},{7,6},{8,9},{9,8},{10,11... | collective-permute-start | bytes 442376 | tf_op jit(solution)/shard_map/ppermute | solution.py:50
  33.1 2.9 %collective-permute-start.21 = (bf16[64,1024]{1,0:T(8,128)(2,1)S(1)}, bf16[64,1024]{1,0:T(8,128)(2,1)S(1)}, u32[]{:S(2)}, u32[]{:S(2)}) collective-permute-start(bf16[64,1024]{1,0:T(8,128)(2,1)S(1)} %get-tuple-element.76), channel_id=1, source_target_pairs={{0,1},{1,0},{2,3},{3,2},{4,5},{5,4},{6,7},{7,6},{8,9},{9,8},{10,11... | collective-permute-start | bytes 393224 | tf_op jit(solution)/shard_map/ppermute | solution.py:50
  33.5 2.6 %collective-permute-start.22 = (bf16[64,1024]{1,0:T(8,128)(2,1)S(1)}, bf16[64,1024]{1,0:T(8,128)(2,1)S(1)}, u32[]{:S(2)}, u32[]{:S(2)}) collective-permute-start(bf16[64,1024]{1,0:T(8,128)(2,1)S(1)} %get-tuple-element.77), channel_id=1, source_target_pairs={{0,1},{1,0},{2,3},{3,2},{4,5},{5,4},{6,7},{7,6},{8,9},{9,8},{10,11... | collective-permute-start | bytes 393224 | tf_op jit(solution)/shard_map/ppermute | solution.py:50
  36.2 18.6 %collective-permute-start.27 = (bf16[64,3200]{1,0:T(8,128)(2,1)S(1)}, bf16[64,3200]{1,0:T(8,128)(2,1)S(1)}, u32[]{:S(2)}, u32[]{:S(2)}) collective-permute-start(bf16[64,3200]{1,0:T(8,128)(2,1)S(1)} %add_cores.7.refs_3_.refs_0_), channel_id=1, source_target_pairs={{0,2},{2,0},{1,3},{3,1},{4,6},{6,4},{5,7},{7,5},{8,10},{10,8},{9,1... | collective-permute-start | bytes 1228808 | tf_op jit(solution)/shard_map/ppermute | solution.py:50
  37.1 13.4 %collective-permute-start.19 = (bf16[128,896]{1,0:T(8,128)(2,1)S(1)}, bf16[128,896]{1,0:T(8,128)(2,1)S(1)}, u32[]{:S(2)}, u32[]{:S(2)}) collective-permute-start(bf16[128,896]{1,0:T(8,128)(2,1)S(1)} %down_rows.3.refs_6_), channel_id=1, source_target_pairs={{0,8},{4,12},{8,0},{12,4},{1,9},{5,13},{9,1},{13,5},{2,10},{6,14},... | collective-permute-start | bytes 688136 | tf_op jit(solution)/shard_map/ppermute | solution.py:50
  43.6 6.9 %collective-permute-start.25 = (bf16[64,1536]{1,0:T(8,128)(2,1)S(1)}, bf16[64,1536]{1,0:T(8,128)(2,1)S(1)}, u32[]{:S(2)}, u32[]{:S(2)}) collective-permute-start(bf16[64,1536]{1,0:T(8,128)(2,1)S(1)} %get-tuple-element.80.refs_4_.refs_10_), channel_id=1, source_target_pairs={{0,1},{1,0},{2,3},{3,2},{4,5},{5,4},{6,7},{7,6},{8,9},{9,8},{10,11... | collective-permute-start | bytes 589832 | tf_op jit(solution)/shard_map/ppermute | solution.py:50
  43.7 6.8 %collective-permute-start.24 = (bf16[64,1536]{1,0:T(8,128)(2,1)S(1)}, bf16[64,1536]{1,0:T(8,128)(2,1)S(1)}, u32[]{:S(2)}, u32[]{:S(2)}) collective-permute-start(bf16[64,1536]{1,0:T(8,128)(2,1)S(1)} %get-tuple-element.79.refs_0_.refs_3_.refs_9_), channel_id=1, source_target_pairs={{0,1},{1,0},{2,3},{3,2},{4,5},{5,4},{6,7},{7,6},{8,9},{9,8},{10,11... | collective-permute-start | bytes 589832 | tf_op jit(solution)/shard_map/ppermute | solution.py:50
  44.2 16.8 %collective-permute-start.31 = (bf16[64,3200]{1,0:T(8,128)(2,1)S(1)}, bf16[64,3200]{1,0:T(8,128)(2,1)S(1)}, u32[]{:S(2)}, u32[]{:S(2)}) collective-permute-start(bf16[64,3200]{1,0:T(8,128)(2,1)S(1)} %add_cores.5.refs_3_.refs_0_), channel_id=1, source_target_pairs={{0,2},{2,0},{1,3},{3,1},{4,6},{6,4},{5,7},{7,5},{8,10},{10,8},{9,1... | collective-permute-start | bytes 1228808 | tf_op jit(solution)/shard_map/ppermute | solution.py:50
  51.5 9.5 %collective-permute-start.26 = (bf16[128,896]{1,0:T(8,128)(2,1)S(1)}, bf16[128,896]{1,0:T(8,128)(2,1)S(1)}, u32[]{:S(2)}, u32[]{:S(2)}) collective-permute-start(bf16[128,896]{1,0:T(8,128)(2,1)S(1)} %down_rows.4.refs_3_), channel_id=1, source_target_pairs={{0,12},{4,8},{8,4},{12,0},{1,13},{5,9},{9,5},{13,1},{2,14},{6,10},... | collective-permute-start | bytes 688136 | tf_op jit(solution)/shard_map/ppermute | solution.py:50
  55.8 1.7 %collective-permute-start.29 = (bf16[64,1536]{1,0:T(8,128)(2,1)S(1)}, bf16[64,1536]{1,0:T(8,128)(2,1)S(1)}, u32[]{:S(2)}, u32[]{:S(2)}) collective-permute-start(bf16[64,1536]{1,0:T(8,128)(2,1)S(1)} %get-tuple-element.82.refs_4_.refs_15_), channel_id=1, source_target_pairs={{0,1},{1,0},{2,3},{3,2},{4,5},{5,4},{6,7},{7,6},{8,9},{9,8},{10,11... | collective-permute-start | bytes 589832 | tf_op jit(solution)/shard_map/ppermute | solution.py:50
  58.5 7.8 %collective-permute-start.30 = (bf16[128,896]{1,0:T(8,128)(2,1)S(1)}, bf16[128,896]{1,0:T(8,128)(2,1)S(1)}, u32[]{:S(2)}, u32[]{:S(2)}) collective-permute-start(bf16[128,896]{1,0:T(8,128)(2,1)S(1)} %down_rows.5.refs_0_), channel_id=1, source_target_pairs={{0,4},{4,0},{8,12},{12,8},{1,5},{5,1},{9,13},{13,9},{2,6},{6,2},{1... | collective-permute-start | bytes 688136 | tf_op jit(solution)/shard_map/ppermute | solution.py:50
  62.1 1.7 %collective-permute-start.33 = (bf16[64,1536]{1,0:T(8,128)(2,1)S(1)}, bf16[64,1536]{1,0:T(8,128)(2,1)S(1)}, u32[]{:S(2)}, u32[]{:S(2)}) collective-permute-start(bf16[64,1536]{1,0:T(8,128)(2,1)S(1)} %get-tuple-element.84.refs_7_.refs_8_.refs_20_), channel_id=1, source_target_pairs={{0,1},{1,0},{2,3},{3,2},{4,5},{5,4},{6,7},{7,6},{8,9},{9,8},{10,11... | collective-permute-start | bytes 589832 | tf_op jit(solution)/shard_map/ppermute | solution.py:50
  67.0 4.7 %collective-permute-start.34 = (bf16[32,768]{1,0:T(8,128)(2,1)S(1)}, bf16[32,768]{1,0:T(8,128)(2,1)S(1)}, u32[]{:S(2)}, u32[]{:S(2)}) collective-permute-start(bf16[32,768]{1,0:T(8,128)(2,1)S(1)} %get-tuple-element.88.refs_0_), channel_id=1, source_target_pairs={{0,4},{4,0},{8,12},{12,8},{1,5},{5,1},{9,13},{13,9},{2,6},{6,2},{1... | collective-permute-start | bytes 147464 | tf_op jit(solution)/shard_map/ppermute | solution.py:50
  68.1 4.6 %collective-permute-start.36 = (bf16[32,768]{1,0:T(8,128)(2,1)S(1)}, bf16[32,768]{1,0:T(8,128)(2,1)S(1)}, u32[]{:S(2)}, u32[]{:S(2)}) collective-permute-start(bf16[32,768]{1,0:T(8,128)(2,1)S(1)} %get-tuple-element.90.refs_0_), channel_id=1, source_target_pairs={{0,4},{4,0},{8,12},{12,8},{1,5},{5,1},{9,13},{13,9},{2,6},{6,2},{1... | collective-permute-start | bytes 147464 | tf_op jit(solution)/shard_map/ppermute | solution.py:50
  71.7 6.1 %collective-permute-start.35 = (bf16[32,768]{1,0:T(8,128)(2,1)S(1)}, bf16[32,768]{1,0:T(8,128)(2,1)S(1)}, u32[]{:S(2)}, u32[]{:S(2)}) collective-permute-start(bf16[32,768]{1,0:T(8,128)(2,1)S(1)} %add_pair.2.refs_2_.refs_0_), channel_id=1, source_target_pairs={{0,8},{4,12},{8,0},{12,4},{1,9},{5,13},{9,1},{13,5},{2,10},{6,14},... | collective-permute-start | bytes 147464 | tf_op jit(solution)/shard_map/ppermute | solution.py:50
  72.7 5.6 %collective-permute-start.37 = (bf16[32,768]{1,0:T(8,128)(2,1)S(1)}, bf16[32,768]{1,0:T(8,128)(2,1)S(1)}, u32[]{:S(2)}, u32[]{:S(2)}) collective-permute-start(bf16[32,768]{1,0:T(8,128)(2,1)S(1)} %add_pair.3.refs_2_), channel_id=1, source_target_pairs={{0,8},{4,12},{8,0},{12,4},{1,9},{5,13},{9,1},{13,5},{2,10},{6,14},... | collective-permute-start | bytes 147464 | tf_op jit(solution)/shard_map/ppermute | solution.py:50
  (13 other events, 75.5 us)
